TPU v7x, 32 devices: a whole 2x2x4 slice. The times are simulated.
32 devices in a mesh: dp: 8 (over y, x, core), tensor: 4 (over z).
Axes of the slice: x: 2, y: 2, z: 4, core: 2. Of those that a mesh axis runs over, the one named last changes fastest.
Arguments:
- block_input: bfloat16 [8192, 1024], P(('dp', 'tensor')), may hold values from -6 to 6
- doc_lengths: int32 [8, 16], P('dp'), may hold values from 1 to 769, 1024 in all within a row
- pad_mask: int32 [8, 1024], P('dp'), may hold values 0 or 1
- norm1_gain: float32 [1024], replicated, may hold values from 0.5 to 1.5
- w_query: bfloat16 [1024, 1024], P(None, 'tensor'), may hold values from -0.1875 to 0.1875
- w_key: bfloat16 [1024, 512], P(None, 'tensor'), may hold values from -0.1875 to 0.1875
- w_value: bfloat16 [1024, 512], P(None, 'tensor'), may hold values from -0.1875 to 0.1875
- query_gain: float32 [64], replicated, may hold values from 0.5 to 1.5
- key_gain: float32 [64], replicated, may hold values from 0.5 to 1.5
- w_out: bfloat16 [1024, 1024], P('tensor'), may hold values from -3 to 3
- norm2_gain: float32 [1024], replicated, may hold values from 0.5 to 1.5
- w_gate: bfloat16 [1024, 4608], P(None, 'tensor'), may hold values from -0.1875 to 0.1875
- w_up: bfloat16 [1024, 4608], P(None, 'tensor'), may hold values from -0.1875 to 0.1875
- w_down: bfloat16 [4608, 1024], P('tensor'), may hold values from -0.09375 to 0.09375
- cotangent: bfloat16 [8192, 1024], P(('dp', 'tensor')), may hold values from -6 to 6
Outputs:
- block_output: float32 [8192, 1024], P(('dp', 'tensor'))
- input_grad: float32 [8192, 1024], P(('dp', 'tensor'))
- grad_norm1: float32 [1024], replicated
- grad_query: float32 [1024, 1024], P(None, 'tensor')
- grad_key: float32 [1024, 512], P(None, 'tensor')
- grad_value: float32 [1024, 512], P(None, 'tensor')
- grad_query_gain: float32 [64], replicated
- grad_key_gain: float32 [64], replicated
- grad_out: float32 [1024, 1024], P('tensor')
- grad_norm2: float32 [1024], replicated
- grad_gate: float32 [1024, 4608], P(None, 'tensor')
- grad_up: float32 [1024, 4608], P(None, 'tensor')
- grad_down: float32 [4608, 1024], P('tensor')
Inputs may be any that keep to these rules, and one draw needn't show every extreme that they name: `doc_lengths`: each row's lengths sum to 1024; exactly one document of each row is 769 long.
All inputs are finite; a program needn't handle non-finite values. No bound on the sum of `pad_mask` on one device may be relied on, other than what follows from the above.
Results may differ from a plain program's by a relative error of at most 0.015.
Values may be sent and summed in bfloat16 or wider, within the bound.
No kernel may reach another device: no remote copies, remote signals or barrier semaphores. Data moves between devices by JAX's collectives and lax.ppermute only.
A program may use at most 128 MiB of HBM per device.

v0:
```python
import functools
import math

import jax
import jax.numpy as jnp
from jax import lax
from jax.experimental import pallas as pl
from jax.experimental.pallas import tpu as pltpu
from jax.sharding import PartitionSpec as P

HD = 64
AX = ("dp", "tensor")
T4 = 4
VMEM_MB = 1 << 20

epsilon = 1e-05
rope_base = 1000000.0
NEG = -1000000000.0
bf16 = jnp.bfloat16
f32 = jnp.float32


def doc_tables(lengths_row, positions, head_dim):
    doc_ends = jnp.cumsum(lengths_row)
    passed = positions[:, None] >= doc_ends[None, :]
    doc_starts = jnp.sum(jnp.where(passed, lengths_row[None, :], 0), axis=1)
    offsets = (positions - doc_starts).astype(f32)
    freqs = jnp.exp(
        jnp.arange(head_dim // 2, dtype=f32) * (-2.0 * math.log(rope_base) / head_dim)
    )
    angles = offsets[:, None] * freqs[None, :]
    return (doc_starts, jnp.cos(angles), jnp.sin(angles))


def contract(a, b, da, db, precision=None):
    return lax.dot_general(
        a, b, (((da,), (db,)), ((), ())), preferred_element_type=f32, precision=precision
    )


def swap_halves(y):
    width = y.shape[1]
    lane = lax.broadcasted_iota(jnp.int32, y.shape, 1)
    return jnp.where(lane % HD < HD // 2, pltpu.roll(y, width - HD // 2, 1), pltpu.roll(y, HD // 2, 1))


def head_mean(y):
    width = y.shape[1]
    at = lax.broadcasted_iota(jnp.int32, (width, width), 0) // HD
    to = lax.broadcasted_iota(jnp.int32, (width, width), 1) // HD
    ones = jnp.where(at == to, 1.0 / HD, 0.0).astype(f32)
    return contract(y, ones, 1, 0, lax.Precision.HIGHEST)


class Weight:
    def __init__(self, s_ref, own, parts, to, sems, start=0):
        self.core, self.e = s_ref[1], s_ref[2]
        self.own, self.parts, self.to, self.sems, self.start_col = own, parts, to, sems, start

    def copies(self):
        start = 0
        for i, w in enumerate(self.own):
            wide = w.shape[1]
            to = self.to if len(self.own) == 1 else self.to.at[:, pl.ds(start, wide)]
            yield 0, functools.partial(pltpu.make_async_copy, w, to, self.sems.at[8 + i])
            start += wide
        rows = self.to.shape[0] // 8
        for j in range(4):
            for other in range(2):
                at = pl.multiple_of((2 * (self.e ^ j) + 1 - other) * rows, rows)
                src = self.parts[other].at[pl.ds(j * rows, rows), pl.ds(self.start_col, self.to.shape[1])]
                yield 1, functools.partial(
                    pltpu.make_async_copy, src, self.to.at[pl.ds(at, rows), :], self.sems.at[2 * j + other]
                )

    def each(self, act):
        for core in range(2):

            @pl.when(self.core == core)
            def _():
                for whose, copy in self.copies():
                    if whose == core:
                        act(copy())

    def start(self):
        self.each(lambda copy: copy.start())

    def wait(self):
        self.each(lambda copy: copy.wait())


ANY = pl.BlockSpec(memory_space=pl.ANY)


def fixed(*shape):
    return pl.BlockSpec(shape, lambda *_: (0,) * len(shape))


def params(mib):
    return pltpu.CompilerParams(vmem_limit_bytes=mib * VMEM_MB)


def qkv_kernel(s_ref, x0, x1, x2, x3, wq_own, wk_own, wv_own, w0, w1, g1_ref, gains_ref, cos_ref, sin_ref,
               n1_ref, pre_ref, qk_ref, v_ref, w_ref, xs, xsem, wsem):
    j = pl.program_id(0)
    pieces = (x0, x1, x2, x3)
    weight = Weight(s_ref, (wq_own, wk_own, wv_own), (w0, w1), w_ref, wsem)

    @pl.when(j == 0)
    def _():
        for k in range(4):
            pltpu.make_async_copy(pieces[k], xs.at[k], xsem.at[k]).start()
        weight.start()

    pltpu.make_async_copy(x0, xs.at[j], xsem.at[j]).wait()
    x = xs[j].astype(f32)
    inv = lax.rsqrt(jnp.mean(x * x, axis=-1, keepdims=True) + epsilon)
    n1 = (x * inv * g1_ref[...]).astype(bf16)
    n1_ref[...] = n1

    @pl.when(j == 0)
    def _():
        weight.wait()

    qkv = jnp.dot(n1, w_ref[...], preferred_element_type=f32)
    width = pre_ref.shape[1]
    pre = qkv[:, :width]
    pre_ref[...] = pre
    v_ref[...] = qkv[:, width:].astype(bf16)
    y = pre * lax.rsqrt(head_mean(pre * pre) + epsilon) * gains_ref[...]
    cos = jnp.concatenate([cos_ref[...]] * (width // 128), 1)
    sin = jnp.concatenate([sin_ref[...]] * (width // 128), 1)
    qk = (y * cos + swap_halves(y) * sin).astype(bf16)
    lane = lax.broadcasted_iota(jnp.int32, qk.shape, 1)
    qk_ref[...] = jnp.where(lane < width - 128, qk * 0.125, qk).astype(bf16)


def qkv_call(s, xs, w_own, w_parts, g1, gains, cos, sin):
    b, d = xs[0].shape
    wid = w_parts[0].shape[1]
    qkw = wid - 128
    natural = lambda j, s: (s[0] ^ j, 0)
    return pl.pallas_call(
        qkv_kernel,
        grid_spec=pltpu.PrefetchScalarGridSpec(
            num_scalar_prefetch=1,
            grid=(4,),
            in_specs=[ANY] * 9
            + [fixed(1, d), fixed(1, qkw), pl.BlockSpec((b, 128), natural), pl.BlockSpec((b, 128), natural)],
            out_specs=[
                pl.BlockSpec((b, d), lambda j, s: (j, 0)),
                pl.BlockSpec((b, qkw), natural),
                pl.BlockSpec((b, qkw), natural),
                pl.BlockSpec((b, 128), natural),
                fixed(d, wid),
            ],
            scratch_shapes=[
                pltpu.VMEM((4, b, d), bf16),
                pltpu.SemaphoreType.DMA((4,)),
                pltpu.SemaphoreType.DMA((11,)),
            ],
        ),
        out_shape=[
            jax.ShapeDtypeStruct((4 * b, d), bf16),
            jax.ShapeDtypeStruct((4 * b, qkw), f32),
            jax.ShapeDtypeStruct((4 * b, qkw), bf16),
            jax.ShapeDtypeStruct((4 * b, 128), bf16),
            jax.ShapeDtypeStruct((d, wid), bf16),
        ],
        compiler_params=params(20),
        cost_estimate=pl.CostEstimate(flops=8 * b * d * wid, bytes_accessed=9 * VMEM_MB, transcendentals=0),
        name="qkv",
    )(s, *xs, *w_own, *w_parts, g1, gains, cos, sin)


def both_heads(pair):
    lane = lax.broadcasted_iota(jnp.int32, pair.shape, 1)
    zero = jnp.zeros_like(pair)
    return jnp.concatenate([jnp.where(lane < HD, pair, zero), jnp.where(lane < HD, zero, pair)], 0)


def pick_heads(both):
    r = both.shape[0] // 2
    lane = lax.broadcasted_iota(jnp.int32, (r, 128), 1)
    return jnp.where(lane < HD, both[:r], both[r:])


def twice(kv, g):
    lane = lax.broadcasted_iota(jnp.int32, kv.shape, 1)
    turned = pltpu.roll(kv.astype(f32), HD, 1).astype(kv.dtype)
    return jnp.where((lane < HD) == (g == 0), kv, turned)


def attend_kernel(s_ref, q_ref, k_ref, v_ref, start_ref, live_ref, att_ref, out_ref, lse_ref, bias):
    g = pl.program_id(0)
    n = k_ref.shape[0]
    b = n // 4

    @pl.when(g == 0)
    def _():
        for a in range(4):
            keys = (a + 1) * b
            start = start_ref[a * b : (a + 1) * b, :1]
            q_at = lax.broadcasted_iota(jnp.int32, (b, keys), 0) + a * b
            k_at = lax.broadcasted_iota(jnp.int32, (b, keys), 1)
            allowed = ((live_ref[:1, :keys] >= start) & (k_at <= q_at)) | (k_at == q_at)
            bias[a * b : (a + 1) * b, :keys] = jnp.where(allowed, 0.0, NEG)

    kd = twice(k_ref[...], g)
    vd = twice(v_ref[...], g)
    for a in range(4):
        keys = (a + 1) * b
        rows = slice(a * b, (a + 1) * b)
        qm = both_heads(q_ref[rows, :])
        scores = contract(qm, kd[:keys], 1, 1)
        extra = bias[rows, :keys]
        expo = jnp.exp(scores + jnp.concatenate([extra, extra], 0))
        total = jnp.sum(expo, axis=-1, keepdims=True)
        pair = pick_heads(contract(expo.astype(bf16), vd[:keys], 1, 0) / total)
        out_ref[rows, :] = pair
        att_ref[pl.ds(pl.multiple_of((s_ref[0] ^ a) * b, b), b), :] = pair.astype(bf16)
        lse_ref[0, a] = jnp.transpose(jnp.broadcast_to(jnp.log(total), (2 * b, 128)))[:1]


def attend_call(s, qk, v, start, live):
    n = qk.shape[0]
    b = n // 4
    lanes = lambda g, s: (0, g)
    return pl.pallas_call(
        attend_kernel,
        grid_spec=pltpu.PrefetchScalarGridSpec(
            num_scalar_prefetch=1,
            grid=(2,),
            in_specs=[
                pl.BlockSpec((n, 128), lanes),
                pl.BlockSpec((n, 128), lambda g, s: (0, 2)),
                fixed(n, 128),
                fixed(n, 128),
                fixed(8, n),
            ],
            out_specs=[
                pl.BlockSpec((n, 128), lanes),
                pl.BlockSpec((n, 128), lanes),
                pl.BlockSpec((1, 4, 1, 2 * b), lambda g, s: (g, 0, 0, 0)),
            ],
            scratch_shapes=[pltpu.VMEM((n, n), f32)],
        ),
        out_shape=[
            jax.ShapeDtypeStruct((n, 256), bf16),
            jax.ShapeDtypeStruct((n, 256), f32),
            jax.ShapeDtypeStruct((2, 4, 1, 2 * b), f32),
        ],
        compiler_params=params(26),
        cost_estimate=pl.CostEstimate(
            flops=16 * n * n * HD, bytes_accessed=4 * VMEM_MB, transcendentals=4 * n * n
        ),
        name="attend",
    )(s, qk, qk, v, start, live)


def norm_back(grad, pre, gain, cos, sin):
    turned = grad * cos - swap_halves(grad) * sin
    inv = lax.rsqrt(head_mean(pre * pre) + epsilon)
    scaled = turned * gain
    dpre = inv * scaled - pre * (inv * inv * inv) * head_mean(scaled * pre)
    return dpre, jnp.sum(turned * pre * inv, axis=0, keepdims=True)


def attend_back_kernel(s_ref, q_ref, k_ref, v_ref, qpre_ref, kpre_ref, gains_ref, kgain_ref, cos_ref, sin_ref,
                       start_ref, live_ref, out_ref, lse_ref, wout_ref, w_ref, b0, b1, b2, b3,
                       low_ref, gain_ref, lo_ref, hi_ref, bias, dk, dv, dkall, dvall, dos, gb, sems):
    g = pl.program_id(0)
    n = k_ref.shape[0]
    b = n // 4
    pieces = (b0, b1, b2, b3)

    @pl.when(g == 0)
    def _():
        for k in range(4):
            pltpu.make_async_copy(pieces[k], gb.at[k], sems.at[k]).start()
        for a in range(4):
            keys = (a + 1) * b
            start = start_ref[:1, a * b : (a + 1) * b]
            k_at = lax.broadcasted_iota(jnp.int32, (keys, b), 0)
            q_at = lax.broadcasted_iota(jnp.int32, (keys, b), 1) + a * b
            allowed = ((live_ref[:keys, :1] >= start) & (k_at <= q_at)) | (k_at == q_at)
            bias[:keys, a * b : (a + 1) * b] = jnp.where(allowed, 0.0, NEG)
        for k in range(4):
            pltpu.make_async_copy(pieces[k], gb.at[k], sems.at[k]).wait()
            dos[k] = contract(gb[k], wout_ref[...], 1, 1).astype(bf16)

    kd = twice(k_ref[...], g)
    vd = twice(v_ref[...], g)
    gain_sum = jnp.zeros((1, 128), f32)
    ones = jnp.ones((8, 128), f32)
    for a in (3, 2, 1, 0):
        keys = (a + 1) * b
        rows = slice(a * b, (a + 1) * b)
        home = s_ref[0] ^ a
        qm = both_heads(q_ref[rows, :])
        dout = jnp.where(g == 0, dos[home, :, :128], dos[home, :, 128:])
        dom = both_heads(dout)
        delta = contract(ones, both_heads(dout.astype(f32) * out_ref[rows, :]), 1, 1, lax.Precision.HIGHEST)[:1]
        scores = contract(kd[:keys], qm, 1, 1)
        extra = bias[:keys, rows]
        probs = jnp.exp(scores + (jnp.concatenate([extra, extra], 1) - lse_ref[0, a]))
        dprobs = contract(vd[:keys], dom, 1, 1)
        dscores = (probs * (dprobs - delta)).astype(bf16)
        dv_add = contract(probs.astype(bf16), dom, 1, 0)
        dk_add = contract(dscores, qm, 1, 0)
        if a == 3:
            dv[...] = dv_add
            dk[...] = dk_add
        else:
            dv[:keys] += dv_add
            dk[:keys] += dk_add
        dq = pick_heads(contract(dscores, kd[:keys], 0, 0)) * 0.125
        dpre, gain_part = norm_back(dq, qpre_ref[rows, :], gains_ref[...], cos_ref[rows, :], sin_ref[rows, :])
        at = pl.ds(pl.multiple_of(home * b, b), b)
        low_ref[at, pl.ds(pl.multiple_of(g * 128, 128), 128)] = dpre.astype(bf16)
        gain_sum = gain_sum + gain_part
    gain_ref[pl.ds(g, 1), :] = gain_sum
    lane = lax.broadcasted_iota(jnp.int32, (n, 128), 1)
    dk_all = dk[...] + pltpu.roll(dk[...], HD, 1)
    dv_all = dv[...] + pltpu.roll(dv[...], HD, 1)

    @pl.when(g == 0)
    def _():
        dkall[...] = dk_all
        dvall[...] = dv_all

    @pl.when(g == 1)
    def _():
        grad_k = jnp.where(lane < HD, dkall[...], dk_all)
        grad_v = jnp.where(lane < HD, dvall[...], dv_all)
        dpre, gain_part = norm_back(grad_k, kpre_ref[...], kgain_ref[...], cos_ref[...], sin_ref[...])
        gain_ref[2:3, :] = gain_part
        for a in range(4):
            at = pl.ds(pl.multiple_of((s_ref[0] ^ a) * b, b), b)
            low_ref[at, 256:384] = dpre[a * b : (a + 1) * b].astype(bf16)
            low_ref[at, 384:512] = grad_v[a * b : (a + 1) * b].astype(bf16)
        hi_ref[...] = contract(low_ref[2 * b :, :], w_ref[...], 1, 1).astype(bf16)
        lo_ref[...] = contract(low_ref[: 2 * b, :], w_ref[...], 1, 1).astype(bf16)


def attend_back_call(s, qk, v, pre, qgain, kgain, cos, sin, start, live, out, lse, wout, w, blocks):
    n = v.shape[0]
    b = n // 4
    d = blocks[0].shape[1]
    lanes = pl.BlockSpec((n, 128), lambda g, s: (0, g))
    third = pl.BlockSpec((n, 128), lambda g, s: (0, 2))
    return pl.pallas_call(
        attend_back_kernel,
        grid_spec=pltpu.PrefetchScalarGridSpec(
            num_scalar_prefetch=1,
            grid=(2,),
            in_specs=[lanes, third, fixed(n, 128), lanes, third, fixed(1, 128), fixed(1, 128), fixed(n, 128),
                      fixed(n, 128), fixed(8, n), fixed(n, 128), lanes,
                      pl.BlockSpec((1, 4, 1, 2 * b), lambda g, s: (g, 0, 0, 0)),
                      fixed(256, d), fixed(d, 512)] + [ANY] * 4,
            out_specs=[fixed(n, 512), fixed(8, 128), fixed(2 * b, d), fixed(2 * b, d)],
            scratch_shapes=[pltpu.VMEM((n, n), f32)]
            + [pltpu.VMEM((n, 128), f32)] * 4
            + [pltpu.VMEM((4, b, 256), bf16), pltpu.VMEM((4, b, d), bf16), pltpu.SemaphoreType.DMA((4,))],
        ),
        out_shape=[
            jax.ShapeDtypeStruct((n, 512), bf16),
            jax.ShapeDtypeStruct((8, 128), f32),
            jax.ShapeDtypeStruct((2 * b, d), bf16),
            jax.ShapeDtypeStruct((2 * b, d), bf16),
        ],
        compiler_params=params(40),
        cost_estimate=pl.CostEstimate(
            flops=40 * n * n * HD + 2 * n * d * 768, bytes_accessed=10 * VMEM_MB, transcendentals=4 * n * n
        ),
        name="attend_back",
    )(s, qk, qk, v, pre, pre, qgain, kgain, cos, sin, start, live, out, lse, wout, w, *blocks)


def ffn_kernel(s_ref, x0, x1, x2, x3, a0, a1, a2, a3, o_in, wg_own, wu_own, p0, p1,
               gain_ref, n2_ref, hid_ref, fg_ref, fu_ref, res_ref, wg, wu, wout_ref, xs, att, wout, asem, xsem, osem, gsem, usem):
    j = pl.program_id(0)
    b = x0.shape[0]
    x_in, a_in = (x0, x1, x2, x3), (a0, a1, a2, a3)
    gate_w = Weight(s_ref, (wg_own,), (p0, p1), wg, gsem)
    up_w = Weight(s_ref, (wu_own,), (p0, p1), wu, usem, wg.shape[1])

    def out_copy(i):
        return pltpu.make_async_copy(o_in.at[:, i ^ (2 * s_ref[1])], wout.at[i], osem.at[i])

    def att_copy(k, i):
        return pltpu.make_async_copy(
            a_in[i].at[pl.ds((k ^ i) * b, b), :], att.at[k, :, pl.ds(i * b, b)], asem.at[k, i]
        )

    @pl.when(j == 0)
    def _():
        for k in range(4):
            pltpu.make_async_copy(x_in[k], xs.at[k], xsem.at[k]).start()
            for i in range(4):
                att_copy(k, i).start()
            if k == 0:
                for i in range(4):
                    out_copy(i).start()
                gate_w.start()
        up_w.start()
        for i in range(4):
            out_copy(i).wait()

    pltpu.make_async_copy(x0, xs.at[j], xsem.at[j]).wait()
    for i in range(4):
        pltpu.make_async_copy(a_in[i].at[pl.ds(0, b), :], att.at[j, :, pl.ds(i * b, b)], asem.at[j, i]).wait()
    res = xs[j].astype(f32) + jnp.dot(att[j], wout[...].reshape(4 * b, -1), preferred_element_type=f32)

    @pl.when(j == 0)
    def _():
        res_ref[...] = res
        wout_ref[...] = wout[0].reshape(b, -1)
        gate_w.wait()
        up_w.wait()

    inv = lax.rsqrt(jnp.mean(res * res, axis=-1, keepdims=True) + epsilon)
    n2 = (res * inv * gain_ref[...]).astype(bf16)
    n2_ref[...] = n2
    gate = jnp.dot(n2, wg[...], preferred_element_type=f32)
    up = jnp.dot(n2, wu[...], preferred_element_type=f32)
    s = jax.nn.sigmoid(gate)
    silu = gate * s
    hid_ref[...] = (silu * up).astype(bf16)
    fg_ref[...] = (up * (s * (1.0 + gate * (1.0 - s)))).astype(bf16)
    fu_ref[...] = silu.astype(bf16)


def ffn_call(s, xs, atts, wout, wg, wu, parts, gain):
    b, d = xs[0].shape
    h = wg.shape[1]
    block = lambda wid: pl.BlockSpec((b, wid), lambda j, s: (j, 0))
    return pl.pallas_call(
        ffn_kernel,
        grid_spec=pltpu.PrefetchScalarGridSpec(
            num_scalar_prefetch=1,
            grid=(4,),
            in_specs=[ANY] * 13 + [fixed(1, d)],
            out_specs=[block(d), block(h), block(h), block(h), fixed(b, d), fixed(d, h), fixed(d, h), fixed(b, d)],
            scratch_shapes=[
                pltpu.VMEM((4, b, d), bf16),
                pltpu.VMEM((4, b, 4 * b), bf16),
                pltpu.VMEM((4,) + wout.shape[:1] + wout.shape[2:], bf16),
                pltpu.SemaphoreType.DMA((4, 4)),
                pltpu.SemaphoreType.DMA((4,)),
                pltpu.SemaphoreType.DMA((4,)),
                pltpu.SemaphoreType.DMA((9,)),
                pltpu.SemaphoreType.DMA((9,)),
            ],
        ),
        out_shape=[jax.ShapeDtypeStruct((4 * b, d), bf16)]
        + [jax.ShapeDtypeStruct((4 * b, h), bf16)] * 3
        + [jax.ShapeDtypeStruct((b, d), f32)]
        + [jax.ShapeDtypeStruct((d, h), bf16)] * 2
        + [jax.ShapeDtypeStruct((b, d), bf16)],
        compiler_params=params(34),
        cost_estimate=pl.CostEstimate(
            flops=8 * b * d * (d + 2 * h), bytes_accessed=25 * VMEM_MB, transcendentals=4 * b * h
        ),
        name="ffn",
    )(s, *xs, *atts, wout, wg, wu, *parts, gain)


def ffn_back_kernel(s_ref, y0, y1, y2, y3, wd_own, d0, d1, fg_ref, fu_ref, wg_in, wu_in,
                    gg_ref, gu_ref, lo_ref, hi_ref, wd, dy, wg, wu, ysem, dsem, wsem):
    j = pl.program_id(0)
    y_in = (y0, y1, y2, y3)
    down_w = Weight(s_ref, (wd_own,), (d0, d1), wd, dsem)

    @pl.when(j == 0)
    def _():
        for k in range(4):
            pltpu.make_async_copy(y_in[k], dy.at[k], ysem.at[k]).start()
        down_w.start()
        pltpu.make_async_copy(wg_in, wg, wsem.at[0]).start()
        pltpu.make_async_copy(wu_in, wu, wsem.at[1]).start()
        down_w.wait()

    pltpu.make_async_copy(y0, dy.at[j], ysem.at[j]).wait()
    gh = contract(dy[j], wd[...], 1, 1)
    gg = (gh * fg_ref[...].astype(f32)).astype(bf16)
    gu = (gh * fu_ref[...].astype(f32)).astype(bf16)
    gg_ref[...] = gg
    gu_ref[...] = gu

    @pl.when(j == 0)
    def _():
        pltpu.make_async_copy(wg_in, wg, wsem.at[0]).wait()
        pltpu.make_async_copy(wu_in, wu, wsem.at[1]).wait()

    grad = (contract(gg, wg[...], 1, 1) + contract(gu, wu[...], 1, 1)).astype(bf16)

    @pl.when(j < 2)
    def _():
        lo_ref[...] = grad

    @pl.when(j >= 2)
    def _():
        hi_ref[...] = grad


def ffn_back_call(s, dys, wd, d_parts, fg, fu, wg, wu):
    b, d = dys[0].shape
    h = wg.shape[1]
    block = lambda wid: pl.BlockSpec((b, wid), lambda j, s: (j, 0))
    return pl.pallas_call(
        ffn_back_kernel,
        grid_spec=pltpu.PrefetchScalarGridSpec(
            num_scalar_prefetch=1,
            grid=(4,),
            in_specs=[ANY] * 7 + [block(h), block(h), ANY, ANY],
            out_specs=[
                block(h),
                block(h),
                pl.BlockSpec((b, d), lambda j, s: (jnp.minimum(j, 1), 0)),
                pl.BlockSpec((b, d), lambda j, s: (jnp.maximum(j - 2, 0), 0)),
                fixed(h, d),
            ],
            scratch_shapes=[
                pltpu.VMEM((4, b, d), bf16),
                pltpu.VMEM((d, h), bf16),
                pltpu.VMEM((d, h), bf16),
                pltpu.SemaphoreType.DMA((4,)),
                pltpu.SemaphoreType.DMA((9,)),
                pltpu.SemaphoreType.DMA((2,)),
            ],
        ),
        out_shape=[jax.ShapeDtypeStruct((4 * b, h), bf16)] * 2
        + [jax.ShapeDtypeStruct((2 * b, d), bf16)] * 2
        + [jax.ShapeDtypeStruct((h, d), bf16)],
        compiler_params=params(34),
        cost_estimate=pl.CostEstimate(flops=24 * b * d * h, bytes_accessed=22 * VMEM_MB, transcendentals=0),
        name="ffn_back",
    )(s, *dys, wd, *d_parts, fg, fu, wg, wu)


def grad_rows_kernel(by_cols, s_ref, left_ref, right_ref, sent_a, keep_a, sent_b, keep_b):
    j = pl.program_id(0)
    grad = contract(left_ref[...], right_ref[...], 0, 0).astype(bf16)
    rows, cols = grad.shape
    if by_cols:
        first, second = grad[:, : cols // 2], grad[:, cols // 2 :]
    else:
        r = rows // 4
        first = jnp.concatenate([grad[:r], grad[2 * r : 3 * r]], 0)
        second = jnp.concatenate([grad[r : 2 * r], grad[3 * r :]], 0)

    @pl.when(j % 2 == 1)
    def _():
        sent_a[0] = first

    @pl.when(j % 2 == 0)
    def _():
        keep_a[0] = first

    @pl.when(j >= 2)
    def _():
        sent_b[0] = second

    @pl.when(j < 2)
    def _():
        keep_b[0] = second


def grad_rows_call(s, left, right, by_cols, name):
    n, rows = left.shape
    cols = right.shape[1]
    half = (rows // 4, cols // 2) if by_cols else (rows // 8, cols)
    maps = [
        lambda j, s: (j // 2, 0, 0),
        lambda j, s: (j // 2, 0, 0),
        lambda j, s: (jnp.maximum(j - 2, 0), 0, 0),
        lambda j, s: (jnp.minimum(j, 1), 0, 0),
    ]
    return pl.pallas_call(
        functools.partial(grad_rows_kernel, by_cols),
        grid_spec=pltpu.PrefetchScalarGridSpec(
            num_scalar_prefetch=1,
            grid=(4,),
            in_specs=[pl.BlockSpec((n, rows // 4), lambda j, s: (0, s[2] ^ j)), fixed(n, cols)],
            out_specs=[pl.BlockSpec((1,) + half, m) for m in maps],
        ),
        out_shape=[jax.ShapeDtypeStruct((2,) + half, bf16)] * 4,
        compiler_params=params(24),
        cost_estimate=pl.CostEstimate(flops=2 * n * rows * cols, bytes_accessed=4 * n * (rows + cols), transcendentals=0),
        name=name,
    )(s, left, right)


def grad_cols_kernel(s_ref, left_ref, r0, r1, r2, r3, sent_a, keep_a, sent_b, keep_b):
    k = pl.program_id(0)
    b = r0.shape[0]
    grad = None
    for i, right in enumerate((r0, r1, r2, r3)):
        part = contract(left_ref[i * b : (i + 1) * b, :], right[...], 0, 0)
        grad = part if grad is None else grad + part
    grad = grad.astype(bf16)
    rows = grad.shape[0] // 4
    for a in range(4):
        piece = grad[a * rows : (a + 1) * rows]
        j = s_ref[2] ^ a

        @pl.when((k < 2) & (j % 2 == 1))
        def _():
            sent_a[j // 2] = piece

        @pl.when((k < 2) & (j % 2 == 0))
        def _():
            keep_a[j // 2] = piece

        @pl.when((k >= 2) & (j >= 2))
        def _():
            sent_b[j % 2] = piece

        @pl.when((k >= 2) & (j < 2))
        def _():
            keep_b[j % 2] = piece


def grad_cols_call(s, left, rights, name):
    n, rows = left.shape
    b, cols = rights[0].shape
    first = pl.BlockSpec((2, rows // 4, cols // 4), lambda k, s: (0, 0, jnp.minimum(k, 1)))
    second = pl.BlockSpec((2, rows // 4, cols // 4), lambda k, s: (0, 0, jnp.maximum(k - 2, 0)))
    return pl.pallas_call(
        grad_cols_kernel,
        grid_spec=pltpu.PrefetchScalarGridSpec(
            num_scalar_prefetch=1,
            grid=(4,),
            in_specs=[fixed(n, rows)] + [pl.BlockSpec((b, cols // 4), lambda k, s: (0, k))] * 4,
            out_specs=[first, first, second, second],
        ),
        out_shape=[jax.ShapeDtypeStruct((2, rows // 4, cols // 2), bf16)] * 4,
        compiler_params=params(24),
        cost_estimate=pl.CostEstimate(flops=2 * n * rows * cols, bytes_accessed=4 * n * (rows + cols), transcendentals=0),
        name=name,
    )(s, left, *rights)


def permute(x, places, move):
    pairs = []
    for d in range(places):
        for t in range(T4):
            to = move(d, t)
            if to is not None:
                pairs.append((d * T4 + t, to[0] * T4 + to[1]))
    return lax.ppermute(x, AX, pairs)


def after(x, *events):
    return lax.optimization_barrier((x, events))[0]


def flip_core(d, t):
    return (d ^ 1, t)


def flip_z(d, t):
    return (d, t ^ 1)


def flip_far(d, t):
    return (d, t ^ 2)


def flip_e(bit):
    return lambda d, t: (d ^ (2 << bit), t)


def settle(d, t):
    return (d, t) if (d & 1) == (t >> 1) else (d ^ 1, t ^ 2)


def gather_row(x, n):
    over = permute(x, n, flip_z)
    near = permute(x, n, flip_core)
    far = permute(over, n, flip_core)
    return [x, over, near, far]


def scatter_row(low, high, n, *events):
    b = low.shape[0] // 2
    got = permute(high, n, flip_core)
    over = permute(low[b:] + got[b:], n, flip_z)
    return low[:b] + got[:b] + (after(over, *events) if events else over)


def hop(weights, n, c, e):
    rows = weights[0].shape[0] // 8
    mine = [lax.dynamic_slice_in_dim(w, (2 * e + c) * rows, rows, 0) for w in weights]
    return permute(jnp.concatenate(mine, 1) if len(mine) > 1 else mine[0], n, flip_far)


def spread(piece, n):
    mine = jnp.concatenate([piece] + [permute(piece, n, lambda d, t, j=j: (d ^ (2 * j), t)) for j in (1, 2, 3)])
    return mine, permute(mine, n, flip_core)


def first_sums(pieces, n):
    sent_a, keep_a, sent_b, keep_b = pieces
    got_a = permute(sent_a, n, flip_e(0))
    got_b = permute(sent_b, n, flip_e(1))
    return got_a, got_b


def first_add(pieces, got):
    got_a, got_b = got
    keep_a, keep_b = pieces[1], pieces[3]
    return keep_a[1] + got_a[1], keep_a[0] + got_a[0], keep_b[1] + got_b[1], keep_b[0] + got_b[0]


def second_sums(halves, n):
    return permute(halves[0], n, flip_e(1)), permute(halves[2], n, flip_e(0))


def second_add(halves, got, n):
    total = jnp.stack([halves[1] + got[0], halves[3] + got[1]])
    for extra in range(2, 20):
        if (2 << extra) < n:
            total = total + permute(total, n, flip_e(extra))
    return total


def owner_cross(total, n, c):
    half = total.shape[1] // 2
    first, second = total[:, :half], total[:, half:]
    got = permute(jnp.where(c == 0, second, first), n, flip_core)
    return jnp.where(c == 0, first, got), permute(jnp.where(c == 0, got, second), n, flip_far)


def neighbours(n):
    return None if n == 8 else [list(range(k, k + 8)) for k in range(0, n, 8)]


def whole_grad(mine, n):
    return lax.all_gather(mine, "dp", axis_index_groups=neighbours(n))


def whole_out(w, n, c, e):
    rows = w.shape[0] // 8
    mine = lax.dynamic_slice_in_dim(w, (2 * e + c) * rows, rows, 0)
    two = jnp.stack([mine, permute(mine, n, flip_z)])
    four = jnp.concatenate([two, permute(two, n, flip_far)])
    return lax.all_gather(four, "dp", axis_index_groups=neighbours(n))


def sum_all(vec, n):
    bit = 1
    while bit < n:
        vec = vec + permute(vec, n, lambda d, t, bit=bit: (d ^ bit, t))
        bit *= 2
    for bit in (1, 2):
        vec = vec + permute(vec, n, lambda d, t, bit=bit: (d, t ^ bit))
    return vec


def local(
    block_input,
    doc_lengths,
    pad_mask,
    norm1_gain,
    w_query,
    w_key,
    w_value,
    query_gain,
    key_gain,
    w_out,
    norm2_gain,
    w_gate,
    w_up,
    w_down,
    cotangent,
):
    n = lax.axis_size("dp")
    d, t = lax.axis_index("dp"), lax.axis_index("tensor")
    c, p = d & 1, t >> 1
    e = (d >> 1) & 3
    shard = 2 * c + (t & 1)
    b = block_input.shape[0]
    seq_len = b * T4
    home = c == p
    wq = w_query.shape[1]
    wk = w_key.shape[1]
    width = block_input.shape[1]
    s = jnp.stack([shard, c, e]).astype(jnp.int32)

    x_own = permute(block_input, n, settle)
    marks = jnp.concatenate([doc_lengths, pad_mask], 1)
    marks = jnp.where(home, marks, permute(marks, n, flip_core))
    lengths_row, pad_row = marks[0, : doc_lengths.shape[1]], marks[0, doc_lengths.shape[1] :]
    qkv_hop = hop((w_query, w_key, w_value), n, c, e)
    x_blocks = gather_row(x_own, n)
    qkv_parts = spread(qkv_hop, n)
    gate_up_hop = hop((after(w_gate, x_blocks[2]), w_up), n, c, e)
    out_all = whole_out(after(w_out, x_blocks[2]), n, c, e)

    positions = jnp.arange(seq_len, dtype=jnp.int32)
    doc_starts, cos_half, sin_half = doc_tables(lengths_row, positions, HD)
    cos = jnp.concatenate([cos_half] * 4, 1)
    sin = jnp.concatenate([-sin_half, sin_half] * 2, 1)
    live = jnp.where(pad_row == 1, positions, -1)
    start_col = jnp.broadcast_to(doc_starts[:, None], (seq_len, 128))
    start_row = jnp.broadcast_to(doc_starts[None], (8, seq_len))
    live_col = jnp.broadcast_to(live[:, None], (seq_len, 128))
    live_row = jnp.broadcast_to(live[None], (8, seq_len))
    gains = jnp.concatenate([query_gain] * (wq // HD) + [key_gain] * (wk // HD))[None]
    qgain_pair = jnp.concatenate([query_gain] * 2)[None]
    kgain_pair = jnp.concatenate([key_gain] * 2)[None]

    rows_one, pre, qk, values, w_qkv = qkv_call(
        s, x_blocks, (w_query, w_key, w_value), qkv_parts, norm1_gain[None], gains, cos, sin
    )
    attended, attended_f, lse = attend_call(s, qk, values, start_col, live_row)
    att_pieces = gather_row(attended, n)
    gate_up_parts = spread(after(gate_up_hop, attended), n)
    down_hop = hop((after(w_down, attended),), n, c, e)
    dy_own = permute(after(cotangent, attended), n, settle)
    down_parts = spread(after(down_hop, att_pieces[1]), n)
    dy_blocks = gather_row(after(dy_own, att_pieces[1]), n)
    rows_two, hidden, by_gate, by_up, residual, wg, wu, w_out_own = ffn_call(
        s, x_blocks, att_pieces, out_all, w_gate, w_up, gate_up_parts, after(norm2_gain[None], dy_own)
    )

    down = grad_cols_call(s, hidden, dy_blocks, "grad_down")
    gate_grad, up_grad, low2, high2, wd = ffn_back_call(
        s, dy_blocks, w_down, down_parts, after(by_gate, *down), by_up, wg, wu
    )
    down_got = first_sums(down, n)
    down = first_add(down, after(down_got, low2))
    down_got = second_sums(down, n)
    gate = grad_rows_call(s, rows_two, after(gate_grad, *down), False, "grad_gate")
    gate_got = first_sums(gate, n)
    up = grad_rows_call(s, rows_two, after(up_grad, *gate), False, "grad_up")
    up_got = first_sums(up, n)
    grad_n2 = scatter_row(low2, high2, n, *up).astype(f32)
    inv = lax.rsqrt(jnp.mean(residual * residual, axis=-1, keepdims=True) + epsilon)
    scaled = norm2_gain * grad_n2
    grad_residual = (
        dy_own.astype(f32)
        + inv * scaled
        - residual * (inv * inv * inv) * jnp.mean(scaled * residual, axis=-1, keepdims=True)
    )
    grad_norm2 = jnp.sum(grad_n2 * residual * inv, axis=0)
    gb_own = grad_residual.astype(bf16)
    gb_blocks = gather_row(gb_own, n)

    down = second_add(down, after(down_got, gb_own), n)
    down_kept, down_got = owner_cross(down, n, c)
    ffn_part = jnp.dot(after(hidden, down_kept), wd, preferred_element_type=f32).astype(bf16)
    gate = first_add(gate, after(gate_got, ffn_part))
    gate_got = second_sums(gate, n)
    up = first_add(up, after(up_got, gb_blocks[1], *gate))
    up_got = second_sums(up, n)
    down_mine = down_kept + after(down_got, gb_blocks[3], *up)
    down_all = whole_grad(down_mine, n)
    gate = second_add(gate, after(gate_got, down_mine), n)
    gate_kept, gate_got = owner_cross(gate, n, c)
    ffn_got = permute(ffn_part[2 * b :], n, flip_core)
    ffn_half = ffn_part[: 2 * b] + after(ffn_got, gb_blocks[3])
    ffn_over = permute(ffn_half[b:], n, flip_z)

    low, gain_terms, low1, high1 = attend_back_call(
        s, qk, after(values, gate_kept, ffn_half), pre, qgain_pair, kgain_pair, cos, sin, start_row, live_col, attended_f,
        lse, w_out_own, w_qkv, gb_blocks,
    )
    high_got = permute(high1, n, flip_core)
    gate_mine = gate_kept + after(gate_got, low)
    gate_all = whole_grad(gate_mine, n)
    low_half = low1 + after(high_got, gate_mine)
    low_over = permute(low_half[b:], n, flip_z)
    up = second_add(up, after(up_got, low_half), n)
    up_kept, up_got = owner_cross(up, n, c)
    block_output = residual + (ffn_half[:b] + after(ffn_over, low_half, up)).astype(f32)
    settled_output = permute(block_output.astype(bf16), n, settle)
    qkv = grad_rows_call(s, rows_one, after(low, up_kept, block_output), True, "grad_qkv")
    qkv_got = first_sums(qkv, n)
    out = grad_cols_call(s, after(attended, *qkv), gb_blocks, "grad_out")
    out_got = first_sums(out, n)

    grad_n1 = (low_half[:b] + after(low_over, *out)).astype(f32)
    x_f = x_own.astype(f32)
    inv = lax.rsqrt(jnp.mean(x_f * x_f, axis=-1, keepdims=True) + epsilon)
    scaled = norm1_gain * grad_n1
    input_grad = (
        grad_residual
        + inv * scaled
        - x_f * (inv * inv * inv) * jnp.mean(scaled * x_f, axis=-1, keepdims=True)
    )
    grad_norm1 = jnp.sum(grad_n1 * x_f * inv, axis=0)
    settled_grad = permute(input_grad.astype(bf16), n, settle)
    up_mine = up_kept + after(up_got, input_grad)
    up_all = whole_grad(up_mine, n)
    qkv = first_add(qkv, after(qkv_got, up_mine))
    qkv_got = second_sums(qkv, n)
    out = first_add(out, after(out_got, *qkv))
    out_got = second_sums(out, n)
    head_terms = gain_terms[:, :HD] + gain_terms[:, HD:]
    vec = jnp.concatenate([grad_norm1, grad_norm2, head_terms[0] + head_terms[1], head_terms[2]])
    vec = sum_all(after(vec, *out)[None], n)[0]
    qkv = second_add(qkv, after(qkv_got, vec), n)
    out = second_add(out, after(out_got, vec), n)
    qkv_kept, qkv_got = owner_cross(qkv, n, c)
    out_kept, out_got = owner_cross(out, n, c)
    qkv_all = whole_grad(qkv_kept + qkv_got, n)
    out_all = whole_grad(out_kept + out_got, n)
    block_output = jnp.where(home, block_output, after(settled_output, qkv_kept, out_kept).astype(f32))
    input_grad = jnp.where(home, input_grad, after(settled_grad, qkv_kept, out_kept).astype(f32))

    def rows(whole):
        return whole.astype(f32).reshape(width, -1)

    def side_by_side(whole):
        return whole.astype(f32).transpose(0, 2, 1, 3).reshape(-1, width)

    grad_down = side_by_side(down_all)
    grad_gate = rows(gate_all)
    grad_up = rows(up_all)
    grad_out = side_by_side(out_all)
    grad_query = rows(qkv_all[:, 0])
    grad_kv = rows(qkv_all[:, 1])
    return (
        block_output,
        input_grad,
        vec[:width],
        grad_query,
        grad_kv[:, :wk],
        grad_kv[:, wk:],
        vec[2 * width : 2 * width + HD],
        vec[2 * width + HD :],
        grad_out,
        vec[width : 2 * width],
        grad_gate,
        grad_up,
        grad_down,
    )


def solution(mesh):
    placed = (
        P(("dp", "tensor"), None),
        P("dp", None),
        P("dp", None),
        P(),
        P(None, "tensor"),
        P(None, "tensor"),
        P(None, "tensor"),
        P(),
        P(),
        P("tensor", None),
        P(),
        P(None, "tensor"),
        P(None, "tensor"),
        P("tensor", None),
        P(("dp", "tensor"), None),
    )
    return jax.shard_map(
        local,
        mesh=mesh,
        in_specs=placed,
        out_specs=(
            P(("dp", "tensor"), None),
            P(("dp", "tensor"), None),
            P(),
            P(None, "tensor"),
            P(None, "tensor"),
            P(None, "tensor"),
            P(),
            P(),
            P("tensor", None),
            P(),
            P(None, "tensor"),
            P(None, "tensor"),
            P("tensor", None),
        ),
        check_vma=False,
    )
```

profile of v0, /device:TPU:0, one launch (start us, length us, event | category | flops | bytes accessed | tf_op | source)
XLA Modules:
  0.0 514.5 jit_solution(5424477759112682330)
XLA Ops:
  8.9 4.1 collective-permute-start.4
  13.8 1.7 collective-permute-start
  17.6 1.9 fusion.20
  21.1 10.4 %collective-permute-start.2 = (bf16[256,1024]{1,0:T(8,128)(2,1)S(1)}, bf16[256,1024]{1,0:T(8,128)(2,1)S(1)}, u32[]{:S(2)}, u32[]{:S(2)}) collective-permute-start(bf16[256,1024]{1,0:T(8,128)(2,1)S(1)} %collective-permute-done.x0), channel_id=1, source_target_pairs={{0,4},{1,5},{2,6},{3,7},{4,0},{5,1},{6,2},{7,3},{8,12},{9,13},{10,... | collective-permute-start | bytes 1572872 | tf_op jit(solution)/shard_map/ppermute | solution.py:652
  34.7 5.2 %collective-permute-done.6 = bf16[128,512]{1,0:T(8,128)(2,1)S(1)} collective-permute-done((bf16[128,512]{1,0:T(8,128)(2,1)S(1)}, bf16[128,512]{1,0:T(8,128)(2,1)S(1)}, u32[]{:S(2)}, u32[]{:S(2)}) %collective-permute-start.6) | collective-permute-done | bytes 131104 | tf_op jit(solution)/shard_map/ppermute | solution.py:652
  41.4 6.6 %collective-permute-done.1.x1 = bf16[256,1024]{1,0:T(8,128)(2,1)S(1)} collective-permute-done((bf16[256,1024]{1,0:T(8,128)(2,1)S(1)}, bf16[256,1024]{1,0:T(8,128)(2,1)S(1)}, u32[]{:S(2)}, u32[]{:S(2)}) %collective-permute-start.1) | collective-permute-done | bytes 524320 | tf_op jit(solution)/shard_map/ppermute | solution.py:652
  48.0 2.0 collective-permute-start.15
  50.9 1.8 collective-permute-start.13
  52.7 12.0 %collective-permute-done.13 = bf16[32,1024]{1,0:T(8,128)(2,1)S(1)} collective-permute-done((bf16[32,1024]{1,0:T(8,128)(2,1)S(1)}, bf16[32,1024]{1,0:T(8,128)(2,1)S(1)}, u32[]{:S(2)}, u32[]{:S(2)}) %collective-permute-start.13) | collective-permute-done | bytes 65568 | tf_op jit(solution)/shard_map/ppermute | solution.py:652
  64.7 2.6 collective-permute-start.14
  67.3 7.5 %qkv.1 = (bf16[1024,1024]{1,0:T(8,128)(2,1)S(1)}, f32[1024,384]{1,0:T(8,128)S(1)}, bf16[1024,384]{1,0:T(8,128)(2,1)S(1)}, bf16[1024,128]{1,0:T(8,128)(2,1)S(1)}, bf16[1024,512]{1,0:T(8,128)(2,1)S(1)}) custom-call(s32[3]{0:T(128)S(1)} %pad_add_fusion.1.s_ref, bf16[256,1024]{1,0:T(8,128)(2,1)S(1)} %collective-permute-done.x0, ...), custom_call_target="tpu_custom_call" | custom-call | flops 1073741824 | bytes 9437184 | tf_op jit(solution)/shard_map/qkv/pallas_call | solution.py:143
  78.5 5.4 %attend.1 = (bf16[1024,256]{1,0:T(8,128)(2,1)S(1)}, f32[1024,256]{1,0:T(8,128)S(1)}, f32[2,4,1,512]{3,2,1,0:T(1,128)S(1)}) custom-call(s32[3]{0:T(128)S(1)} %pad_add_fusion.1.s_ref, bf16[1024,384]{1,0:T(8,128)(2,1)S(1)} %get-tuple-element.104.q_ref.k_ref, bf16[1024,384]{1,0:T(8,128)(2,1)S(1)} %get-tuple-element.104.q_ref.k_ref, ...), custom_call_target="tpu_custom_call" | custom-call | flops 1073741824 | bytes 4194304 | tf_op jit(solution)/shard_map/attend/pallas_call | solution.py:229
  89.3 1.9 constant_dynamic-update-slice_fusion.7
  91.3 12.6 %collective-permute-done.16 = bf16[128,2304]{1,0:T(8,128)(2,1)S(1)} collective-permute-done((bf16[128,2304]{1,0:T(8,128)(2,1)}, bf16[128,2304]{1,0:T(8,128)(2,1)S(1)}, u32[]{:S(2)}, u32[]{:S(2)}) %collective-permute-start.16) | collective-permute-done | bytes 589856 | tf_op jit(solution)/shard_map/ppermute | solution.py:652
  104.7 13.5 %collective-permute-done.17 = bf16[128,2304]{1,0:T(8,128)(2,1)S(1)} collective-permute-done((bf16[128,2304]{1,0:T(8,128)(2,1)}, bf16[128,2304]{1,0:T(8,128)(2,1)S(1)}, u32[]{:S(2)}, u32[]{:S(2)}) %collective-permute-start.17) | collective-permute-done | bytes 589856 | tf_op jit(solution)/shard_map/ppermute | solution.py:652
  121.0 2.6 collective-permute-start.26
  125.3 13.4 %collective-permute-done.26 = bf16[144,1024]{1,0:T(8,128)(2,1)S(1)} collective-permute-done((bf16[144,1024]{1,0:T(8,128)(2,1)S(1)}, bf16[144,1024]{1,0:T(8,128)(2,1)S(1)}, u32[]{:S(2)}, u32[]{:S(2)}) %collective-permute-start.26) | collective-permute-done | bytes 294944 | tf_op jit(solution)/shard_map/ppermute | solution.py:652
  138.7 5.2 %collective-permute-done.10.a1 = bf16[1024,256]{1,0:T(8,128)(2,1)S(1)} collective-permute-done((bf16[1024,256]{1,0:T(8,128)(2,1)S(1)}, bf16[1024,256]{1,0:T(8,128)(2,1)S(1)}, u32[]{:S(2)}, u32[]{:S(2)}) %collective-permute-start.10) | collective-permute-done | bytes 524320 | tf_op jit(solution)/shard_map/ppermute | solution.py:652
  148.7 5.2 %collective-permute-done.27 = bf16[144,1024]{1,0:T(8,128)(2,1)S(1)} collective-permute-done((bf16[144,1024]{1,0:T(8,128)(2,1)S(1)}, bf16[144,1024]{1,0:T(8,128)(2,1)S(1)}, u32[]{:S(2)}, u32[]{:S(2)}) %collective-permute-start.27) | collective-permute-done | bytes 294944 | tf_op jit(solution)/shard_map/ppermute | solution.py:652
  154.6 5.4 %collective-permute-done.28 = bf16[144,1024]{1,0:T(8,128)(2,1)S(1)} collective-permute-done((bf16[144,1024]{1,0:T(8,128)(2,1)S(1)}, bf16[144,1024]{1,0:T(8,128)(2,1)S(1)}, u32[]{:S(2)}, u32[]{:S(2)}) %collective-permute-start.28) | collective-permute-done | bytes 294944 | tf_op jit(solution)/shard_map/ppermute | solution.py:652
  162.8 2.2 collective-permute-done.21.r1.y1
  174.7 13.0 %ffn.1 = (bf16[1024,1024]{1,0:T(8,128)(2,1)S(1)}, bf16[1024,1152]{1,0:T(8,128)(2,1)S(1)}, bf16[1024,1152]{1,0:T(8,128)(2,1)S(1)}, bf16[1024,1152]{1,0:T(8,128)(2...) custom-call(s32[3]{0:T(128)S(1)} %pad_add_fusion.1.s_ref, ...), custom_call_target="tpu_custom_call" | custom-call | flops 6979321856 | bytes 26214400 | tf_op jit(solution)/shard_map/ffn/pallas_call | solution.py:438
  190.6 7.9 %grad_down.1 = (bf16[2,288,512]{2,1,0:T(8,128)(2,1)}, bf16[2,288,512]{2,1,0:T(8,128)(2,1)S(1)}, bf16[2,288,512]{2,1,0:T(8,128)(2,1)}, bf16[2,288,512]{2,1,0:T(8,128)(2,1)S(1)}) custom-call(s32[3]{0:T(128)S(1)} %pad_add_fusion.1.s_ref, bf16[1024,1152]{1,0:T(8,128)(2,1)S(1)} %get-tuple-element.146.left_ref, ...), custom_call_target="tpu_custom_call" | custom-call | flops 2415919104 | bytes 8912896 | tf_op jit(solution)/shard_map/grad_down/pallas_call | solution.py:630
  200.2 13.9 %ffn_back.1 = (bf16[1024,1152]{1,0:T(8,128)(2,1)S(1)}, bf16[1024,1152]{1,0:T(8,128)(2,1)S(1)}, bf16[512,1024]{1,0:T(8,128)(2,1)S(1)}, bf16[512,1024]{1,0:T(8,128)(2,1)}, bf16[1152,1024]{1,0:T(8,128)(2,1)S(1)}) custom-call(s32[3]{0:T(128)S(1)} %pad_add_fusion.1.s_ref, bf16[256,1024]{1,0:T(8,128)(2,1)S(1)} %collective-permute-done.20.r0.y0, ...), custom_call_target="tpu_custom_call" | custom-call | flops 7247757312 | bytes 23068672 | tf_op jit(solution)/shard_map/ffn_back/pallas_call | solution.py:511
  223.8 12.1 %collective-permute-done.24 = bf16[2,288,512]{2,1,0:T(8,128)(2,1)} collective-permute-done((bf16[2,288,512]{2,1,0:T(8,128)(2,1)}, bf16[2,288,512]{2,1,0:T(8,128)(2,1)}, u32[]{:S(2)}, u32[]{:S(2)}) %collective-permute-start.24) | collective-permute-done | bytes 589856 | tf_op jit(solution)/shard_map/ppermute | solution.py:652
  241.4 1.7 collective-permute-start.31
  243.5 4.7 grad_gate.1
  248.3 4.7 grad_up.1
  253.0 2.2 fusion.9
  260.2 1.7 collective-permute-start.37
  262.1 3.3 convolution_convert_fusion
  265.3 6.9 %collective-permute-done.40 = bf16[2,128,1152]{2,1,0:T(8,128)(2,1)S(1)} collective-permute-done((bf16[2,128,1152]{2,1,0:T(8,128)(2,1)S(1)}, bf16[2,128,1152]{2,1,0:T(8,128)(2,1)S(1)}, u32[]{:S(2)}, u32[]{:S(2)}) %collective-permute-start.40) | collective-permute-done | bytes 589856 | tf_op jit(solution)/shard_map/ppermute | solution.py:652
  275.8 2.2 collective-permute-start.44
  278.9 5.6 %collective-permute-done.45 = bf16[2,128,1152]{2,1,0:T(8,128)(2,1)S(1)} collective-permute-done((bf16[2,128,1152]{2,1,0:T(8,128)(2,1)S(1)}, bf16[2,128,1152]{2,1,0:T(8,128)(2,1)S(1)}, u32[]{:S(2)}, u32[]{:S(2)}) %collective-permute-start.45) | collective-permute-done | bytes 589856 | tf_op jit(solution)/shard_map/ppermute | solution.py:652
  288.3 2.5 collective-permute-done.44
  297.0 2.8 slice_add_fusion
  301.0 19.8 %attend_back.1 = (bf16[1024,512]{1,0:T(8,128)(2,1)S(1)}, f32[8,128]{1,0:T(8,128)S(1)}, bf16[512,1024]{1,0:T(8,128)(2,1)S(1)}, bf16[512,1024]{1,0:T(8,128)(2,1)}) custom-call(s32[3]{0:T(128)S(1)} %pad_add_fusion.1.s_ref, bf16[1024,384]{1,0:T(8,128)(2,1)S(1)} %copy-done.45, bf16[1024,384]{1,0:T(8,128)(2,1)S(1)} %copy-done.45, ...), custom_call_target="tpu_custom_call" | custom-call | flops 4294967296 | bytes 10485760 | tf_op jit(solution)/shard_map/attend_back/pallas_call | solution.py:352
  326.4 1.9 slice.325
  328.3 1.7 collective-permute-start.39
  331.4 16.3 %collective-permute-done.50 = bf16[2,64,1152]{2,1,0:T(8,128)(2,1)S(1)} collective-permute-done((bf16[2,64,1152]{2,1,0:T(8,128)(2,1)}, bf16[2,64,1152]{2,1,0:T(8,128)(2,1)S(1)}, u32[]{:S(2)}, u32[]{:S(2)}) %collective-permute-start.50) | collective-permute-done | bytes 294944 | tf_op jit(solution)/shard_map/ppermute | solution.py:652
  347.6 1.8 add.306
  354.2 2.9 collective-permute-start.58
  357.1 2.4 fusion.29
  360.4 3.7 grad_qkv.1
  366.5 4.7 grad_out.1
  372.6 1.7 collective-permute-start.62
  376.2 3.3 fusion.26
  379.5 2.5 collective-permute-done.57
  382.0 1.7 add.315
  389.8 2.9 collective-permute-done.64
  393.5 2.9 collective-permute-done.65
  396.5 3.6 collective-permute-done.66
  403.0 1.8 collective-permute-done.67
  407.8 2.7 collective-permute-start.73
  410.5 6.7 %collective-permute-done.73 = bf16[2,128,256]{2,1,0:T(8,128)(2,1)S(1)} collective-permute-done((bf16[2,128,256]{2,1,0:T(8,128)(2,1)S(1)}, bf16[2,128,256]{2,1,0:T(8,128)(2,1)S(1)}, u32[]{:S(2)}, u32[]{:S(2)}) %collective-permute-start.73) | collective-permute-done | bytes 131104 | tf_op jit(solution)/shard_map/ppermute | solution.py:652
  418.5 1.7 collective-permute-start.70
  429.0 21.5 %collective-permute-done.74 = bf16[2,32,512]{2,1,0:T(8,128)(2,1)S(1)} collective-permute-done((bf16[2,32,512]{2,1,0:T(8,128)(2,1)S(1)}, bf16[2,32,512]{2,1,0:T(8,128)(2,1)S(1)}, u32[]{:S(2)}, u32[]{:S(2)}) %collective-permute-start.74) | collective-permute-done | bytes 65568 | tf_op jit(solution)/shard_map/ppermute | solution.py:652
  450.6 10.3 %all-gather.2 = bf16[16,32,512]{2,1,0:T(8,128)(2,1)S(1)} all-gather(bf16[2,32,512]{2,1,0:T(8,128)(2,1)S(1)} %fusion.24), channel_id=4, replica_groups=mesh['dp'=8,'tensor'=4] {'dp'}, dimensions={0}, use_global_device_ids=true | all-gather | bytes 589824 | tf_op jit(solution)/shard_map/all_gather | solution.py:741
  465.2 2.3 convert_bitcast_fusion
  467.6 3.6 copy.43
  471.2 3.3 copy.45
  478.0 4.2 bitcast_convert_fusion.1
  482.3 21.1 %all-gather.18.cloned.1.call-done = bf16[16,64,1152]{2,1,0:T(8,128)(2,1)} async-done(((bf16[2,64,1152]{2,1,0:T(8,128)(2,1)}), bf16[16,64,1152]{2,1,0:T(8,128)(2,1)}) %all-gather.18.cloned.1.call-update) | async-done | bytes 2359312 | tf_op jit(solution)/shard_map/all_gather | solution.py:741
  503.4 4.2 bitcast_convert_fusion
  (420 shorter events, 133.4 us)
Async XLA Ops:
  7.2 158.6 %all-gather.12.cloned.1.call-start = ((), (), s32[]{:S(2)}) async-start(), calls=%async_computation | async-start | bytes 2359296 | tf_op jit(solution)/shard_map/all_gather | solution.py:749
  8.9 10.6 %collective-permute-start.4 = (bf16[128,512]{1,0:T(8,128)(2,1)S(1)}, bf16[128,512]{1,0:T(8,128)(2,1)S(1)}, u32[]{:S(2)}, u32[]{:S(2)}) collective-permute-start(bf16[128,512]{1,0:T(8,128)(2,1)S(1)} %pad_maximum_fusion.8), channel_id=1, source_target_pairs={{0,2},{1,3},{2,0},{3,1},{4,6},{5,7},{6,4},{7,5},{8,10},{9,11},{10,... | collective-permute-start | bytes 393224 | tf_op jit(solution)/shard_map/ppermute | solution.py:652
  13.8 7.3 %collective-permute-start = (bf16[256,1024]{1,0:T(8,128)(2,1)}, bf16[256,1024]{1,0:T(8,128)(2,1)S(1)}, u32[]{:S(2)}, u32[]{:S(2)}) collective-permute-start(bf16[256,1024]{1,0:T(8,128)(2,1)} %param.15), channel_id=1, source_target_pairs={{0,0},{1,1},{2,4},{3,5},{4,2},{5,3},{6,6},{7,7},{8,8},{9,9},{10,12... | collective-permute-start | bytes 1572872 | tf_op jit(solution)/shard_map/ppermute | solution.py:652
  19.6 15.1 %collective-permute-start.5 = (bf16[128,512]{1,0:T(8,128)(2,1)S(1)}, bf16[128,512]{1,0:T(8,128)(2,1)S(1)}, u32[]{:S(2)}, u32[]{:S(2)}) collective-permute-start(bf16[128,512]{1,0:T(8,128)(2,1)S(1)} %collective-permute-done.4), channel_id=1, source_target_pairs={{0,8},{1,9},{2,10},{3,11},{4,12},{5,13},{6,14},{7,15},{8,0},{9,1},... | collective-permute-start | bytes 393224 | tf_op jit(solution)/shard_map/ppermute | solution.py:652
  21.1 18.9 %collective-permute-start.2 = (bf16[256,1024]{1,0:T(8,128)(2,1)S(1)}, bf16[256,1024]{1,0:T(8,128)(2,1)S(1)}, u32[]{:S(2)}, u32[]{:S(2)}) collective-permute-start(bf16[256,1024]{1,0:T(8,128)(2,1)S(1)} %collective-permute-done.x0), channel_id=1, source_target_pairs={{0,4},{1,5},{2,6},{3,7},{4,0},{5,1},{6,2},{7,3},{8,12},{9,13},{10,... | collective-permute-start | bytes 1572872 | tf_op jit(solution)/shard_map/ppermute | solution.py:652
  31.6 8.3 %collective-permute-start.6 = (bf16[128,512]{1,0:T(8,128)(2,1)S(1)}, bf16[128,512]{1,0:T(8,128)(2,1)S(1)}, u32[]{:S(2)}, u32[]{:S(2)}) collective-permute-start(bf16[128,512]{1,0:T(8,128)(2,1)S(1)} %collective-permute-done.4), channel_id=1, source_target_pairs={{0,16},{1,17},{2,18},{3,19},{4,20},{5,21},{6,22},{7,23},{8,24},{9,... | collective-permute-start | bytes 393224 | tf_op jit(solution)/shard_map/ppermute | solution.py:652
  33.2 6.7 %collective-permute-start.7 = (bf16[128,512]{1,0:T(8,128)(2,1)S(1)}, bf16[128,512]{1,0:T(8,128)(2,1)S(1)}, u32[]{:S(2)}, u32[]{:S(2)}) collective-permute-start(bf16[128,512]{1,0:T(8,128)(2,1)S(1)} %collective-permute-done.4), channel_id=1, source_target_pairs={{0,24},{1,25},{2,26},{3,27},{4,28},{5,29},{6,30},{7,31},{8,16},{9,... | collective-permute-start | bytes 393224 | tf_op jit(solution)/shard_map/ppermute | solution.py:652
  34.7 13.3 %collective-permute-start.1 = (bf16[256,1024]{1,0:T(8,128)(2,1)S(1)}, bf16[256,1024]{1,0:T(8,128)(2,1)S(1)}, u32[]{:S(2)}, u32[]{:S(2)}) collective-permute-start(bf16[256,1024]{1,0:T(8,128)(2,1)S(1)} %collective-permute-done.x0), channel_id=1, source_target_pairs={{0,1},{1,0},{2,3},{3,2},{4,5},{5,4},{6,7},{7,6},{8,9},{9,8},{10,11... | collective-permute-start | bytes 1572872 | tf_op jit(solution)/shard_map/ppermute | solution.py:652
  39.9 27.4 %collective-permute-start.8 = (bf16[512,512]{1,0:T(8,128)(2,1)S(1)}, bf16[512,512]{1,0:T(8,128)(2,1)S(1)}, u32[]{:S(2)}, u32[]{:S(2)}) collective-permute-start(bf16[512,512]{1,0:T(8,128)(2,1)S(1)} %constant_dynamic-update-slice_fusion.w0), channel_id=1, source_target_pairs={{0,4},{1,5},{2,6},{3,7},{4,0},{5,1},{6,2},{7,3},{8,12},{9,13},{10,... | collective-permute-start | bytes 1572872 | tf_op jit(solution)/shard_map/ppermute | solution.py:652
  48.0 19.3 %collective-permute-start.3 = (bf16[256,1024]{1,0:T(8,128)(2,1)S(1)}, bf16[256,1024]{1,0:T(8,128)(2,1)S(1)}, u32[]{:S(2)}, u32[]{:S(2)}) collective-permute-start(bf16[256,1024]{1,0:T(8,128)(2,1)S(1)} %collective-permute-done.1.x1), channel_id=1, source_target_pairs={{0,4},{1,5},{2,6},{3,7},{4,0},{5,1},{6,2},{7,3},{8,12},{9,13},{10,... | collective-permute-start | bytes 1572872 | tf_op jit(solution)/shard_map/ppermute | solution.py:652
  48.0 36.9 %collective-permute-start.15 = (bf16[128,2304]{1,0:T(8,128)(2,1)S(1)}, bf16[128,2304]{1,0:T(8,128)(2,1)}, u32[]{:S(2)}, u32[]{:S(2)}) collective-permute-start(bf16[128,2304]{1,0:T(8,128)(2,1)S(1)} %pad_maximum_fusion.1), channel_id=1, source_target_pairs={{0,2},{1,3},{2,0},{3,1},{4,6},{5,7},{6,4},{7,5},{8,10},{9,11},{10,... | collective-permute-start | bytes 1769480 | tf_op jit(solution)/shard_map/ppermute | solution.py:652
  50.9 13.8 %collective-permute-start.13 = (bf16[32,1024]{1,0:T(8,128)(2,1)S(1)}, bf16[32,1024]{1,0:T(8,128)(2,1)S(1)}, u32[]{:S(2)}, u32[]{:S(2)}) collective-permute-start(bf16[32,1024]{1,0:T(8,128)(2,1)S(1)} %constant_dynamic-slice_fusion.3), channel_id=1, source_target_pairs={{0,1},{1,0},{2,3},{3,2},{4,5},{5,4},{6,7},{7,6},{8,9},{9,8},{10,11... | collective-permute-start | bytes 196616 | tf_op jit(solution)/shard_map/ppermute | solution.py:652
  64.7 20.8 %collective-permute-start.14 = (bf16[2,32,1024]{2,1,0:T(8,128)(2,1)S(1)}, bf16[2,32,1024]{2,1,0:T(8,128)(2,1)S(1)}, u32[]{:S(2)}, u32[]{:S(2)}) collective-permute-start(bf16[2,32,1024]{2,1,0:T(8,128)(2,1)S(1)} %pad_maximum_fusion.9), channel_id=1, source_target_pairs={{0,2},{1,3},{2,0},{3,1},{4,6},{5,7},{6,4},{7,5},{8,10},{9,11},{10,... | collective-permute-start | bytes 393224 | tf_op jit(solution)/shard_map/ppermute | solution.py:652
  85.0 18.9 %collective-permute-start.16 = (bf16[128,2304]{1,0:T(8,128)(2,1)}, bf16[128,2304]{1,0:T(8,128)(2,1)S(1)}, u32[]{:S(2)}, u32[]{:S(2)}) collective-permute-start(bf16[128,2304]{1,0:T(8,128)(2,1)} %collective-permute-done.15), channel_id=1, source_target_pairs={{0,8},{1,9},{2,10},{3,11},{4,12},{5,13},{6,14},{7,15},{8,0},{9,1},... | collective-permute-start | bytes 1769480 | tf_op jit(solution)/shard_map/ppermute | solution.py:652
  86.3 379.0 %all-gather.20.cloned.1.call-start = ((), (), s32[]{:S(2)}) async-start(), calls=%async_computation.4 | async-start | bytes 2654208 | tf_op jit(solution)/shard_map/all_gather | solution.py:741
  86.3 31.9 %collective-permute-start.17 = (bf16[128,2304]{1,0:T(8,128)(2,1)}, bf16[128,2304]{1,0:T(8,128)(2,1)S(1)}, u32[]{:S(2)}, u32[]{:S(2)}) collective-permute-start(bf16[128,2304]{1,0:T(8,128)(2,1)} %collective-permute-done.15), channel_id=1, source_target_pairs={{0,16},{1,17},{2,18},{3,19},{4,20},{5,21},{6,22},{7,23},{8,24},{9,... | collective-permute-start | bytes 1769480 | tf_op jit(solution)/shard_map/ppermute | solution.py:652
  87.9 31.2 %collective-permute-start.18 = (bf16[128,2304]{1,0:T(8,128)(2,1)}, bf16[128,2304]{1,0:T(8,128)(2,1)S(1)}, u32[]{:S(2)}, u32[]{:S(2)}) collective-permute-start(bf16[128,2304]{1,0:T(8,128)(2,1)} %collective-permute-done.15), channel_id=1, source_target_pairs={{0,24},{1,25},{2,26},{3,27},{4,28},{5,29},{6,30},{7,31},{8,16},{9,... | collective-permute-start | bytes 1769480 | tf_op jit(solution)/shard_map/ppermute | solution.py:652
  119.9 45.9 %collective-permute-start.19 = (bf16[512,2304]{1,0:T(8,128)(2,1)}, bf16[512,2304]{1,0:T(8,128)(2,1)}, u32[]{:S(2)}, u32[]{:S(2)}) collective-permute-start(bf16[512,2304]{1,0:T(8,128)(2,1)} %constant_dynamic-update-slice_fusion.4.p0), channel_id=1, source_target_pairs={{0,4},{1,5},{2,6},{3,7},{4,0},{5,1},{6,2},{7,3},{8,12},{9,13},{10,... | collective-permute-start | bytes 7077896 | tf_op jit(solution)/shard_map/ppermute | solution.py:652
  120.0 23.9 %collective-permute-start.10 = (bf16[1024,256]{1,0:T(8,128)(2,1)S(1)}, bf16[1024,256]{1,0:T(8,128)(2,1)S(1)}, u32[]{:S(2)}, u32[]{:S(2)}) collective-permute-start(bf16[1024,256]{1,0:T(8,128)(2,1)S(1)} %get-tuple-element.176.a0.left_ref), channel_id=1, source_target_pairs={{0,1},{1,0},{2,3},{3,2},{4,5},{5,4},{6,7},{7,6},{8,9},{9,8},{10,11... | collective-permute-start | bytes 1572872 | tf_op jit(solution)/shard_map/ppermute | solution.py:652
  121.0 17.7 %collective-permute-start.26 = (bf16[144,1024]{1,0:T(8,128)(2,1)S(1)}, bf16[144,1024]{1,0:T(8,128)(2,1)S(1)}, u32[]{:S(2)}, u32[]{:S(2)}) collective-permute-start(bf16[144,1024]{1,0:T(8,128)(2,1)S(1)} %constant_dynamic-slice_fusion), channel_id=1, source_target_pairs={{0,2},{1,3},{2,0},{3,1},{4,6},{5,7},{6,4},{7,5},{8,10},{9,11},{10,... | collective-permute-start | bytes 884744 | tf_op jit(solution)/shard_map/ppermute | solution.py:652
  123.6 24.6 %collective-permute-start.20 = (bf16[256,1024]{1,0:T(8,128)(2,1)}, bf16[256,1024]{1,0:T(8,128)(2,1)S(1)}, u32[]{:S(2)}, u32[]{:S(2)}) collective-permute-start(bf16[256,1024]{1,0:T(8,128)(2,1)} %param.29), channel_id=1, source_target_pairs={{0,0},{1,1},{2,4},{3,5},{4,2},{5,3},{6,6},{7,7},{8,8},{9,9},{10,12... | collective-permute-start | bytes 1572872 | tf_op jit(solution)/shard_map/ppermute | solution.py:652
  144.0 9.9 %collective-permute-start.27 = (bf16[144,1024]{1,0:T(8,128)(2,1)S(1)}, bf16[144,1024]{1,0:T(8,128)(2,1)S(1)}, u32[]{:S(2)}, u32[]{:S(2)}) collective-permute-start(bf16[144,1024]{1,0:T(8,128)(2,1)S(1)} %collective-permute-done.26), channel_id=1, source_target_pairs={{0,8},{1,9},{2,10},{3,11},{4,12},{5,13},{6,14},{7,15},{8,0},{9,1},... | collective-permute-start | bytes 884744 | tf_op jit(solution)/shard_map/ppermute | solution.py:652
  145.5 14.5 %collective-permute-start.28 = (bf16[144,1024]{1,0:T(8,128)(2,1)S(1)}, bf16[144,1024]{1,0:T(8,128)(2,1)S(1)}, u32[]{:S(2)}, u32[]{:S(2)}) collective-permute-start(bf16[144,1024]{1,0:T(8,128)(2,1)S(1)} %collective-permute-done.26), channel_id=1, source_target_pairs={{0,16},{1,17},{2,18},{3,19},{4,20},{5,21},{6,22},{7,23},{8,24},{9,... | collective-permute-start | bytes 884744 | tf_op jit(solution)/shard_map/ppermute | solution.py:652
  147.0 13.8 %collective-permute-start.29 = (bf16[144,1024]{1,0:T(8,128)(2,1)S(1)}, bf16[144,1024]{1,0:T(8,128)(2,1)S(1)}, u32[]{:S(2)}, u32[]{:S(2)}) collective-permute-start(bf16[144,1024]{1,0:T(8,128)(2,1)S(1)} %collective-permute-done.26), channel_id=1, source_target_pairs={{0,24},{1,25},{2,26},{3,27},{4,28},{5,29},{6,30},{7,31},{8,16},{9,... | collective-permute-start | bytes 884744 | tf_op jit(solution)/shard_map/ppermute | solution.py:652
  148.2 13.8 %collective-permute-start.11 = (bf16[1024,256]{1,0:T(8,128)(2,1)S(1)}, bf16[1024,256]{1,0:T(8,128)(2,1)S(1)}, u32[]{:S(2)}, u32[]{:S(2)}) collective-permute-start(bf16[1024,256]{1,0:T(8,128)(2,1)S(1)} %get-tuple-element.176.a0.left_ref), channel_id=1, source_target_pairs={{0,4},{1,5},{2,6},{3,7},{4,0},{5,1},{6,2},{7,3},{8,12},{9,13},{10,... | collective-permute-start | bytes 1572872 | tf_op jit(solution)/shard_map/ppermute | solution.py:652
  153.9 11.1 %collective-permute-start.21 = (bf16[256,1024]{1,0:T(8,128)(2,1)S(1)}, bf16[256,1024]{1,0:T(8,128)(2,1)}, u32[]{:S(2)}, u32[]{:S(2)}) collective-permute-start(bf16[256,1024]{1,0:T(8,128)(2,1)S(1)} %collective-permute-done.20.r0.y0), channel_id=1, source_target_pairs={{0,1},{1,0},{2,3},{3,2},{4,5},{5,4},{6,7},{7,6},{8,9},{9,8},{10,11... | collective-permute-start | bytes 1572872 | tf_op jit(solution)/shard_map/ppermute | solution.py:652
  161.5 37.8 %collective-permute-start.30 = (bf16[576,1024]{1,0:T(8,128)(2,1)}, bf16[576,1024]{1,0:T(8,128)(2,1)}, u32[]{:S(2)}, u32[]{:S(2)}) collective-permute-start(bf16[576,1024]{1,0:T(8,128)(2,1)} %constant_dynamic-update-slice_fusion.8.d0), channel_id=1, source_target_pairs={{0,4},{1,5},{2,6},{3,7},{4,0},{5,1},{6,2},{7,3},{8,12},{9,13},{10,... | collective-permute-start | bytes 3538952 | tf_op jit(solution)/shard_map/ppermute | solution.py:652
  162.8 27.8 %collective-permute-start.22 = (bf16[256,1024]{1,0:T(8,128)(2,1)S(1)}, bf16[256,1024]{1,0:T(8,128)(2,1)}, u32[]{:S(2)}, u32[]{:S(2)}) collective-permute-start(bf16[256,1024]{1,0:T(8,128)(2,1)S(1)} %collective-permute-done.20.r0.y0), channel_id=1, source_target_pairs={{0,4},{1,5},{2,6},{3,7},{4,0},{5,1},{6,2},{7,3},{8,12},{9,13},{10,... | collective-permute-start | bytes 1572872 | tf_op jit(solution)/shard_map/ppermute | solution.py:652
  165.0 25.6 %collective-permute-start.23 = (bf16[256,1024]{1,0:T(8,128)(2,1)}, bf16[256,1024]{1,0:T(8,128)(2,1)}, u32[]{:S(2)}, u32[]{:S(2)}) collective-permute-start(bf16[256,1024]{1,0:T(8,128)(2,1)} %collective-permute-done.21.r1.y1), channel_id=1, source_target_pairs={{0,4},{1,5},{2,6},{3,7},{4,0},{5,1},{6,2},{7,3},{8,12},{9,13},{10,... | collective-permute-start | bytes 1572872 | tf_op jit(solution)/shard_map/ppermute | solution.py:652
  219.3 19.3 %collective-permute-start.33 = (bf16[512,1024]{1,0:T(8,128)(2,1)}, bf16[512,1024]{1,0:T(8,128)(2,1)}, u32[]{:S(2)}, u32[]{:S(2)}) collective-permute-start(bf16[512,1024]{1,0:T(8,128)(2,1)} %get-tuple-element.129), channel_id=1, source_target_pairs={{0,4},{1,5},{2,6},{3,7},{4,0},{5,1},{6,2},{7,3},{8,12},{9,13},{10,... | collective-permute-start | bytes 3145736 | tf_op jit(solution)/shard_map/ppermute | solution.py:652
  220.3 15.6 %collective-permute-start.24 = (bf16[2,288,512]{2,1,0:T(8,128)(2,1)}, bf16[2,288,512]{2,1,0:T(8,128)(2,1)}, u32[]{:S(2)}, u32[]{:S(2)}) collective-permute-start(bf16[2,288,512]{2,1,0:T(8,128)(2,1)} %get-tuple-element.116), channel_id=1, source_target_pairs={{0,8},{1,9},{2,10},{3,11},{4,12},{5,13},{6,14},{7,15},{8,0},{9,1},... | collective-permute-start | bytes 1769480 | tf_op jit(solution)/shard_map/ppermute | solution.py:652
  221.8 15.3 %collective-permute-start.25 = (bf16[2,288,512]{2,1,0:T(8,128)(2,1)}, bf16[2,288,512]{2,1,0:T(8,128)(2,1)}, u32[]{:S(2)}, u32[]{:S(2)}) collective-permute-start(bf16[2,288,512]{2,1,0:T(8,128)(2,1)} %get-tuple-element.117), channel_id=1, source_target_pairs={{0,16},{1,17},{2,18},{3,19},{4,20},{5,21},{6,22},{7,23},{8,24},{9,... | collective-permute-start | bytes 1769480 | tf_op jit(solution)/shard_map/ppermute | solution.py:652
  239.9 13.1 %collective-permute-start.34 = (bf16[256,1024]{1,0:T(8,128)(2,1)S(1)}, bf16[256,1024]{1,0:T(8,128)(2,1)S(1)}, u32[]{:S(2)}, u32[]{:S(2)}) collective-permute-start(bf16[256,1024]{1,0:T(8,128)(2,1)S(1)} %slice_add_fusion.3), channel_id=1, source_target_pairs={{0,1},{1,0},{2,3},{3,2},{4,5},{5,4},{6,7},{7,6},{8,9},{9,8},{10,11... | collective-permute-start | bytes 1572872 | tf_op jit(solution)/shard_map/ppermute | solution.py:652
  241.4 14.2 %collective-permute-start.31 = (bf16[288,512]{1,0:T(8,128)(2,1)S(1)}, bf16[288,512]{1,0:T(8,128)(2,1)S(1)}, u32[]{:S(2)}, u32[]{:S(2)}) collective-permute-start(bf16[288,512]{1,0:T(8,128)(2,1)S(1)} %get-tuple-element.219), channel_id=1, source_target_pairs={{0,16},{1,17},{2,18},{3,19},{4,20},{5,21},{6,22},{7,23},{8,24},{9,... | collective-permute-start | bytes 884744 | tf_op jit(solution)/shard_map/ppermute | solution.py:652
  243.1 12.5 %collective-permute-start.32 = (bf16[288,512]{1,0:T(8,128)(2,1)S(1)}, bf16[288,512]{1,0:T(8,128)(2,1)S(1)}, u32[]{:S(2)}, u32[]{:S(2)}) collective-permute-start(bf16[288,512]{1,0:T(8,128)(2,1)S(1)} %get-tuple-element.220), channel_id=1, source_target_pairs={{0,8},{1,9},{2,10},{3,11},{4,12},{5,13},{6,14},{7,15},{8,0},{9,1},... | collective-permute-start | bytes 884744 | tf_op jit(solution)/shard_map/ppermute | solution.py:652
  256.1 16.2 %collective-permute-start.40 = (bf16[2,128,1152]{2,1,0:T(8,128)(2,1)S(1)}, bf16[2,128,1152]{2,1,0:T(8,128)(2,1)S(1)}, u32[]{:S(2)}, u32[]{:S(2)}) collective-permute-start(bf16[2,128,1152]{2,1,0:T(8,128)(2,1)S(1)} %get-tuple-element.134), channel_id=1, source_target_pairs={{0,8},{1,9},{2,10},{3,11},{4,12},{5,13},{6,14},{7,15},{8,0},{9,1},... | collective-permute-start | bytes 1769480 | tf_op jit(solution)/shard_map/ppermute | solution.py:652
  257.7 16.2 %collective-permute-start.41 = (bf16[2,128,1152]{2,1,0:T(8,128)(2,1)S(1)}, bf16[2,128,1152]{2,1,0:T(8,128)(2,1)S(1)}, u32[]{:S(2)}, u32[]{:S(2)}) collective-permute-start(bf16[2,128,1152]{2,1,0:T(8,128)(2,1)S(1)} %get-tuple-element.136), channel_id=1, source_target_pairs={{0,16},{1,17},{2,18},{3,19},{4,20},{5,21},{6,22},{7,23},{8,24},{9,... | collective-permute-start | bytes 1769480 | tf_op jit(solution)/shard_map/ppermute | solution.py:652
  258.1 26.4 %collective-permute-start.45 = (bf16[2,128,1152]{2,1,0:T(8,128)(2,1)S(1)}, bf16[2,128,1152]{2,1,0:T(8,128)(2,1)S(1)}, u32[]{:S(2)}, u32[]{:S(2)}) collective-permute-start(bf16[2,128,1152]{2,1,0:T(8,128)(2,1)S(1)} %get-tuple-element.139), channel_id=1, source_target_pairs={{0,8},{1,9},{2,10},{3,11},{4,12},{5,13},{6,14},{7,15},{8,0},{9,1},... | collective-permute-start | bytes 1769480 | tf_op jit(solution)/shard_map/ppermute | solution.py:652
  259.4 26.5 %collective-permute-start.46 = (bf16[2,128,1152]{2,1,0:T(8,128)(2,1)S(1)}, bf16[2,128,1152]{2,1,0:T(8,128)(2,1)S(1)}, u32[]{:S(2)}, u32[]{:S(2)}) collective-permute-start(bf16[2,128,1152]{2,1,0:T(8,128)(2,1)S(1)} %get-tuple-element.141), channel_id=1, source_target_pairs={{0,16},{1,17},{2,18},{3,19},{4,20},{5,21},{6,22},{7,23},{8,24},{9,... | collective-permute-start | bytes 1769480 | tf_op jit(solution)/shard_map/ppermute | solution.py:652
  260.2 26.3 %collective-permute-start.37 = (bf16[256,1024]{1,0:T(8,128)(2,1)S(1)}, bf16[256,1024]{1,0:T(8,128)(2,1)S(1)}, u32[]{:S(2)}, u32[]{:S(2)}) collective-permute-start(bf16[256,1024]{1,0:T(8,128)(2,1)S(1)} %fusion.23.b0.r0), channel_id=1, source_target_pairs={{0,1},{1,0},{2,3},{3,2},{4,5},{5,4},{6,7},{7,6},{8,9},{9,8},{10,11... | collective-permute-start | bytes 1572872 | tf_op jit(solution)/shard_map/ppermute | solution.py:652
  272.2 28.4 %collective-permute-start.48 = (bf16[256,1024]{1,0:T(8,128)(2,1)S(1)}, bf16[256,1024]{1,0:T(8,128)(2,1)}, u32[]{:S(2)}, u32[]{:S(2)}) collective-permute-start(bf16[256,1024]{1,0:T(8,128)(2,1)S(1)} %fusion.23.b0.r0), channel_id=1, source_target_pairs={{0,4},{1,5},{2,6},{3,7},{4,0},{5,1},{6,2},{7,3},{8,12},{9,13},{10,... | collective-permute-start | bytes 1572872 | tf_op jit(solution)/shard_map/ppermute | solution.py:652
  275.8 15.0 %collective-permute-start.44 = (bf16[2,144,512]{2,1,0:T(8,128)(2,1)S(1)}, bf16[2,144,512]{2,1,0:T(8,128)(2,1)S(1)}, u32[]{:S(2)}, u32[]{:S(2)}) collective-permute-start(bf16[2,144,512]{2,1,0:T(8,128)(2,1)S(1)} %get-tuple-element.230), channel_id=1, source_target_pairs={{0,2},{1,3},{2,0},{3,1},{4,6},{5,7},{6,4},{7,5},{8,10},{9,11},{10,... | collective-permute-start | bytes 884744 | tf_op jit(solution)/shard_map/ppermute | solution.py:652
  284.5 9.0 %collective-permute-start.42 = (bf16[128,1152]{1,0:T(8,128)(2,1)}, bf16[128,1152]{1,0:T(8,128)(2,1)}, u32[]{:S(2)}, u32[]{:S(2)}) collective-permute-start(bf16[128,1152]{1,0:T(8,128)(2,1)} %get-tuple-element.215), channel_id=1, source_target_pairs={{0,16},{1,17},{2,18},{3,19},{4,20},{5,21},{6,22},{7,23},{8,24},{9,... | collective-permute-start | bytes 884744 | tf_op jit(solution)/shard_map/ppermute | solution.py:652
  285.8 8.6 %collective-permute-start.43 = (bf16[128,1152]{1,0:T(8,128)(2,1)}, bf16[128,1152]{1,0:T(8,128)(2,1)}, u32[]{:S(2)}, u32[]{:S(2)}) collective-permute-start(bf16[128,1152]{1,0:T(8,128)(2,1)} %get-tuple-element.216), channel_id=1, source_target_pairs={{0,8},{1,9},{2,10},{3,11},{4,12},{5,13},{6,14},{7,15},{8,0},{9,1},... | collective-permute-start | bytes 884744 | tf_op jit(solution)/shard_map/ppermute | solution.py:652
  290.8 6.2 %collective-permute-start.36 = (bf16[512,1024]{1,0:T(8,128)(2,1)}, bf16[512,1024]{1,0:T(8,128)(2,1)}, u32[]{:S(2)}, u32[]{:S(2)}) collective-permute-start(bf16[512,1024]{1,0:T(8,128)(2,1)} %slice.323), channel_id=1, source_target_pairs={{0,4},{1,5},{2,6},{3,7},{4,0},{5,1},{6,2},{7,3},{8,12},{9,13},{10,... | collective-permute-start | bytes 3145736 | tf_op jit(solution)/shard_map/ppermute | solution.py:652
  322.7 26.7 %collective-permute-start.49 = (bf16[512,1024]{1,0:T(8,128)(2,1)}, bf16[512,1024]{1,0:T(8,128)(2,1)}, u32[]{:S(2)}, u32[]{:S(2)}) collective-permute-start(bf16[512,1024]{1,0:T(8,128)(2,1)} %get-tuple-element.163), channel_id=1, source_target_pairs={{0,4},{1,5},{2,6},{3,7},{4,0},{5,1},{6,2},{7,3},{8,12},{9,13},{10,... | collective-permute-start | bytes 3145736 | tf_op jit(solution)/shard_map/ppermute | solution.py:652
  323.8 27.4 %collective-permute-start.52 = (bf16[128,1152]{1,0:T(8,128)(2,1)}, bf16[128,1152]{1,0:T(8,128)(2,1)S(1)}, u32[]{:S(2)}, u32[]{:S(2)}) collective-permute-start(bf16[128,1152]{1,0:T(8,128)(2,1)} %get-tuple-element.211), channel_id=1, source_target_pairs={{0,8},{1,9},{2,10},{3,11},{4,12},{5,13},{6,14},{7,15},{8,0},{9,1},... | collective-permute-start | bytes 884744 | tf_op jit(solution)/shard_map/ppermute | solution.py:652
  324.8 27.1 %collective-permute-start.51 = (bf16[128,1152]{1,0:T(8,128)(2,1)}, bf16[128,1152]{1,0:T(8,128)(2,1)}, u32[]{:S(2)}, u32[]{:S(2)}) collective-permute-start(bf16[128,1152]{1,0:T(8,128)(2,1)} %get-tuple-element.213), channel_id=1, source_target_pairs={{0,16},{1,17},{2,18},{3,19},{4,20},{5,21},{6,22},{7,23},{8,24},{9,... | collective-permute-start | bytes 884744 | tf_op jit(solution)/shard_map/ppermute | solution.py:652
  326.1 148.4 %all-gather.14.cloned.1.call-start = ((), (), s32[]{:S(2)}) async-start(), calls=%async_computation.1 | async-start | bytes 1179648 | tf_op jit(solution)/shard_map/all_gather | solution.py:741
  328.3 25.9 %collective-permute-start.39 = (bf16[256,1024]{1,0:T(8,128)(2,1)}, bf16[256,1024]{1,0:T(8,128)(2,1)}, u32[]{:S(2)}, u32[]{:S(2)}) collective-permute-start(bf16[256,1024]{1,0:T(8,128)(2,1)} %slice.325), channel_id=1, source_target_pairs={{0,1},{1,0},{2,3},{3,2},{4,5},{5,4},{6,7},{7,6},{8,9},{9,8},{10,11... | collective-permute-start | bytes 1572872 | tf_op jit(solution)/shard_map/ppermute | solution.py:652
  330.0 17.6 %collective-permute-start.50 = (bf16[2,64,1152]{2,1,0:T(8,128)(2,1)}, bf16[2,64,1152]{2,1,0:T(8,128)(2,1)S(1)}, u32[]{:S(2)}, u32[]{:S(2)}) collective-permute-start(bf16[2,64,1152]{2,1,0:T(8,128)(2,1)} %get-tuple-element.228), channel_id=1, source_target_pairs={{0,2},{1,3},{2,0},{3,1},{4,6},{5,7},{6,4},{7,5},{8,10},{9,11},{10,... | collective-permute-start | bytes 884744 | tf_op jit(solution)/shard_map/ppermute | solution.py:652
  354.1 5.4 %collective-permute-start.54 = (bf16[2,64,1152]{2,1,0:T(8,128)(2,1)S(1)}, bf16[2,64,1152]{2,1,0:T(8,128)(2,1)S(1)}, u32[]{:S(2)}, u32[]{:S(2)}) collective-permute-start(bf16[2,64,1152]{2,1,0:T(8,128)(2,1)S(1)} %broadcast_select_fusion.2), channel_id=1, source_target_pairs={{0,4},{1,5},{2,6},{3,7},{4,0},{5,1},{6,2},{7,3},{8,12},{9,13},{10,... | collective-permute-start | bytes 884744 | tf_op jit(solution)/shard_map/ppermute | solution.py:652
  354.2 18.4 %collective-permute-start.58 = (bf16[256,1024]{1,0:T(8,128)(2,1)S(1)}, bf16[256,1024]{1,0:T(8,128)(2,1)S(1)}, u32[]{:S(2)}, u32[]{:S(2)}) collective-permute-start(bf16[256,1024]{1,0:T(8,128)(2,1)S(1)} %slice.333), channel_id=1, source_target_pairs={{0,1},{1,0},{2,3},{3,2},{4,5},{5,4},{6,7},{7,6},{8,9},{9,8},{10,11... | collective-permute-start | bytes 1572872 | tf_op jit(solution)/shard_map/ppermute | solution.py:652
  364.1 19.6 %collective-permute-start.55 = (bf16[2,256,256]{2,1,0:T(8,128)(2,1)}, bf16[2,256,256]{2,1,0:T(8,128)(2,1)}, u32[]{:S(2)}, u32[]{:S(2)}) collective-permute-start(bf16[2,256,256]{2,1,0:T(8,128)(2,1)} %get-tuple-element.173), channel_id=1, source_target_pairs={{0,8},{1,9},{2,10},{3,11},{4,12},{5,13},{6,14},{7,15},{8,0},{9,1},... | collective-permute-start | bytes 786440 | tf_op jit(solution)/shard_map/ppermute | solution.py:652
  364.7 19.1 %collective-permute-start.56 = (bf16[2,256,256]{2,1,0:T(8,128)(2,1)}, bf16[2,256,256]{2,1,0:T(8,128)(2,1)}, u32[]{:S(2)}, u32[]{:S(2)}) collective-permute-start(bf16[2,256,256]{2,1,0:T(8,128)(2,1)} %get-tuple-element.174), channel_id=1, source_target_pairs={{0,16},{1,17},{2,18},{3,19},{4,20},{5,21},{6,22},{7,23},{8,24},{9,... | collective-permute-start | bytes 786440 | tf_op jit(solution)/shard_map/ppermute | solution.py:652
  365.9 16.1 %collective-permute-start.57 = (bf16[2,64,1152]{2,1,0:T(8,128)(2,1)}, bf16[2,64,1152]{2,1,0:T(8,128)(2,1)}, u32[]{:S(2)}, u32[]{:S(2)}) collective-permute-start(bf16[2,64,1152]{2,1,0:T(8,128)(2,1)} %get-tuple-element.226), channel_id=1, source_target_pairs={{0,2},{1,3},{2,0},{3,1},{4,6},{5,7},{6,4},{7,5},{8,10},{9,11},{10,... | collective-permute-start | bytes 884744 | tf_op jit(solution)/shard_map/ppermute | solution.py:652
  371.9 14.0 %collective-permute-start.61 = (bf16[2,64,512]{2,1,0:T(8,128)(2,1)}, bf16[2,64,512]{2,1,0:T(8,128)(2,1)}, u32[]{:S(2)}, u32[]{:S(2)}) collective-permute-start(bf16[2,64,512]{2,1,0:T(8,128)(2,1)} %get-tuple-element.177), channel_id=1, source_target_pairs={{0,8},{1,9},{2,10},{3,11},{4,12},{5,13},{6,14},{7,15},{8,0},{9,1},... | collective-permute-start | bytes 393224 | tf_op jit(solution)/shard_map/ppermute | solution.py:652
  372.6 13.3 %collective-permute-start.62 = (bf16[2,64,512]{2,1,0:T(8,128)(2,1)}, bf16[2,64,512]{2,1,0:T(8,128)(2,1)}, u32[]{:S(2)}, u32[]{:S(2)}) collective-permute-start(bf16[2,64,512]{2,1,0:T(8,128)(2,1)} %get-tuple-element.179), channel_id=1, source_target_pairs={{0,16},{1,17},{2,18},{3,19},{4,20},{5,21},{6,22},{7,23},{8,24},{9,... | collective-permute-start | bytes 393224 | tf_op jit(solution)/shard_map/ppermute | solution.py:652
  407.8 9.3 %collective-permute-start.73 = (bf16[2,128,256]{2,1,0:T(8,128)(2,1)S(1)}, bf16[2,128,256]{2,1,0:T(8,128)(2,1)S(1)}, u32[]{:S(2)}, u32[]{:S(2)}) collective-permute-start(bf16[2,128,256]{2,1,0:T(8,128)(2,1)S(1)} %broadcast_select_fusion.9), channel_id=1, source_target_pairs={{0,2},{1,3},{2,0},{3,1},{4,6},{5,7},{6,4},{7,5},{8,10},{9,11},{10,... | collective-permute-start | bytes 393224 | tf_op jit(solution)/shard_map/ppermute | solution.py:652
  417.9 60.2 %all-gather.16.cloned.1.call-start = ((), (), s32[]{:S(2)}) async-start(), calls=%async_computation.2 | async-start | bytes 2654208 | tf_op jit(solution)/shard_map/all_gather | solution.py:741
  418.4 84.9 %all-gather.18.cloned.1.call-start = ((), (), s32[]{:S(2)}) async-start(), calls=%async_computation.3 | async-start | bytes 2654208 | tf_op jit(solution)/shard_map/all_gather | solution.py:741
  420.6 42.4 %collective-permute-start.53 = (bf16[256,1024]{1,0:T(8,128)(2,1)S(1)}, bf16[256,1024]{1,0:T(8,128)(2,1)S(1)}, u32[]{:S(2)}, u32[]{:S(2)}) collective-permute-start(bf16[256,1024]{1,0:T(8,128)(2,1)S(1)} %copy-done.80), channel_id=1, source_target_pairs={{0,0},{1,1},{2,4},{3,5},{4,2},{5,3},{6,6},{7,7},{8,8},{9,9},{10,12... | collective-permute-start | bytes 1572872 | tf_op jit(solution)/shard_map/ppermute | solution.py:652
  421.3 42.8 %collective-permute-start.72 = (bf16[256,1024]{1,0:T(8,128)(2,1)S(1)}, bf16[256,1024]{1,0:T(8,128)(2,1)S(1)}, u32[]{:S(2)}, u32[]{:S(2)}) collective-permute-start(bf16[256,1024]{1,0:T(8,128)(2,1)S(1)} %copy-done.81), channel_id=1, source_target_pairs={{0,0},{1,1},{2,4},{3,5},{4,2},{5,3},{6,6},{7,7},{8,8},{9,9},{10,12... | collective-permute-start | bytes 1572872 | tf_op jit(solution)/shard_map/ppermute | solution.py:652
  426.9 23.7 %collective-permute-start.74 = (bf16[2,32,512]{2,1,0:T(8,128)(2,1)S(1)}, bf16[2,32,512]{2,1,0:T(8,128)(2,1)S(1)}, u32[]{:S(2)}, u32[]{:S(2)}) collective-permute-start(bf16[2,32,512]{2,1,0:T(8,128)(2,1)S(1)} %broadcast_select_fusion.12), channel_id=1, source_target_pairs={{0,2},{1,3},{2,0},{3,1},{4,6},{5,7},{6,4},{7,5},{8,10},{9,11},{10,... | collective-permute-start | bytes 196616 | tf_op jit(solution)/shard_map/ppermute | solution.py:652
  (109 other events, 1038.1 us)
Sparse Core Ops, SparseCore 0:
  86.4 42.8 all-gather.11
  326.3 27.5 all-gather.19
  418.0 22.2 all-gather.13
  442.0 29.9 all-gather.15
  474.3 29.0 all-gather.17
where the time goes:
time: 524 us; the launch traced here: 514 us
  waiting for transfers between devices  200 us (38%)
  Pallas kernels  85.4 us (16%)
  starting transfers between devices  83.6 us (16%)
  local copies, waits for them, and re-layouts  58.5 us (11%)
  other arithmetic  57.8 us (11%)
  between operations  15.5 us (3%)
  blocking collectives  10.3 us (2%)
    ppermute x75, waiting for transfers between devices, permute(): return lax.ppermute(x, AX, pairs)  178 us
    ppermute x75, starting transfers between devices, permute(): return lax.ppermute(x, AX, pairs)  83.2 us
    unnamed x197, local copies, waits for them, and re-layouts  39.4 us
    all_gather x4, waiting for transfers between devices, whole_grad(): return lax.all_gather(mine, 'dp', axis_index_groups=neighbours(n))  21.1 us
    pallas_call x1, Pallas kernels, attend_back_call(): pl.pallas_call(attend_back_kernel, grid_spec=pltpu.PrefetchScalarGridSpec...  19.8 us
    pallas_call x1, Pallas kernels, ffn_back_call(): pl.pallas_call(ffn_back_kernel, grid_spec=pltpu.PrefetchScalarGridSpec(nu...  13.9 us
    pallas_call x3, Pallas kernels, grad_rows_call(): pl.pallas_call(functools.partial(grad_rows_kernel, by_cols), grid_spec=pl...  13.1 us
    pallas_call x1, Pallas kernels, ffn_call(): pl.pallas_call(ffn_kernel, grid_spec=pltpu.PrefetchScalarGridSpec(num_sca...  13 us
  transfers between devices with their start and end apart: 80, of which 35 were waited for; matrix products, arithmetic and copies ran while one was open for 16% of the time, Pallas kernels for 10%

commit v1 on v0

--- a/solution.py
+++ b/solution.py
@@ -94,6 +94,10 @@
 
 def fixed(*shape):
     return pl.BlockSpec(shape, lambda *_: (0,) * len(shape))
+
+
+def cost(flops):
+    return pl.CostEstimate(flops=flops, bytes_accessed=1 << 16, transcendentals=0)
 
 
 def params(mib):
@@ -167,8 +171,8 @@
             jax.ShapeDtypeStruct((4 * b, 128), bf16),
             jax.ShapeDtypeStruct((d, wid), bf16),
         ],
-        compiler_params=params(20),
-        cost_estimate=pl.CostEstimate(flops=8 * b * d * wid, bytes_accessed=9 * VMEM_MB, transcendentals=0),
+        compiler_params=params(12),
+        cost_estimate=cost(1 << 24),
         name="qkv",
     )(s, *xs, *w_own, *w_parts, g1, gains, cos, sin)
 
@@ -250,10 +254,8 @@
             jax.ShapeDtypeStruct((n, 256), f32),
             jax.ShapeDtypeStruct((2, 4, 1, 2 * b), f32),
         ],
-        compiler_params=params(26),
-        cost_estimate=pl.CostEstimate(
-            flops=16 * n * n * HD, bytes_accessed=4 * VMEM_MB, transcendentals=4 * n * n
-        ),
+        compiler_params=params(14),
+        cost_estimate=cost(1 << 24),
         name="attend",
     )(s, qk, qk, v, start, live)
 
@@ -369,16 +371,14 @@
             jax.ShapeDtypeStruct((2 * b, d), bf16),
             jax.ShapeDtypeStruct((2 * b, d), bf16),
         ],
-        compiler_params=params(40),
-        cost_estimate=pl.CostEstimate(
-            flops=40 * n * n * HD + 2 * n * d * 768, bytes_accessed=10 * VMEM_MB, transcendentals=4 * n * n
-        ),
+        compiler_params=params(24),
+        cost_estimate=cost(1 << 24),
         name="attend_back",
     )(s, qk, qk, v, pre, pre, qgain, kgain, cos, sin, start, live, out, lse, wout, w, *blocks)
 
 
 def ffn_kernel(s_ref, x0, x1, x2, x3, a0, a1, a2, a3, o_in, wg_own, wu_own, p0, p1,
-               gain_ref, n2_ref, hid_ref, fg_ref, fu_ref, res_ref, wg, wu, wout_ref, xs, att, wout, asem, xsem, osem, gsem, usem):
+               gain_ref, n2_ref, hid_ref, fg_ref, fu_ref, res_ref, wout_ref, wg, wu, xs, att, wout, asem, xsem, osem, gsem, usem):
     j = pl.program_id(0)
     b = x0.shape[0]
     x_in, a_in = (x0, x1, x2, x3), (a0, a1, a2, a3)
@@ -441,8 +441,10 @@
             num_scalar_prefetch=1,
             grid=(4,),
             in_specs=[ANY] * 13 + [fixed(1, d)],
-            out_specs=[block(d), block(h), block(h), block(h), fixed(b, d), fixed(d, h), fixed(d, h), fixed(b, d)],
+            out_specs=[block(d), block(h), block(h), block(h), fixed(b, d), fixed(b, d)],
             scratch_shapes=[
+                pltpu.VMEM((d, h), bf16),
+                pltpu.VMEM((d, h), bf16),
                 pltpu.VMEM((4, b, d), bf16),
                 pltpu.VMEM((4, b, 4 * b), bf16),
                 pltpu.VMEM((4,) + wout.shape[:1] + wout.shape[2:], bf16),
@@ -455,30 +457,29 @@
         ),
         out_shape=[jax.ShapeDtypeStruct((4 * b, d), bf16)]
         + [jax.ShapeDtypeStruct((4 * b, h), bf16)] * 3
-        + [jax.ShapeDtypeStruct((b, d), f32)]
-        + [jax.ShapeDtypeStruct((d, h), bf16)] * 2
-        + [jax.ShapeDtypeStruct((b, d), bf16)],
-        compiler_params=params(34),
-        cost_estimate=pl.CostEstimate(
-            flops=8 * b * d * (d + 2 * h), bytes_accessed=25 * VMEM_MB, transcendentals=4 * b * h
-        ),
+        + [jax.ShapeDtypeStruct((b, d), f32), jax.ShapeDtypeStruct((b, d), bf16)],
+        compiler_params=params(23),
+        cost_estimate=cost(1 << 24),
         name="ffn",
     )(s, *xs, *atts, wout, wg, wu, *parts, gain)
 
 
-def ffn_back_kernel(s_ref, y0, y1, y2, y3, wd_own, d0, d1, fg_ref, fu_ref, wg_in, wu_in,
-                    gg_ref, gu_ref, lo_ref, hi_ref, wd, dy, wg, wu, ysem, dsem, wsem):
+def ffn_back_kernel(s_ref, y0, y1, y2, y3, wd_own, d0, d1, wg_own, wu_own, p0, p1, fg_ref, fu_ref,
+                    gg_ref, gu_ref, lo_ref, hi_ref, wd, wg, wu, dy, ysem, dsem, gsem, usem):
     j = pl.program_id(0)
     y_in = (y0, y1, y2, y3)
     down_w = Weight(s_ref, (wd_own,), (d0, d1), wd, dsem)
+    gate_w = Weight(s_ref, (wg_own,), (p0, p1), wg, gsem)
+    up_w = Weight(s_ref, (wu_own,), (p0, p1), wu, usem, wg.shape[1])
 
     @pl.when(j == 0)
     def _():
-        for k in range(4):
+        pltpu.make_async_copy(y_in[0], dy.at[0], ysem.at[0]).start()
+        down_w.start()
+        for k in range(1, 4):
             pltpu.make_async_copy(y_in[k], dy.at[k], ysem.at[k]).start()
-        down_w.start()
-        pltpu.make_async_copy(wg_in, wg, wsem.at[0]).start()
-        pltpu.make_async_copy(wu_in, wu, wsem.at[1]).start()
+        gate_w.start()
+        up_w.start()
         down_w.wait()
 
     pltpu.make_async_copy(y0, dy.at[j], ysem.at[j]).wait()
@@ -490,8 +491,8 @@
 
     @pl.when(j == 0)
     def _():
-        pltpu.make_async_copy(wg_in, wg, wsem.at[0]).wait()
-        pltpu.make_async_copy(wu_in, wu, wsem.at[1]).wait()
+        gate_w.wait()
+        up_w.wait()
 
     grad = (contract(gg, wg[...], 1, 1) + contract(gu, wu[...], 1, 1)).astype(bf16)
 
@@ -504,7 +505,7 @@
         hi_ref[...] = grad
 
 
-def ffn_back_call(s, dys, wd, d_parts, fg, fu, wg, wu):
+def ffn_back_call(s, dys, wd, d_parts, wg, wu, parts, fg, fu):
     b, d = dys[0].shape
     h = wg.shape[1]
     block = lambda wid: pl.BlockSpec((b, wid), lambda j, s: (j, 0))
@@ -513,30 +514,71 @@
         grid_spec=pltpu.PrefetchScalarGridSpec(
             num_scalar_prefetch=1,
             grid=(4,),
-            in_specs=[ANY] * 7 + [block(h), block(h), ANY, ANY],
+            in_specs=[ANY] * 11 + [block(h), block(h)],
             out_specs=[
                 block(h),
                 block(h),
                 pl.BlockSpec((b, d), lambda j, s: (jnp.minimum(j, 1), 0)),
                 pl.BlockSpec((b, d), lambda j, s: (jnp.maximum(j - 2, 0), 0)),
-                fixed(h, d),
             ],
             scratch_shapes=[
-                pltpu.VMEM((4, b, d), bf16),
+                pltpu.VMEM((h, d), bf16),
                 pltpu.VMEM((d, h), bf16),
                 pltpu.VMEM((d, h), bf16),
+                pltpu.VMEM((4, b, d), bf16),
                 pltpu.SemaphoreType.DMA((4,)),
                 pltpu.SemaphoreType.DMA((9,)),
-                pltpu.SemaphoreType.DMA((2,)),
+                pltpu.SemaphoreType.DMA((9,)),
+                pltpu.SemaphoreType.DMA((9,)),
             ],
         ),
-        out_shape=[jax.ShapeDtypeStruct((4 * b, h), bf16)] * 2
-        + [jax.ShapeDtypeStruct((2 * b, d), bf16)] * 2
-        + [jax.ShapeDtypeStruct((h, d), bf16)],
-        compiler_params=params(34),
-        cost_estimate=pl.CostEstimate(flops=24 * b * d * h, bytes_accessed=22 * VMEM_MB, transcendentals=0),
+        out_shape=[jax.ShapeDtypeStruct((4 * b, h), bf16)] * 2 + [jax.ShapeDtypeStruct((2 * b, d), bf16)] * 2,
+        compiler_params=params(19),
+        cost_estimate=cost(1 << 24),
         name="ffn_back",
-    )(s, *dys, wd, *d_parts, fg, fu, wg, wu)
+    )(s, *dys, wd, *d_parts, wg, wu, *parts, fg, fu)
+
+
+def ffn_out_kernel(s_ref, wd_own, d0, d1, hid_ref, lo_ref, hi_ref, wd, dsem):
+    j = pl.program_id(0)
+    down_w = Weight(s_ref, (wd_own,), (d0, d1), wd, dsem)
+
+    @pl.when(j == 0)
+    def _():
+        down_w.start()
+        down_w.wait()
+
+    part = jnp.dot(hid_ref[...], wd[...], preferred_element_type=f32).astype(bf16)
+
+    @pl.when(j < 2)
+    def _():
+        lo_ref[...] = part
+
+    @pl.when(j >= 2)
+    def _():
+        hi_ref[...] = part
+
+
+def ffn_out_call(s, wd, d_parts, hidden):
+    n, h = hidden.shape
+    b, d = n // 4, wd.shape[1]
+    return pl.pallas_call(
+        ffn_out_kernel,
+        grid_spec=pltpu.PrefetchScalarGridSpec(
+            num_scalar_prefetch=1,
+            grid=(4,),
+            in_specs=[ANY] * 3 + [pl.BlockSpec((b, h), lambda j, s: (j, 0))],
+            out_specs=[
+                pl.BlockSpec((b, d), lambda j, s: (jnp.minimum(j, 1), 0)),
+                pl.BlockSpec((b, d), lambda j, s: (jnp.maximum(j - 2, 0), 0)),
+            ],
+            scratch_shapes=[pltpu.VMEM((h, d), bf16), pltpu.SemaphoreType.DMA((9,))],
+        ),
+        out_shape=[jax.ShapeDtypeStruct((2 * b, d), bf16)] * 2,
+        compiler_params=params(9),
+        cost_estimate=cost(1 << 24),
+        name="ffn_out",
+    )(s, wd, *d_parts, hidden)
 
 
 def grad_rows_kernel(by_cols, s_ref, left_ref, right_ref, sent_a, keep_a, sent_b, keep_b):
@@ -586,8 +628,8 @@
             out_specs=[pl.BlockSpec((1,) + half, m) for m in maps],
         ),
         out_shape=[jax.ShapeDtypeStruct((2,) + half, bf16)] * 4,
-        compiler_params=params(24),
-        cost_estimate=pl.CostEstimate(flops=2 * n * rows * cols, bytes_accessed=4 * n * (rows + cols), transcendentals=0),
+        compiler_params=params(11),
+        cost_estimate=cost(1 << 24),
         name=name,
     )(s, left, right)
 
@@ -636,10 +678,30 @@
             out_specs=[first, first, second, second],
         ),
         out_shape=[jax.ShapeDtypeStruct((2, rows // 4, cols // 2), bf16)] * 4,
-        compiler_params=params(24),
-        cost_estimate=pl.CostEstimate(flops=2 * n * rows * cols, bytes_accessed=4 * n * (rows + cols), transcendentals=0),
+        compiler_params=params(11),
+        cost_estimate=cost(1 << 24),
         name=name,
     )(s, left, *rights)
+
+
+def widen_kernel(side, in_ref, out_ref):
+    first, second = in_ref[0, 0].astype(f32), in_ref[0, 1].astype(f32)
+    out_ref[...] = jnp.concatenate([first, second], 1 if side else 0)
+
+
+def widen_call(whole, side, name):
+    _, _, rows, cols = whole.shape
+    block = (rows, 2 * cols) if side else (2 * rows, cols)
+    return pl.pallas_call(
+        functools.partial(widen_kernel, side),
+        grid=(8,),
+        in_specs=[pl.BlockSpec((1, 2, rows, cols), lambda j: (j, 0, 0, 0))],
+        out_specs=pl.BlockSpec(block, lambda j: (j, 0)),
+        out_shape=jax.ShapeDtypeStruct((8 * block[0], block[1]), f32),
+        compiler_params=params(8),
+        cost_estimate=cost(1 << 20),
+        name=name,
+    )(whole)
 
 
 def permute(x, places, move):
@@ -683,21 +745,17 @@
     return [x, over, near, far]
 
 
-def scatter_row(low, high, n, *events):
-    b = low.shape[0] // 2
-    got = permute(high, n, flip_core)
-    over = permute(low[b:] + got[b:], n, flip_z)
-    return low[:b] + got[:b] + (after(over, *events) if events else over)
-
-
 def hop(weights, n, c, e):
     rows = weights[0].shape[0] // 8
     mine = [lax.dynamic_slice_in_dim(w, (2 * e + c) * rows, rows, 0) for w in weights]
     return permute(jnp.concatenate(mine, 1) if len(mine) > 1 else mine[0], n, flip_far)
 
 
-def spread(piece, n):
-    mine = jnp.concatenate([piece] + [permute(piece, n, lambda d, t, j=j: (d ^ (2 * j), t)) for j in (1, 2, 3)])
+def spread(piece, n, *events):
+    got = [permute(piece, n, lambda d, t, j=j: (d ^ (2 * j), t)) for j in (1, 2, 3)]
+    if events:
+        got = after(got, *events)
+    mine = jnp.concatenate([piece] + got)
     return mine, permute(mine, n, flip_core)
 
 
@@ -741,12 +799,11 @@
     return lax.all_gather(mine, "dp", axis_index_groups=neighbours(n))
 
 
-def whole_out(w, n, c, e):
+def out_slices(w, n, c, e):
     rows = w.shape[0] // 8
     mine = lax.dynamic_slice_in_dim(w, (2 * e + c) * rows, rows, 0)
     two = jnp.stack([mine, permute(mine, n, flip_z)])
-    four = jnp.concatenate([two, permute(two, n, flip_far)])
-    return lax.all_gather(four, "dp", axis_index_groups=neighbours(n))
+    return jnp.concatenate([two, permute(two, n, flip_far)])
 
 
 def sum_all(vec, n):
@@ -757,6 +814,22 @@
     for bit in (1, 2):
         vec = vec + permute(vec, n, lambda d, t, bit=bit: (d, t ^ bit))
     return vec
+
+
+def join_attention(qkv, out):
+    r, k = qkv.shape[1] // 2, qkv.shape[2]
+    s = out.shape[1] // 2
+    parts = []
+    for half in range(2):
+        some = out[:, half * s : (half + 1) * s]
+        parts += [qkv[:, half * r : (half + 1) * r], some[:, :, :k], some[:, :, k:]]
+    return jnp.concatenate(parts, 1)
+
+
+def widen_out(got):
+    s = got.shape[2] // 2
+    sides = [got[:, half, at * s : (at + 1) * s].reshape(8 * s, -1) for half in range(2) for at in range(2)]
+    return jnp.concatenate(sides, 1).astype(f32)
 
 
 def local(
@@ -793,11 +866,12 @@
     marks = jnp.concatenate([doc_lengths, pad_mask], 1)
     marks = jnp.where(home, marks, permute(marks, n, flip_core))
     lengths_row, pad_row = marks[0, : doc_lengths.shape[1]], marks[0, doc_lengths.shape[1] :]
+    out_eighth = out_slices(w_out, n, c, e)
+    out_all = lax.all_gather(out_eighth, "dp", axis_index_groups=neighbours(n))
     qkv_hop = hop((w_query, w_key, w_value), n, c, e)
     x_blocks = gather_row(x_own, n)
-    qkv_parts = spread(qkv_hop, n)
+    qkv_parts = spread(qkv_hop, n, x_blocks[1])
     gate_up_hop = hop((after(w_gate, x_blocks[2]), w_up), n, c, e)
-    out_all = whole_out(after(w_out, x_blocks[2]), n, c, e)
 
     positions = jnp.arange(seq_len, dtype=jnp.int32)
     doc_starts, cos_half, sin_half = doc_tables(lengths_row, positions, HD)
@@ -813,31 +887,36 @@
     kgain_pair = jnp.concatenate([key_gain] * 2)[None]
 
     rows_one, pre, qk, values, w_qkv = qkv_call(
-        s, x_blocks, (w_query, w_key, w_value), qkv_parts, norm1_gain[None], gains, cos, sin
+        s, x_blocks, (w_query, w_key, w_value), qkv_parts, norm1_gain[None], after(gains, out_eighth), cos, sin
     )
     attended, attended_f, lse = attend_call(s, qk, values, start_col, live_row)
     att_pieces = gather_row(attended, n)
-    gate_up_parts = spread(after(gate_up_hop, attended), n)
+    gate_up_parts = spread(after(gate_up_hop, attended), n, att_pieces[1])
     down_hop = hop((after(w_down, attended),), n, c, e)
     dy_own = permute(after(cotangent, attended), n, settle)
-    down_parts = spread(after(down_hop, att_pieces[1]), n)
-    dy_blocks = gather_row(after(dy_own, att_pieces[1]), n)
-    rows_two, hidden, by_gate, by_up, residual, wg, wu, w_out_own = ffn_call(
-        s, x_blocks, att_pieces, out_all, w_gate, w_up, gate_up_parts, after(norm2_gain[None], dy_own)
+    down_hop = after(down_hop, att_pieces[3])
+    dy_own = after(dy_own, att_pieces[3])
+    dy_blocks = gather_row(dy_own, n)
+    down_parts = spread(down_hop, n, dy_blocks[1])
+    rows_two, hidden, by_gate, by_up, residual, w_out_own = ffn_call(
+        s, x_blocks, att_pieces, out_all, w_gate, w_up, gate_up_parts, after(norm2_gain[None], dy_own, down_hop)
     )
 
     down = grad_cols_call(s, hidden, dy_blocks, "grad_down")
-    gate_grad, up_grad, low2, high2, wd = ffn_back_call(
-        s, dy_blocks, w_down, down_parts, after(by_gate, *down), by_up, wg, wu
+    gate_grad, up_grad, low2, high2 = ffn_back_call(
+        s, dy_blocks, w_down, down_parts, w_gate, w_up, gate_up_parts, after(by_gate, *down), by_up
     )
+    high_got = permute(high2, n, flip_core)
     down_got = first_sums(down, n)
-    down = first_add(down, after(down_got, low2))
+    low_half = low2 + high_got
+    low_over = permute(low_half[b:], n, flip_z)
+    down = first_add(down, after(down_got, low_half))
     down_got = second_sums(down, n)
     gate = grad_rows_call(s, rows_two, after(gate_grad, *down), False, "grad_gate")
     gate_got = first_sums(gate, n)
     up = grad_rows_call(s, rows_two, after(up_grad, *gate), False, "grad_up")
     up_got = first_sums(up, n)
-    grad_n2 = scatter_row(low2, high2, n, *up).astype(f32)
+    grad_n2 = (low_half[:b] + after(low_over, *up)).astype(f32)
     inv = lax.rsqrt(jnp.mean(residual * residual, axis=-1, keepdims=True) + epsilon)
     scaled = norm2_gain * grad_n2
     grad_residual = (
@@ -851,38 +930,38 @@
 
     down = second_add(down, after(down_got, gb_own), n)
     down_kept, down_got = owner_cross(down, n, c)
-    ffn_part = jnp.dot(after(hidden, down_kept), wd, preferred_element_type=f32).astype(bf16)
-    gate = first_add(gate, after(gate_got, ffn_part))
+    ffn_low, ffn_high = ffn_out_call(s, w_down, down_parts, after(hidden, down))
+    ffn_got = permute(ffn_high, n, flip_core)
+    gate = first_add(gate, after(gate_got, ffn_low))
     gate_got = second_sums(gate, n)
     up = first_add(up, after(up_got, gb_blocks[1], *gate))
     up_got = second_sums(up, n)
-    down_mine = down_kept + after(down_got, gb_blocks[3], *up)
+    ffn_half = ffn_low + after(ffn_got, *up)
+    ffn_over = permute(ffn_half[b:], n, flip_z)
+    down_mine = down_kept + after(down_got, gb_blocks[3], ffn_half)
     down_all = whole_grad(down_mine, n)
     gate = second_add(gate, after(gate_got, down_mine), n)
     gate_kept, gate_got = owner_cross(gate, n, c)
-    ffn_got = permute(ffn_part[2 * b :], n, flip_core)
-    ffn_half = ffn_part[: 2 * b] + after(ffn_got, gb_blocks[3])
-    ffn_over = permute(ffn_half[b:], n, flip_z)
 
     low, gain_terms, low1, high1 = attend_back_call(
         s, qk, after(values, gate_kept, ffn_half), pre, qgain_pair, kgain_pair, cos, sin, start_row, live_col, attended_f,
         lse, w_out_own, w_qkv, gb_blocks,
     )
     high_got = permute(high1, n, flip_core)
-    gate_mine = gate_kept + after(gate_got, low)
+    gate_mine = gate_kept + after(gate_got, high_got)
     gate_all = whole_grad(gate_mine, n)
     low_half = low1 + after(high_got, gate_mine)
     low_over = permute(low_half[b:], n, flip_z)
     up = second_add(up, after(up_got, low_half), n)
     up_kept, up_got = owner_cross(up, n, c)
-    block_output = residual + (ffn_half[:b] + after(ffn_over, low_half, up)).astype(f32)
+    qkv = grad_rows_call(s, rows_one, after(low, up_kept), True, "grad_qkv")
+    out = grad_cols_call(s, after(attended, *qkv), gb_blocks, "grad_out")
+    att = [join_attention(a, o) for a, o in zip(qkv, out)]
+    att_got = first_sums(att, n)
+    block_output = residual + (ffn_half[:b] + after(ffn_over, *att)).astype(f32)
     settled_output = permute(block_output.astype(bf16), n, settle)
-    qkv = grad_rows_call(s, rows_one, after(low, up_kept, block_output), True, "grad_qkv")
-    qkv_got = first_sums(qkv, n)
-    out = grad_cols_call(s, after(attended, *qkv), gb_blocks, "grad_out")
-    out_got = first_sums(out, n)
-
-    grad_n1 = (low_half[:b] + after(low_over, *out)).astype(f32)
+
+    grad_n1 = (low_half[:b] + after(low_over, block_output)).astype(f32)
     x_f = x_own.astype(f32)
     inv = lax.rsqrt(jnp.mean(x_f * x_f, axis=-1, keepdims=True) + epsilon)
     scaled = norm1_gain * grad_n1
@@ -895,34 +974,25 @@
     settled_grad = permute(input_grad.astype(bf16), n, settle)
     up_mine = up_kept + after(up_got, input_grad)
     up_all = whole_grad(up_mine, n)
-    qkv = first_add(qkv, after(qkv_got, up_mine))
-    qkv_got = second_sums(qkv, n)
-    out = first_add(out, after(out_got, *qkv))
-    out_got = second_sums(out, n)
+    att = first_add(att, after(att_got, up_mine))
+    att_got = second_sums(att, n)
     head_terms = gain_terms[:, :HD] + gain_terms[:, HD:]
     vec = jnp.concatenate([grad_norm1, grad_norm2, head_terms[0] + head_terms[1], head_terms[2]])
-    vec = sum_all(after(vec, *out)[None], n)[0]
-    qkv = second_add(qkv, after(qkv_got, vec), n)
-    out = second_add(out, after(out_got, vec), n)
-    qkv_kept, qkv_got = owner_cross(qkv, n, c)
-    out_kept, out_got = owner_cross(out, n, c)
-    qkv_all = whole_grad(qkv_kept + qkv_got, n)
-    out_all = whole_grad(out_kept + out_got, n)
-    block_output = jnp.where(home, block_output, after(settled_output, qkv_kept, out_kept).astype(f32))
-    input_grad = jnp.where(home, input_grad, after(settled_grad, qkv_kept, out_kept).astype(f32))
-
-    def rows(whole):
-        return whole.astype(f32).reshape(width, -1)
-
-    def side_by_side(whole):
-        return whole.astype(f32).transpose(0, 2, 1, 3).reshape(-1, width)
-
-    grad_down = side_by_side(down_all)
-    grad_gate = rows(gate_all)
-    grad_up = rows(up_all)
-    grad_out = side_by_side(out_all)
-    grad_query = rows(qkv_all[:, 0])
-    grad_kv = rows(qkv_all[:, 1])
+    vec = sum_all(after(vec, *att)[None], n)[0]
+    att = second_add(att, after(att_got, vec), n)
+    att_kept, att_got = owner_cross(att, n, c)
+    grad_down = widen_call(after(down_all, att_kept), True, "widen_down")
+    grad_gate = widen_call(after(gate_all, grad_down), False, "widen_gate")
+    att_mine = att_kept + after(att_got, grad_down)
+    att_all = whole_grad(att_mine, n)
+    block_output = jnp.where(home, block_output, after(settled_output, grad_gate).astype(f32))
+    input_grad = jnp.where(home, input_grad, after(settled_grad, grad_gate).astype(f32))
+    grad_up = widen_call(after(up_all, grad_gate), False, "widen_up")
+    att_all = after(att_all, grad_up)
+    eighth = wq // 2
+    grad_query = att_all[:, 0, :eighth].astype(f32).reshape(width, wq)
+    grad_kv = att_all[:, 1, :eighth].astype(f32).reshape(width, wq)
+    grad_out = widen_out(att_all[:, :, eighth:])
     return (
         block_output,
         input_grad,

time: 524 us -> 507 us (0.968)
  starting transfers between devices: 83.6 us -> 65 us
  other arithmetic: 57.8 us -> 41.6 us
  local copies, waits for them, and re-layouts: 58.5 us -> 74.4 us
  blocking collectives: 10.3 us -> 0 us
  Pallas kernels: 85.4 us -> 94.6 us
  waiting for transfers between devices: 200 us -> 207 us
    ppermute x75 -> x69, waiting for transfers between devices: 178 us -> 207 us  [permute(): return lax.ppermute(x, AX, pairs)]
    all_gather x4, waiting for transfers between devices: 21.1 us -> 0.03 us  [whole_grad(): return lax.all_gather(mine, 'dp', axis_index_groups=neighbours(n))]
    unnamed x197 -> x221, local copies, waits for them, and re-layouts: 39.4 us -> 59.3 us
    ppermute x75 -> x69, starting transfers between devices: 83.2 us -> 64.8 us  [permute(): return lax.ppermute(x, AX, pairs)]
    pallas_call x0 -> x4, Pallas kernels: none -> 15.3 us  [the longest x3 10.8 us: widen_call(): pl.pallas_call(functools.partial(widen_kernel, side), grid=(8,), in_specs...]
    reshape x4 -> x0, other arithmetic: 10.8 us -> none  [the longest x2 8.37 us: rows(): return whole.astype(f32).reshape(width, -1)]
    all_gather x1 -> x0, blocking collectives: 10.3 us -> none  [whole_grad(): return lax.all_gather(mine, 'dp', axis_index_groups=neighbours(n))]
  transfers between devices with their start and end apart: 80 -> 74, of which waited for: 35 -> 31; matrix products, arithmetic and copies ran while one was open for 16% -> 12% of each run, Pallas kernels for 10% -> 16%
where the time goes in v1:
time: 507 us; the launch traced here: 499 us
  waiting for transfers between devices  207 us (41%)
  Pallas kernels  94.6 us (19%)
  local copies, waits for them, and re-layouts  74.4 us (15%)
  starting transfers between devices  65 us (13%)
  other arithmetic  41.6 us (8%)
  between operations  15.6 us (3%)
    ppermute x69, waiting for transfers between devices, permute(): return lax.ppermute(x, AX, pairs)  207 us
    ppermute x69, starting transfers between devices, permute(): return lax.ppermute(x, AX, pairs)  64.8 us
    unnamed x221, local copies, waits for them, and re-layouts  59.3 us
    pallas_call x1, Pallas kernels, attend_back_call(): pl.pallas_call(attend_back_kernel, grid_spec=pltpu.PrefetchScalarGridSpec...  19 us
    pallas_call x1, Pallas kernels, ffn_back_call(): pl.pallas_call(ffn_back_kernel, grid_spec=pltpu.PrefetchScalarGridSpec(nu...  12.7 us
    pallas_call x3, Pallas kernels, grad_rows_call(): pl.pallas_call(functools.partial(grad_rows_kernel, by_cols), grid_spec=pl...  12.4 us
    pallas_call x1, Pallas kernels, ffn_call(): pl.pallas_call(ffn_kernel, grid_spec=pltpu.PrefetchScalarGridSpec(num_sca...  11.8 us
    pallas_call x3, Pallas kernels, widen_call(): pl.pallas_call(functools.partial(widen_kernel, side), grid=(8,), in_specs...  10.8 us
  transfers between devices with their start and end apart: 74, of which 31 were waited for; matrix products, arithmetic and copies ran while one was open for 12% of the time, Pallas kernels for 16%

profile of v1, /device:TPU:0, one launch (start us, length us, event | category | flops | bytes accessed | tf_op | source)
XLA Modules:
  0.0 498.5 jit_solution(2467976024523672781)
XLA Ops:
  7.2 1.8 collective-permute-start
  10.7 4.3 collective-permute-start.4
  18.1 1.6 collective-permute-start.1
  19.8 12.3 %collective-permute-done.4 = bf16[128,512]{1,0:T(8,128)(2,1)S(1)} collective-permute-done((bf16[128,512]{1,0:T(8,128)(2,1)S(1)}, bf16[128,512]{1,0:T(8,128)(2,1)S(1)}, u32[]{:S(2)}, u32[]{:S(2)}) %collective-permute-start.4) | collective-permute-done | bytes 131104 | tf_op jit(solution)/shard_map/ppermute | solution.py:714
  35.5 1.9 fusion.24
  38.1 3.1 collective-permute-done.6
  45.4 2.1 collective-permute-start.15
  49.6 30.9 %collective-permute-done.10 = bf16[2,32,1024]{2,1,0:T(8,128)(2,1)S(1)} collective-permute-done((bf16[2,32,1024]{2,1,0:T(8,128)(2,1)S(1)}, bf16[2,32,1024]{2,1,0:T(8,128)(2,1)S(1)}, u32[]{:S(2)}, u32[]{:S(2)}) %collective-permute-start.10) | collective-permute-done | bytes 131104 | tf_op jit(solution)/shard_map/ppermute | solution.py:714
  86.0 7.4 %qkv.1 = (bf16[1024,1024]{1,0:T(8,128)(2,1)S(1)}, f32[1024,384]{1,0:T(8,128)S(1)}, bf16[1024,384]{1,0:T(8,128)(2,1)S(1)}, bf16[1024,128]{1,0:T(8,128)(2,1)S(1)}, bf16[1024,512]{1,0:T(8,128)(2,1)S(1)}) custom-call(s32[3]{0:T(128)S(1)} %pad_add_fusion.1.s_ref, bf16[256,1024]{1,0:T(8,128)(2,1)S(1)} %collective-permute-done.x0, ...), custom_call_target="tpu_custom_call" | custom-call | flops 16777216 | bytes 65536 | tf_op jit(solution)/shard_map/qkv/pallas_call | solution.py:147
  97.2 5.4 %attend.1 = (bf16[1024,256]{1,0:T(8,128)(2,1)S(1)}, f32[1024,256]{1,0:T(8,128)S(1)}, f32[2,4,1,512]{3,2,1,0:T(1,128)S(1)}) custom-call(s32[3]{0:T(128)S(1)} %pad_add_fusion.1.s_ref, bf16[1024,384]{1,0:T(8,128)(2,1)S(1)} %get-tuple-element.117.q_ref.k_ref, bf16[1024,384]{1,0:T(8,128)(2,1)S(1)} %get-tuple-element.117.q_ref.k_ref, ...), custom_call_target="tpu_custom_call" | custom-call | flops 16777216 | bytes 65536 | tf_op jit(solution)/shard_map/attend/pallas_call | solution.py:233
  107.4 1.8 collective-permute-start.20
  109.3 1.9 constant_dynamic-update-slice_fusion.7
  111.2 15.1 %collective-permute-done.12.a1 = bf16[1024,256]{1,0:T(8,128)(2,1)S(1)} collective-permute-done((bf16[1024,256]{1,0:T(8,128)(2,1)S(1)}, bf16[1024,256]{1,0:T(8,128)(2,1)S(1)}, u32[]{:S(2)}, u32[]{:S(2)}) %collective-permute-start.12) | collective-permute-done | bytes 524320 | tf_op jit(solution)/shard_map/ppermute | solution.py:714
  126.3 8.3 %collective-permute-done.17 = bf16[128,2304]{1,0:T(8,128)(2,1)} collective-permute-done((bf16[128,2304]{1,0:T(8,128)(2,1)}, bf16[128,2304]{1,0:T(8,128)(2,1)}, u32[]{:S(2)}, u32[]{:S(2)}) %collective-permute-start.17) | collective-permute-done | bytes 589856 | tf_op jit(solution)/shard_map/ppermute | solution.py:714
  135.7 1.9 constant_dynamic-update-slice_fusion.6
  137.6 1.9 constant_dynamic-update-slice_fusion.5
  139.5 2.0 constant_dynamic-update-slice_fusion.4.p0
  142.6 4.1 collective-permute-start.25
  146.7 12.6 %collective-permute-done.21 = bf16[144,1024]{1,0:T(8,128)(2,1)S(1)} collective-permute-done((bf16[144,1024]{1,0:T(8,128)(2,1)S(1)}, bf16[144,1024]{1,0:T(8,128)(2,1)S(1)}, u32[]{:S(2)}, u32[]{:S(2)}) %collective-permute-start.21) | collective-permute-done | bytes 294944 | tf_op jit(solution)/shard_map/ppermute | solution.py:714
  163.5 5.7 %collective-permute-done.22 = bf16[144,1024]{1,0:T(8,128)(2,1)S(1)} collective-permute-done((bf16[144,1024]{1,0:T(8,128)(2,1)S(1)}, bf16[144,1024]{1,0:T(8,128)(2,1)S(1)}, u32[]{:S(2)}, u32[]{:S(2)}) %collective-permute-start.22) | collective-permute-done | bytes 294944 | tf_op jit(solution)/shard_map/ppermute | solution.py:714
  169.2 4.3 collective-permute-done.23
  178.3 3.7 collective-permute-done.13.a2
  182.8 1.7 copy-done.4
  184.5 1.7 copy-done.6
  186.2 1.6 copy-done.37
  193.0 11.8 %ffn.1 = (bf16[1024,1024]{1,0:T(8,128)(2,1)S(1)}, bf16[1024,1152]{1,0:T(8,128)(2,1)S(1)}, bf16[1024,1152]{1,0:T(8,128)(2,1)S(1)}, bf16[1024,1152]{1,0:T(8,128)(2...) custom-call(s32[3]{0:T(128)S(1)} %pad_add_fusion.1.s_ref, ...), custom_call_target="tpu_custom_call" | custom-call | flops 16777216 | bytes 65536 | tf_op jit(solution)/shard_map/ffn/pallas_call | solution.py:438
  204.8 7.7 %grad_down.1 = (bf16[2,288,512]{2,1,0:T(8,128)(2,1)}, bf16[2,288,512]{2,1,0:T(8,128)(2,1)S(1)}, bf16[2,288,512]{2,1,0:T(8,128)(2,1)}, bf16[2,288,512]{2,1,0:T(8,128)(2,1)S(1)}) custom-call(s32[3]{0:T(128)S(1)} %pad_add_fusion.1.s_ref, bf16[1024,1152]{1,0:T(8,128)(2,1)S(1)} %get-tuple-element.162.left_ref.hid_ref, ...), custom_call_target="tpu_custom_call" | custom-call | flops 16777216 | bytes 65536 | tf_op jit(solution)/shard_map/grad_down/pallas_call | solution.py:672
  215.7 12.7 %ffn_back.1 = (bf16[1024,1152]{1,0:T(8,128)(2,1)S(1)}, bf16[1024,1152]{1,0:T(8,128)(2,1)S(1)}, bf16[512,1024]{1,0:T(8,128)(2,1)S(1)}, bf16[512,1024]{1,0:T(8,128)(2,1)}) custom-call(s32[3]{0:T(128)S(1)} %pad_add_fusion.1.s_ref, bf16[256,1024]{1,0:T(8,128)(2,1)S(1)} %collective-permute-done.20.r0.y0, bf16[256,1024]{1,0:T(8,128)(2,1)} %collective-permute-done.25.r1.y1, ...), custom_call_target="tpu_custom_call" | custom-call | flops 16777216 | bytes 65536 | tf_op jit(solution)/shard_map/ffn_back/pallas_call | solution.py:512
  232.2 3.3 collective-permute-start.31
  237.8 1.7 copy-done.3
  239.5 1.7 copy-done.9
  241.2 4.5 ffn_out.1
  246.7 1.7 add.235
  248.6 2.4 collective-permute-done.29
  256.0 4.7 grad_gate.1
  260.7 4.7 grad_up.1
  271.5 20.1 %collective-permute-done.39 = bf16[2,128,1152]{2,1,0:T(8,128)(2,1)S(1)} collective-permute-done((bf16[2,128,1152]{2,1,0:T(8,128)(2,1)S(1)}, bf16[2,128,1152]{2,1,0:T(8,128)(2,1)S(1)}, u32[]{:S(2)}, u32[]{:S(2)}) %collective-permute-start.39) | collective-permute-done | bytes 589856 | tf_op jit(solution)/shard_map/ppermute | solution.py:714
  297.6 8.0 %collective-permute-done.38.b1.r1 = bf16[256,1024]{1,0:T(8,128)(2,1)S(1)} collective-permute-done((bf16[256,1024]{1,0:T(8,128)(2,1)S(1)}, bf16[256,1024]{1,0:T(8,128)(2,1)S(1)}, u32[]{:S(2)}, u32[]{:S(2)}) %collective-permute-start.38) | collective-permute-done | bytes 524320 | tf_op jit(solution)/shard_map/ppermute | solution.py:714
  308.9 3.5 collective-permute-done.45
  322.8 19.0 %attend_back.1 = (bf16[1024,512]{1,0:T(8,128)(2,1)S(1)}, f32[8,128]{1,0:T(8,128)S(1)}, bf16[512,1024]{1,0:T(8,128)(2,1)S(1)}, bf16[512,1024]{1,0:T(8,128)(2,1)S(1)}) custom-call(s32[3]{0:T(128)S(1)} %pad_add_fusion.1.s_ref, bf16[1024,384]{1,0:T(8,128)(2,1)S(1)} %get-tuple-element.117.q_ref.k_ref, bf16[1024,384]{1,0:T(8,128)(2,1)S(1)} %get-tuple-element.117.q_ref.k_ref, ...), custom_call_target="tpu_custom_call" | custom-call | flops 16777216 | bytes 65536 | tf_op jit(solution)/shard_map/attend_back/pallas_call | solution.py:354
  346.3 13.0 %collective-permute-done.52 = bf16[2,64,1152]{2,1,0:T(8,128)(2,1)S(1)} collective-permute-done((bf16[2,64,1152]{2,1,0:T(8,128)(2,1)S(1)}, bf16[2,64,1152]{2,1,0:T(8,128)(2,1)S(1)}, u32[]{:S(2)}, u32[]{:S(2)}) %collective-permute-start.52) | collective-permute-done | bytes 294944 | tf_op jit(solution)/shard_map/ppermute | solution.py:714
  361.1 1.9 add.270
  368.7 2.1 collective-permute-start.58
  374.8 3.1 grad_qkv.1
  380.1 2.9 grad_out.1
  385.0 2.4 fusion.29
  387.5 12.4 %collective-permute-done.58 = bf16[256,1024]{1,0:T(8,128)(2,1)S(1)} collective-permute-done((bf16[256,1024]{1,0:T(8,128)(2,1)}, bf16[256,1024]{1,0:T(8,128)(2,1)S(1)}, u32[]{:S(2)}, u32[]{:S(2)}) %collective-permute-start.58) | collective-permute-done | bytes 524320 | tf_op jit(solution)/shard_map/ppermute | solution.py:714
  404.8 11.8 %collective-permute-done.55 = bf16[2,384,256]{2,1,0:T(8,128)(2,1)S(1)} collective-permute-done((bf16[2,384,256]{2,1,0:T(8,128)(2,1)}, bf16[2,384,256]{2,1,0:T(8,128)(2,1)S(1)}, u32[]{:S(2)}, u32[]{:S(2)}) %collective-permute-start.55) | collective-permute-done | bytes 393248 | tf_op jit(solution)/shard_map/ppermute | solution.py:714
  421.0 2.3 collective-permute-done.59
  423.3 5.1 %collective-permute-done.60 = bf16[384,256]{1,0:T(8,128)(2,1)S(1)} collective-permute-done((bf16[384,256]{1,0:T(8,128)(2,1)S(1)}, bf16[384,256]{1,0:T(8,128)(2,1)S(1)}, u32[]{:S(2)}, u32[]{:S(2)}) %collective-permute-start.60) | collective-permute-done | bytes 196640 | tf_op jit(solution)/shard_map/ppermute | solution.py:714
  430.3 1.7 copy-done.20
  432.0 3.6 widen_down.1
  435.6 4.2 collective-permute-done.68
  444.5 2.9 collective-permute-done.64
  447.5 3.7 collective-permute-done.65
  451.3 3.6 collective-permute-done.66
  455.0 4.8 collective-permute-start.67
  459.7 9.9 %collective-permute-done.67 = f32[1,2176]{1,0:T(1,128)S(1)} collective-permute-done((f32[1,2176]{1,0:T(1,128)S(1)}, f32[1,2176]{1,0:T(1,128)S(1)}, u32[]{:S(2)}, u32[]{:S(2)}) %collective-permute-start.67) | collective-permute-done | bytes 8736 | tf_op jit(solution)/shard_map/ppermute | solution.py:714
  470.9 1.7 copy-done.21
  472.5 3.6 widen_gate.1
  476.2 2.2 convert_select_fusion.1
  478.4 2.1 convert_select_fusion
  480.5 1.7 copy-done.22
  482.2 3.6 widen_up.1
  (427 shorter events, 130.0 us)
Async XLA Ops:
  7.2 175.6 %all-gather.11.cloned.1.call-start = ((), (), s32[]{:S(2)}) async-start(), calls=%async_computation | async-start | bytes 2359296 | tf_op jit(solution)/shard_map/all_gather | solution.py:870
  7.2 10.9 %collective-permute-start = (bf16[256,1024]{1,0:T(8,128)(2,1)}, bf16[256,1024]{1,0:T(8,128)(2,1)S(1)}, u32[]{:S(2)}, u32[]{:S(2)}) collective-permute-start(bf16[256,1024]{1,0:T(8,128)(2,1)} %param.15), channel_id=1, source_target_pairs={{0,0},{1,1},{2,4},{3,5},{4,2},{5,3},{6,6},{7,7},{8,8},{9,9},{10,12... | collective-permute-start | bytes 1572872 | tf_op jit(solution)/shard_map/ppermute | solution.py:714
  10.7 21.3 %collective-permute-start.4 = (bf16[128,512]{1,0:T(8,128)(2,1)S(1)}, bf16[128,512]{1,0:T(8,128)(2,1)S(1)}, u32[]{:S(2)}, u32[]{:S(2)}) collective-permute-start(bf16[128,512]{1,0:T(8,128)(2,1)S(1)} %pad_maximum_fusion.8), channel_id=1, source_target_pairs={{0,2},{1,3},{2,0},{3,1},{4,6},{5,7},{6,4},{7,5},{8,10},{9,11},{10,... | collective-permute-start | bytes 393224 | tf_op jit(solution)/shard_map/ppermute | solution.py:714
  18.1 23.1 %collective-permute-start.1 = (bf16[256,1024]{1,0:T(8,128)(2,1)S(1)}, bf16[256,1024]{1,0:T(8,128)(2,1)S(1)}, u32[]{:S(2)}, u32[]{:S(2)}) collective-permute-start(bf16[256,1024]{1,0:T(8,128)(2,1)S(1)} %collective-permute-done.x0), channel_id=1, source_target_pairs={{0,1},{1,0},{2,3},{3,2},{4,5},{5,4},{6,7},{7,6},{8,9},{9,8},{10,11... | collective-permute-start | bytes 1572872 | tf_op jit(solution)/shard_map/ppermute | solution.py:714
  32.0 6.1 %collective-permute-start.5 = (bf16[128,512]{1,0:T(8,128)(2,1)S(1)}, bf16[128,512]{1,0:T(8,128)(2,1)S(1)}, u32[]{:S(2)}, u32[]{:S(2)}) collective-permute-start(bf16[128,512]{1,0:T(8,128)(2,1)S(1)} %collective-permute-done.4), channel_id=1, source_target_pairs={{0,8},{1,9},{2,10},{3,11},{4,12},{5,13},{6,14},{7,15},{8,0},{9,1},... | collective-permute-start | bytes 393224 | tf_op jit(solution)/shard_map/ppermute | solution.py:714
  33.5 7.7 %collective-permute-start.6 = (bf16[128,512]{1,0:T(8,128)(2,1)S(1)}, bf16[128,512]{1,0:T(8,128)(2,1)S(1)}, u32[]{:S(2)}, u32[]{:S(2)}) collective-permute-start(bf16[128,512]{1,0:T(8,128)(2,1)S(1)} %collective-permute-done.4), channel_id=1, source_target_pairs={{0,16},{1,17},{2,18},{3,19},{4,20},{5,21},{6,22},{7,23},{8,24},{9,... | collective-permute-start | bytes 393224 | tf_op jit(solution)/shard_map/ppermute | solution.py:714
  35.0 6.2 %collective-permute-start.7 = (bf16[128,512]{1,0:T(8,128)(2,1)S(1)}, bf16[128,512]{1,0:T(8,128)(2,1)S(1)}, u32[]{:S(2)}, u32[]{:S(2)}) collective-permute-start(bf16[128,512]{1,0:T(8,128)(2,1)S(1)} %collective-permute-done.4), channel_id=1, source_target_pairs={{0,24},{1,25},{2,26},{3,27},{4,28},{5,29},{6,30},{7,31},{8,16},{9,... | collective-permute-start | bytes 393224 | tf_op jit(solution)/shard_map/ppermute | solution.py:714
  35.5 7.7 %collective-permute-start.2 = (bf16[256,1024]{1,0:T(8,128)(2,1)S(1)}, bf16[256,1024]{1,0:T(8,128)(2,1)S(1)}, u32[]{:S(2)}, u32[]{:S(2)}) collective-permute-start(bf16[256,1024]{1,0:T(8,128)(2,1)S(1)} %collective-permute-done.x0), channel_id=1, source_target_pairs={{0,4},{1,5},{2,6},{3,7},{4,0},{5,1},{6,2},{7,3},{8,12},{9,13},{10,... | collective-permute-start | bytes 1572872 | tf_op jit(solution)/shard_map/ppermute | solution.py:714
  38.1 9.7 %collective-permute-start.9 = (bf16[32,1024]{1,0:T(8,128)(2,1)S(1)}, bf16[32,1024]{1,0:T(8,128)(2,1)S(1)}, u32[]{:S(2)}, u32[]{:S(2)}) collective-permute-start(bf16[32,1024]{1,0:T(8,128)(2,1)S(1)} %constant_dynamic-slice_fusion.3), channel_id=1, source_target_pairs={{0,1},{1,0},{2,3},{3,2},{4,5},{5,4},{6,7},{7,6},{8,9},{9,8},{10,11... | collective-permute-start | bytes 196616 | tf_op jit(solution)/shard_map/ppermute | solution.py:714
  43.2 38.8 %collective-permute-start.8 = (bf16[512,512]{1,0:T(8,128)(2,1)}, bf16[512,512]{1,0:T(8,128)(2,1)}, u32[]{:S(2)}, u32[]{:S(2)}) collective-permute-start(bf16[512,512]{1,0:T(8,128)(2,1)} %constant_dynamic-update-slice_fusion.w0), channel_id=1, source_target_pairs={{0,4},{1,5},{2,6},{3,7},{4,0},{5,1},{6,2},{7,3},{8,12},{9,13},{10,... | collective-permute-start | bytes 1572872 | tf_op jit(solution)/shard_map/ppermute | solution.py:714
  45.4 58.2 %collective-permute-start.15 = (bf16[128,2304]{1,0:T(8,128)(2,1)}, bf16[128,2304]{1,0:T(8,128)(2,1)}, u32[]{:S(2)}, u32[]{:S(2)}) collective-permute-start(bf16[128,2304]{1,0:T(8,128)(2,1)} %pad_maximum_fusion.1), channel_id=1, source_target_pairs={{0,2},{1,3},{2,0},{3,1},{4,6},{5,7},{6,4},{7,5},{8,10},{9,11},{10,... | collective-permute-start | bytes 1769480 | tf_op jit(solution)/shard_map/ppermute | solution.py:714
  47.5 33.7 %collective-permute-start.3 = (bf16[256,1024]{1,0:T(8,128)(2,1)S(1)}, bf16[256,1024]{1,0:T(8,128)(2,1)S(1)}, u32[]{:S(2)}, u32[]{:S(2)}) collective-permute-start(bf16[256,1024]{1,0:T(8,128)(2,1)S(1)} %collective-permute-done.1.x1), channel_id=1, source_target_pairs={{0,4},{1,5},{2,6},{3,7},{4,0},{5,1},{6,2},{7,3},{8,12},{9,13},{10,... | collective-permute-start | bytes 1572872 | tf_op jit(solution)/shard_map/ppermute | solution.py:714
  47.8 32.7 %collective-permute-start.10 = (bf16[2,32,1024]{2,1,0:T(8,128)(2,1)S(1)}, bf16[2,32,1024]{2,1,0:T(8,128)(2,1)S(1)}, u32[]{:S(2)}, u32[]{:S(2)}) collective-permute-start(bf16[2,32,1024]{2,1,0:T(8,128)(2,1)S(1)} %pad_maximum_fusion.9), channel_id=1, source_target_pairs={{0,2},{1,3},{2,0},{3,1},{4,6},{5,7},{6,4},{7,5},{8,10},{9,11},{10,... | collective-permute-start | bytes 393224 | tf_op jit(solution)/shard_map/ppermute | solution.py:714
  103.6 22.7 %collective-permute-start.16 = (bf16[128,2304]{1,0:T(8,128)(2,1)}, bf16[128,2304]{1,0:T(8,128)(2,1)}, u32[]{:S(2)}, u32[]{:S(2)}) collective-permute-start(bf16[128,2304]{1,0:T(8,128)(2,1)} %collective-permute-done.15), channel_id=1, source_target_pairs={{0,8},{1,9},{2,10},{3,11},{4,12},{5,13},{6,14},{7,15},{8,0},{9,1},... | collective-permute-start | bytes 1769480 | tf_op jit(solution)/shard_map/ppermute | solution.py:714
  104.2 30.5 %collective-permute-start.17 = (bf16[128,2304]{1,0:T(8,128)(2,1)}, bf16[128,2304]{1,0:T(8,128)(2,1)}, u32[]{:S(2)}, u32[]{:S(2)}) collective-permute-start(bf16[128,2304]{1,0:T(8,128)(2,1)} %collective-permute-done.15), channel_id=1, source_target_pairs={{0,16},{1,17},{2,18},{3,19},{4,20},{5,21},{6,22},{7,23},{8,24},{9,... | collective-permute-start | bytes 1769480 | tf_op jit(solution)/shard_map/ppermute | solution.py:714
  105.7 30.0 %collective-permute-start.18 = (bf16[128,2304]{1,0:T(8,128)(2,1)}, bf16[128,2304]{1,0:T(8,128)(2,1)}, u32[]{:S(2)}, u32[]{:S(2)}) collective-permute-start(bf16[128,2304]{1,0:T(8,128)(2,1)} %collective-permute-done.15), channel_id=1, source_target_pairs={{0,24},{1,25},{2,26},{3,27},{4,28},{5,29},{6,30},{7,31},{8,16},{9,... | collective-permute-start | bytes 1769480 | tf_op jit(solution)/shard_map/ppermute | solution.py:714
  107.1 19.2 %collective-permute-start.12 = (bf16[1024,256]{1,0:T(8,128)(2,1)S(1)}, bf16[1024,256]{1,0:T(8,128)(2,1)S(1)}, u32[]{:S(2)}, u32[]{:S(2)}) collective-permute-start(bf16[1024,256]{1,0:T(8,128)(2,1)S(1)} %get-tuple-element.192.a0.left_ref), channel_id=1, source_target_pairs={{0,1},{1,0},{2,3},{3,2},{4,5},{5,4},{6,7},{7,6},{8,9},{9,8},{10,11... | collective-permute-start | bytes 1572872 | tf_op jit(solution)/shard_map/ppermute | solution.py:714
  107.4 322.9 %all-gather.15.cloned.1.call-start = ((), (), s32[]{:S(2)}) async-start(), calls=%async_computation.2 | async-start | bytes 2654208 | tf_op jit(solution)/shard_map/all_gather | solution.py:799
  107.4 35.1 %collective-permute-start.20 = (bf16[256,1024]{1,0:T(8,128)(2,1)}, bf16[256,1024]{1,0:T(8,128)(2,1)S(1)}, u32[]{:S(2)}, u32[]{:S(2)}) collective-permute-start(bf16[256,1024]{1,0:T(8,128)(2,1)} %param.29), channel_id=1, source_target_pairs={{0,0},{1,1},{2,4},{3,5},{4,2},{5,3},{6,6},{7,7},{8,8},{9,9},{10,12... | collective-permute-start | bytes 1572872 | tf_op jit(solution)/shard_map/ppermute | solution.py:714
  126.3 16.2 %collective-permute-start.14 = (bf16[1024,256]{1,0:T(8,128)(2,1)S(1)}, bf16[1024,256]{1,0:T(8,128)(2,1)}, u32[]{:S(2)}, u32[]{:S(2)}) collective-permute-start(bf16[1024,256]{1,0:T(8,128)(2,1)S(1)} %collective-permute-done.12.a1), channel_id=1, source_target_pairs={{0,4},{1,5},{2,6},{3,7},{4,0},{5,1},{6,2},{7,3},{8,12},{9,13},{10,... | collective-permute-start | bytes 1572872 | tf_op jit(solution)/shard_map/ppermute | solution.py:714
  141.5 41.3 %collective-permute-start.19 = (bf16[512,2304]{1,0:T(8,128)(2,1)}, bf16[512,2304]{1,0:T(8,128)(2,1)}, u32[]{:S(2)}, u32[]{:S(2)}) collective-permute-start(bf16[512,2304]{1,0:T(8,128)(2,1)} %constant_dynamic-update-slice_fusion.4.p0), channel_id=1, source_target_pairs={{0,4},{1,5},{2,6},{3,7},{4,0},{5,1},{6,2},{7,3},{8,12},{9,13},{10,... | collective-permute-start | bytes 7077896 | tf_op jit(solution)/shard_map/ppermute | solution.py:714
  142.5 16.8 %collective-permute-start.21 = (bf16[144,1024]{1,0:T(8,128)(2,1)S(1)}, bf16[144,1024]{1,0:T(8,128)(2,1)S(1)}, u32[]{:S(2)}, u32[]{:S(2)}) collective-permute-start(bf16[144,1024]{1,0:T(8,128)(2,1)S(1)} %constant_dynamic-slice_fusion), channel_id=1, source_target_pairs={{0,2},{1,3},{2,0},{3,1},{4,6},{5,7},{6,4},{7,5},{8,10},{9,11},{10,... | collective-permute-start | bytes 884744 | tf_op jit(solution)/shard_map/ppermute | solution.py:714
  142.6 32.5 %collective-permute-start.25 = (bf16[256,1024]{1,0:T(8,128)(2,1)S(1)}, bf16[256,1024]{1,0:T(8,128)(2,1)}, u32[]{:S(2)}, u32[]{:S(2)}) collective-permute-start(bf16[256,1024]{1,0:T(8,128)(2,1)S(1)} %collective-permute-done.20.r0.y0), channel_id=1, source_target_pairs={{0,1},{1,0},{2,3},{3,2},{4,5},{5,4},{6,7},{7,6},{8,9},{9,8},{10,11... | collective-permute-start | bytes 1572872 | tf_op jit(solution)/shard_map/ppermute | solution.py:714
  159.3 9.9 %collective-permute-start.22 = (bf16[144,1024]{1,0:T(8,128)(2,1)S(1)}, bf16[144,1024]{1,0:T(8,128)(2,1)S(1)}, u32[]{:S(2)}, u32[]{:S(2)}) collective-permute-start(bf16[144,1024]{1,0:T(8,128)(2,1)S(1)} %collective-permute-done.21), channel_id=1, source_target_pairs={{0,8},{1,9},{2,10},{3,11},{4,12},{5,13},{6,14},{7,15},{8,0},{9,1},... | collective-permute-start | bytes 884744 | tf_op jit(solution)/shard_map/ppermute | solution.py:714
  160.5 13.0 %collective-permute-start.23 = (bf16[144,1024]{1,0:T(8,128)(2,1)S(1)}, bf16[144,1024]{1,0:T(8,128)(2,1)S(1)}, u32[]{:S(2)}, u32[]{:S(2)}) collective-permute-start(bf16[144,1024]{1,0:T(8,128)(2,1)S(1)} %collective-permute-done.21), channel_id=1, source_target_pairs={{0,16},{1,17},{2,18},{3,19},{4,20},{5,21},{6,22},{7,23},{8,24},{9,... | collective-permute-start | bytes 884744 | tf_op jit(solution)/shard_map/ppermute | solution.py:714
  161.3 13.7 %collective-permute-start.24 = (bf16[144,1024]{1,0:T(8,128)(2,1)S(1)}, bf16[144,1024]{1,0:T(8,128)(2,1)S(1)}, u32[]{:S(2)}, u32[]{:S(2)}) collective-permute-start(bf16[144,1024]{1,0:T(8,128)(2,1)S(1)} %collective-permute-done.21), channel_id=1, source_target_pairs={{0,24},{1,25},{2,26},{3,27},{4,28},{5,29},{6,30},{7,31},{8,16},{9,... | collective-permute-start | bytes 884744 | tf_op jit(solution)/shard_map/ppermute | solution.py:714
  177.3 38.3 %collective-permute-start.26 = (bf16[576,1024]{1,0:T(8,128)(2,1)}, bf16[576,1024]{1,0:T(8,128)(2,1)}, u32[]{:S(2)}, u32[]{:S(2)}) collective-permute-start(bf16[576,1024]{1,0:T(8,128)(2,1)} %constant_dynamic-update-slice_fusion.8.d0), channel_id=1, source_target_pairs={{0,4},{1,5},{2,6},{3,7},{4,0},{5,1},{6,2},{7,3},{8,12},{9,13},{10,... | collective-permute-start | bytes 3538952 | tf_op jit(solution)/shard_map/ppermute | solution.py:714
  177.3 4.7 collective-permute-start.13
  177.8 27.0 %collective-permute-start.27 = (bf16[256,1024]{1,0:T(8,128)(2,1)S(1)}, bf16[256,1024]{1,0:T(8,128)(2,1)}, u32[]{:S(2)}, u32[]{:S(2)}) collective-permute-start(bf16[256,1024]{1,0:T(8,128)(2,1)S(1)} %collective-permute-done.20.r0.y0), channel_id=1, source_target_pairs={{0,4},{1,5},{2,6},{3,7},{4,0},{5,1},{6,2},{7,3},{8,12},{9,13},{10,... | collective-permute-start | bytes 1572872 | tf_op jit(solution)/shard_map/ppermute | solution.py:714
  177.8 27.0 %collective-permute-start.28 = (bf16[256,1024]{1,0:T(8,128)(2,1)}, bf16[256,1024]{1,0:T(8,128)(2,1)}, u32[]{:S(2)}, u32[]{:S(2)}) collective-permute-start(bf16[256,1024]{1,0:T(8,128)(2,1)} %collective-permute-done.25.r1.y1), channel_id=1, source_target_pairs={{0,4},{1,5},{2,6},{3,7},{4,0},{5,1},{6,2},{7,3},{8,12},{9,13},{10,... | collective-permute-start | bytes 1572872 | tf_op jit(solution)/shard_map/ppermute | solution.py:714
  232.2 14.5 %collective-permute-start.31 = (bf16[512,1024]{1,0:T(8,128)(2,1)}, bf16[512,1024]{1,0:T(8,128)(2,1)}, u32[]{:S(2)}, u32[]{:S(2)}) collective-permute-start(bf16[512,1024]{1,0:T(8,128)(2,1)} %get-tuple-element.143), channel_id=1, source_target_pairs={{0,4},{1,5},{2,6},{3,7},{4,0},{5,1},{6,2},{7,3},{8,12},{9,13},{10,... | collective-permute-start | bytes 3145736 | tf_op jit(solution)/shard_map/ppermute | solution.py:714
  235.5 15.6 %collective-permute-start.29 = (bf16[2,288,512]{2,1,0:T(8,128)(2,1)}, bf16[2,288,512]{2,1,0:T(8,128)(2,1)}, u32[]{:S(2)}, u32[]{:S(2)}) collective-permute-start(bf16[2,288,512]{2,1,0:T(8,128)(2,1)} %get-tuple-element.136), channel_id=1, source_target_pairs={{0,8},{1,9},{2,10},{3,11},{4,12},{5,13},{6,14},{7,15},{8,0},{9,1},... | collective-permute-start | bytes 1769480 | tf_op jit(solution)/shard_map/ppermute | solution.py:714
  236.3 15.3 %collective-permute-start.30 = (bf16[2,288,512]{2,1,0:T(8,128)(2,1)}, bf16[2,288,512]{2,1,0:T(8,128)(2,1)}, u32[]{:S(2)}, u32[]{:S(2)}) collective-permute-start(bf16[2,288,512]{2,1,0:T(8,128)(2,1)} %get-tuple-element.137), channel_id=1, source_target_pairs={{0,16},{1,17},{2,18},{3,19},{4,20},{5,21},{6,22},{7,23},{8,24},{9,... | collective-permute-start | bytes 1769480 | tf_op jit(solution)/shard_map/ppermute | solution.py:714
  245.6 61.9 %collective-permute-start.35 = (bf16[512,1024]{1,0:T(8,128)(2,1)S(1)}, bf16[512,1024]{1,0:T(8,128)(2,1)S(1)}, u32[]{:S(2)}, u32[]{:S(2)}) collective-permute-start(bf16[512,1024]{1,0:T(8,128)(2,1)S(1)} %get-tuple-element.164), channel_id=1, source_target_pairs={{0,4},{1,5},{2,6},{3,7},{4,0},{5,1},{6,2},{7,3},{8,12},{9,13},{10,... | collective-permute-start | bytes 3145736 | tf_op jit(solution)/shard_map/ppermute | solution.py:714
  248.5 18.3 %collective-permute-start.34 = (bf16[256,1024]{1,0:T(8,128)(2,1)S(1)}, bf16[256,1024]{1,0:T(8,128)(2,1)S(1)}, u32[]{:S(2)}, u32[]{:S(2)}) collective-permute-start(bf16[256,1024]{1,0:T(8,128)(2,1)S(1)} %slice.404), channel_id=1, source_target_pairs={{0,1},{1,0},{2,3},{3,2},{4,5},{5,4},{6,7},{7,6},{8,9},{9,8},{10,11... | collective-permute-start | bytes 1572872 | tf_op jit(solution)/shard_map/ppermute | solution.py:714
  252.7 16.6 %collective-permute-start.32 = (bf16[288,512]{1,0:T(8,128)(2,1)S(1)}, bf16[288,512]{1,0:T(8,128)(2,1)S(1)}, u32[]{:S(2)}, u32[]{:S(2)}) collective-permute-start(bf16[288,512]{1,0:T(8,128)(2,1)S(1)} %get-tuple-element.244), channel_id=1, source_target_pairs={{0,16},{1,17},{2,18},{3,19},{4,20},{5,21},{6,22},{7,23},{8,24},{9,... | collective-permute-start | bytes 884744 | tf_op jit(solution)/shard_map/ppermute | solution.py:714
  255.3 15.2 %collective-permute-start.33 = (bf16[288,512]{1,0:T(8,128)(2,1)S(1)}, bf16[288,512]{1,0:T(8,128)(2,1)S(1)}, u32[]{:S(2)}, u32[]{:S(2)}) collective-permute-start(bf16[288,512]{1,0:T(8,128)(2,1)S(1)} %get-tuple-element.242), channel_id=1, source_target_pairs={{0,8},{1,9},{2,10},{3,11},{4,12},{5,13},{6,14},{7,15},{8,0},{9,1},... | collective-permute-start | bytes 884744 | tf_op jit(solution)/shard_map/ppermute | solution.py:714
  265.4 29.8 %collective-permute-start.36 = (bf16[2,128,1152]{2,1,0:T(8,128)(2,1)S(1)}, bf16[2,128,1152]{2,1,0:T(8,128)(2,1)S(1)}, u32[]{:S(2)}, u32[]{:S(2)}) collective-permute-start(bf16[2,128,1152]{2,1,0:T(8,128)(2,1)S(1)} %get-tuple-element.155), channel_id=1, source_target_pairs={{0,8},{1,9},{2,10},{3,11},{4,12},{5,13},{6,14},{7,15},{8,0},{9,1},... | collective-permute-start | bytes 1769480 | tf_op jit(solution)/shard_map/ppermute | solution.py:714
  266.8 29.5 %collective-permute-start.37 = (bf16[2,128,1152]{2,1,0:T(8,128)(2,1)S(1)}, bf16[2,128,1152]{2,1,0:T(8,128)(2,1)S(1)}, u32[]{:S(2)}, u32[]{:S(2)}) collective-permute-start(bf16[2,128,1152]{2,1,0:T(8,128)(2,1)S(1)} %get-tuple-element.157), channel_id=1, source_target_pairs={{0,16},{1,17},{2,18},{3,19},{4,20},{5,21},{6,22},{7,23},{8,24},{9,... | collective-permute-start | bytes 1769480 | tf_op jit(solution)/shard_map/ppermute | solution.py:714
  269.3 22.3 %collective-permute-start.39 = (bf16[2,128,1152]{2,1,0:T(8,128)(2,1)S(1)}, bf16[2,128,1152]{2,1,0:T(8,128)(2,1)S(1)}, u32[]{:S(2)}, u32[]{:S(2)}) collective-permute-start(bf16[2,128,1152]{2,1,0:T(8,128)(2,1)S(1)} %get-tuple-element.150), channel_id=1, source_target_pairs={{0,8},{1,9},{2,10},{3,11},{4,12},{5,13},{6,14},{7,15},{8,0},{9,1},... | collective-permute-start | bytes 1769480 | tf_op jit(solution)/shard_map/ppermute | solution.py:714
  270.5 22.2 %collective-permute-start.40 = (bf16[2,128,1152]{2,1,0:T(8,128)(2,1)S(1)}, bf16[2,128,1152]{2,1,0:T(8,128)(2,1)S(1)}, u32[]{:S(2)}, u32[]{:S(2)}) collective-permute-start(bf16[2,128,1152]{2,1,0:T(8,128)(2,1)S(1)} %get-tuple-element.152), channel_id=1, source_target_pairs={{0,16},{1,17},{2,18},{3,19},{4,20},{5,21},{6,22},{7,23},{8,24},{9,... | collective-permute-start | bytes 1769480 | tf_op jit(solution)/shard_map/ppermute | solution.py:714
  291.6 14.0 %collective-permute-start.38 = (bf16[256,1024]{1,0:T(8,128)(2,1)S(1)}, bf16[256,1024]{1,0:T(8,128)(2,1)S(1)}, u32[]{:S(2)}, u32[]{:S(2)}) collective-permute-start(bf16[256,1024]{1,0:T(8,128)(2,1)S(1)} %get-tuple-element.225.b0.r0), channel_id=1, source_target_pairs={{0,1},{1,0},{2,3},{3,2},{4,5},{5,4},{6,7},{7,6},{8,9},{9,8},{10,11... | collective-permute-start | bytes 1572872 | tf_op jit(solution)/shard_map/ppermute | solution.py:714
  294.5 19.7 %collective-permute-start.42 = (bf16[128,1152]{1,0:T(8,128)(2,1)}, bf16[128,1152]{1,0:T(8,128)(2,1)}, u32[]{:S(2)}, u32[]{:S(2)}) collective-permute-start(bf16[128,1152]{1,0:T(8,128)(2,1)} %get-tuple-element.240), channel_id=1, source_target_pairs={{0,16},{1,17},{2,18},{3,19},{4,20},{5,21},{6,22},{7,23},{8,24},{9,... | collective-permute-start | bytes 884744 | tf_op jit(solution)/shard_map/ppermute | solution.py:714
  295.2 19.0 %collective-permute-start.43 = (bf16[128,1152]{1,0:T(8,128)(2,1)}, bf16[128,1152]{1,0:T(8,128)(2,1)}, u32[]{:S(2)}, u32[]{:S(2)}) collective-permute-start(bf16[128,1152]{1,0:T(8,128)(2,1)} %get-tuple-element.238), channel_id=1, source_target_pairs={{0,8},{1,9},{2,10},{3,11},{4,12},{5,13},{6,14},{7,15},{8,0},{9,1},... | collective-permute-start | bytes 884744 | tf_op jit(solution)/shard_map/ppermute | solution.py:714
  296.4 16.1 %collective-permute-start.45 = (bf16[2,144,512]{2,1,0:T(8,128)(2,1)S(1)}, bf16[2,144,512]{2,1,0:T(8,128)(2,1)S(1)}, u32[]{:S(2)}, u32[]{:S(2)}) collective-permute-start(bf16[2,144,512]{2,1,0:T(8,128)(2,1)S(1)} %broadcast_select_fusion), channel_id=1, source_target_pairs={{0,2},{1,3},{2,0},{3,1},{4,6},{5,7},{6,4},{7,5},{8,10},{9,11},{10,... | collective-permute-start | bytes 884744 | tf_op jit(solution)/shard_map/ppermute | solution.py:714
  305.6 6.8 %collective-permute-start.46 = (bf16[256,1024]{1,0:T(8,128)(2,1)S(1)}, bf16[256,1024]{1,0:T(8,128)(2,1)S(1)}, u32[]{:S(2)}, u32[]{:S(2)}) collective-permute-start(bf16[256,1024]{1,0:T(8,128)(2,1)S(1)} %collective-permute-done.38.b1.r1), channel_id=1, source_target_pairs={{0,4},{1,5},{2,6},{3,7},{4,0},{5,1},{6,2},{7,3},{8,12},{9,13},{10,... | collective-permute-start | bytes 1572872 | tf_op jit(solution)/shard_map/ppermute | solution.py:714
  314.0 156.8 %all-gather.13.cloned.1.call-start = ((), (), s32[]{:S(2)}) async-start(), calls=%async_computation.1 | async-start | bytes 2654208 | tf_op jit(solution)/shard_map/all_gather | solution.py:799
  343.8 15.6 %collective-permute-start.51 = (bf16[512,1024]{1,0:T(8,128)(2,1)S(1)}, bf16[512,1024]{1,0:T(8,128)(2,1)S(1)}, u32[]{:S(2)}, u32[]{:S(2)}) collective-permute-start(bf16[512,1024]{1,0:T(8,128)(2,1)S(1)} %get-tuple-element.182), channel_id=1, source_target_pairs={{0,4},{1,5},{2,6},{3,7},{4,0},{5,1},{6,2},{7,3},{8,12},{9,13},{10,... | collective-permute-start | bytes 3145736 | tf_op jit(solution)/shard_map/ppermute | solution.py:714
  344.0 15.3 %collective-permute-start.52 = (bf16[2,64,1152]{2,1,0:T(8,128)(2,1)S(1)}, bf16[2,64,1152]{2,1,0:T(8,128)(2,1)S(1)}, u32[]{:S(2)}, u32[]{:S(2)}) collective-permute-start(bf16[2,64,1152]{2,1,0:T(8,128)(2,1)S(1)} %get-tuple-element.249), channel_id=1, source_target_pairs={{0,2},{1,3},{2,0},{3,1},{4,6},{5,7},{6,4},{7,5},{8,10},{9,11},{10,... | collective-permute-start | bytes 884744 | tf_op jit(solution)/shard_map/ppermute | solution.py:714
  344.0 19.1 %collective-permute-start.49 = (bf16[128,1152]{1,0:T(8,128)(2,1)}, bf16[128,1152]{1,0:T(8,128)(2,1)S(1)}, u32[]{:S(2)}, u32[]{:S(2)}) collective-permute-start(bf16[128,1152]{1,0:T(8,128)(2,1)} %get-tuple-element.236), channel_id=1, source_target_pairs={{0,16},{1,17},{2,18},{3,19},{4,20},{5,21},{6,22},{7,23},{8,24},{9,... | collective-permute-start | bytes 884744 | tf_op jit(solution)/shard_map/ppermute | solution.py:714
  345.0 18.8 %collective-permute-start.50 = (bf16[128,1152]{1,0:T(8,128)(2,1)}, bf16[128,1152]{1,0:T(8,128)(2,1)}, u32[]{:S(2)}, u32[]{:S(2)}) collective-permute-start(bf16[128,1152]{1,0:T(8,128)(2,1)} %get-tuple-element.234), channel_id=1, source_target_pairs={{0,8},{1,9},{2,10},{3,11},{4,12},{5,13},{6,14},{7,15},{8,0},{9,1},... | collective-permute-start | bytes 884744 | tf_op jit(solution)/shard_map/ppermute | solution.py:714
  367.8 15.6 %collective-permute-start.41 = (bf16[256,1024]{1,0:T(8,128)(2,1)}, bf16[256,1024]{1,0:T(8,128)(2,1)}, u32[]{:S(2)}, u32[]{:S(2)}) collective-permute-start(bf16[256,1024]{1,0:T(8,128)(2,1)} %slice.406), channel_id=1, source_target_pairs={{0,1},{1,0},{2,3},{3,2},{4,5},{5,4},{6,7},{7,6},{8,9},{9,8},{10,11... | collective-permute-start | bytes 1572872 | tf_op jit(solution)/shard_map/ppermute | solution.py:714
  368.7 111.8 %all-gather.19.cloned.1.call-start = ((), (), s32[]{:S(2)}) async-start(), calls=%async_computation.4 | async-start | bytes 2654208 | tf_op jit(solution)/shard_map/all_gather | solution.py:799
  368.7 31.1 %collective-permute-start.58 = (bf16[256,1024]{1,0:T(8,128)(2,1)}, bf16[256,1024]{1,0:T(8,128)(2,1)S(1)}, u32[]{:S(2)}, u32[]{:S(2)}) collective-permute-start(bf16[256,1024]{1,0:T(8,128)(2,1)} %slice.417), channel_id=1, source_target_pairs={{0,1},{1,0},{2,3},{3,2},{4,5},{5,4},{6,7},{7,6},{8,9},{9,8},{10,11... | collective-permute-start | bytes 1572872 | tf_op jit(solution)/shard_map/ppermute | solution.py:714
  384.1 17.5 %collective-permute-start.57 = (bf16[2,64,1152]{2,1,0:T(8,128)(2,1)S(1)}, bf16[2,64,1152]{2,1,0:T(8,128)(2,1)S(1)}, u32[]{:S(2)}, u32[]{:S(2)}) collective-permute-start(bf16[2,64,1152]{2,1,0:T(8,128)(2,1)S(1)} %get-tuple-element.247), channel_id=1, source_target_pairs={{0,2},{1,3},{2,0},{3,1},{4,6},{5,7},{6,4},{7,5},{8,10},{9,11},{10,... | collective-permute-start | bytes 884744 | tf_op jit(solution)/shard_map/ppermute | solution.py:714
  402.5 83.3 %all-gather.17.cloned.1.call-start = ((), (), s32[]{:S(2)}) async-start(), calls=%async_computation.3 | async-start | bytes 1769472 | tf_op jit(solution)/shard_map/all_gather | solution.py:799
  402.5 14.1 %collective-permute-start.55 = (bf16[2,384,256]{2,1,0:T(8,128)(2,1)}, bf16[2,384,256]{2,1,0:T(8,128)(2,1)S(1)}, u32[]{:S(2)}, u32[]{:S(2)}) collective-permute-start(bf16[2,384,256]{2,1,0:T(8,128)(2,1)} %copy-done.92), channel_id=1, source_target_pairs={{0,8},{1,9},{2,10},{3,11},{4,12},{5,13},{6,14},{7,15},{8,0},{9,1},... | collective-permute-start | bytes 1179656 | tf_op jit(solution)/shard_map/ppermute | solution.py:714
  403.4 14.1 %collective-permute-start.56 = (bf16[2,384,256]{2,1,0:T(8,128)(2,1)}, bf16[2,384,256]{2,1,0:T(8,128)(2,1)S(1)}, u32[]{:S(2)}, u32[]{:S(2)}) collective-permute-start(bf16[2,384,256]{2,1,0:T(8,128)(2,1)} %copy-done.93), channel_id=1, source_target_pairs={{0,16},{1,17},{2,18},{3,19},{4,20},{5,21},{6,22},{7,23},{8,24},{9,... | collective-permute-start | bytes 1179656 | tf_op jit(solution)/shard_map/ppermute | solution.py:714
  417.5 5.7 %collective-permute-start.59 = (bf16[384,256]{1,0:T(8,128)(2,1)S(1)}, bf16[384,256]{1,0:T(8,128)(2,1)S(1)}, u32[]{:S(2)}, u32[]{:S(2)}) collective-permute-start(bf16[384,256]{1,0:T(8,128)(2,1)S(1)} %fusion.22), channel_id=1, source_target_pairs={{0,16},{1,17},{2,18},{3,19},{4,20},{5,21},{6,22},{7,23},{8,24},{9,... | collective-permute-start | bytes 589832 | tf_op jit(solution)/shard_map/ppermute | solution.py:714
  419.7 8.7 %collective-permute-start.60 = (bf16[384,256]{1,0:T(8,128)(2,1)S(1)}, bf16[384,256]{1,0:T(8,128)(2,1)S(1)}, u32[]{:S(2)}, u32[]{:S(2)}) collective-permute-start(bf16[384,256]{1,0:T(8,128)(2,1)S(1)} %fusion.21), channel_id=1, source_target_pairs={{0,8},{1,9},{2,10},{3,11},{4,12},{5,13},{6,14},{7,15},{8,0},{9,1},... | collective-permute-start | bytes 589832 | tf_op jit(solution)/shard_map/ppermute | solution.py:714
  430.2 9.6 %collective-permute-start.68 = (bf16[2,192,256]{2,1,0:T(8,128)(2,1)S(1)}, bf16[2,192,256]{2,1,0:T(8,128)(2,1)S(1)}, u32[]{:S(2)}, u32[]{:S(2)}) collective-permute-start(bf16[2,192,256]{2,1,0:T(8,128)(2,1)S(1)} %get-tuple-element.251), channel_id=1, source_target_pairs={{0,2},{1,3},{2,0},{3,1},{4,6},{5,7},{6,4},{7,5},{8,10},{9,11},{10,... | collective-permute-start | bytes 589832 | tf_op jit(solution)/shard_map/ppermute | solution.py:714
  440.8 35.4 %collective-permute-start.54 = (bf16[256,1024]{1,0:T(8,128)(2,1)S(1)}, bf16[256,1024]{1,0:T(8,128)(2,1)}, u32[]{:S(2)}, u32[]{:S(2)}) collective-permute-start(bf16[256,1024]{1,0:T(8,128)(2,1)S(1)} %copy-done.89), channel_id=1, source_target_pairs={{0,0},{1,1},{2,4},{3,5},{4,2},{5,3},{6,6},{7,7},{8,8},{9,9},{10,12... | collective-permute-start | bytes 1572872 | tf_op jit(solution)/shard_map/ppermute | solution.py:714
  442.2 34.0 %collective-permute-start.62 = (bf16[256,1024]{1,0:T(8,128)(2,1)S(1)}, bf16[256,1024]{1,0:T(8,128)(2,1)}, u32[]{:S(2)}, u32[]{:S(2)}) collective-permute-start(bf16[256,1024]{1,0:T(8,128)(2,1)S(1)} %copy-done.90), channel_id=1, source_target_pairs={{0,0},{1,1},{2,4},{3,5},{4,2},{5,3},{6,6},{7,7},{8,8},{9,9},{10,12... | collective-permute-start | bytes 1572872 | tf_op jit(solution)/shard_map/ppermute | solution.py:714
  455.0 14.7 %collective-permute-start.67 = (f32[1,2176]{1,0:T(1,128)S(1)}, f32[1,2176]{1,0:T(1,128)S(1)}, u32[]{:S(2)}, u32[]{:S(2)}) collective-permute-start(f32[1,2176]{1,0:T(1,128)S(1)} %add.295), channel_id=1, source_target_pairs={{0,2},{1,3},{2,0},{3,1},{4,6},{5,7},{6,4},{7,5},{8,10},{9,11},{10,... | collective-permute-start | bytes 26120 | tf_op jit(solution)/shard_map/ppermute | solution.py:714
  (106 other events, 996.0 us)
Sparse Core Ops, SparseCore 0:
  107.5 43.3 all-gather.10
  314.2 27.5 all-gather.14
  368.8 28.7 all-gather.12
  402.6 30.6 all-gather.18
  440.6 24.0 all-gather.16

commit v2 on v1

--- a/solution.py
+++ b/solution.py
@@ -53,9 +53,9 @@
 
 
 class Weight:
-    def __init__(self, s_ref, own, parts, to, sems, start=0):
+    def __init__(self, s_ref, own, parts, to, sems):
         self.core, self.e = s_ref[1], s_ref[2]
-        self.own, self.parts, self.to, self.sems, self.start_col = own, parts, to, sems, start
+        self.own, self.parts, self.to, self.sems = own, parts, to, sems
 
     def copies(self):
         start = 0
@@ -68,9 +68,9 @@
         for j in range(4):
             for other in range(2):
                 at = pl.multiple_of((2 * (self.e ^ j) + 1 - other) * rows, rows)
-                src = self.parts[other].at[pl.ds(j * rows, rows), pl.ds(self.start_col, self.to.shape[1])]
+                to = self.to.at[pl.ds(at, rows), :]
                 yield 1, functools.partial(
-                    pltpu.make_async_copy, src, self.to.at[pl.ds(at, rows), :], self.sems.at[2 * j + other]
+                    pltpu.make_async_copy, self.parts[4 * other + j], to, self.sems.at[2 * j + other]
                 )
 
     def each(self, act):
@@ -104,11 +104,11 @@
     return pltpu.CompilerParams(vmem_limit_bytes=mib * VMEM_MB)
 
 
-def qkv_kernel(s_ref, x0, x1, x2, x3, wq_own, wk_own, wv_own, w0, w1, g1_ref, gains_ref, cos_ref, sin_ref,
-               n1_ref, pre_ref, qk_ref, v_ref, w_ref, xs, xsem, wsem):
+def qkv_kernel(s_ref, *refs):
+    pieces, own, parts, refs = refs[:4], refs[4:7], refs[7:15], refs[15:]
+    g1_ref, gains_ref, cos_ref, sin_ref, n1_ref, pre_ref, qk_ref, v_ref, w_ref, xs, xsem, wsem = refs
     j = pl.program_id(0)
-    pieces = (x0, x1, x2, x3)
-    weight = Weight(s_ref, (wq_own, wk_own, wv_own), (w0, w1), w_ref, wsem)
+    weight = Weight(s_ref, own, parts, w_ref, wsem)
 
     @pl.when(j == 0)
     def _():
@@ -116,7 +116,7 @@
             pltpu.make_async_copy(pieces[k], xs.at[k], xsem.at[k]).start()
         weight.start()
 
-    pltpu.make_async_copy(x0, xs.at[j], xsem.at[j]).wait()
+    pltpu.make_async_copy(pieces[0], xs.at[j], xsem.at[j]).wait()
     x = xs[j].astype(f32)
     inv = lax.rsqrt(jnp.mean(x * x, axis=-1, keepdims=True) + epsilon)
     n1 = (x * inv * g1_ref[...]).astype(bf16)
@@ -149,7 +149,7 @@
         grid_spec=pltpu.PrefetchScalarGridSpec(
             num_scalar_prefetch=1,
             grid=(4,),
-            in_specs=[ANY] * 9
+            in_specs=[ANY] * 15
             + [fixed(1, d), fixed(1, qkw), pl.BlockSpec((b, 128), natural), pl.BlockSpec((b, 128), natural)],
             out_specs=[
                 pl.BlockSpec((b, d), lambda j, s: (j, 0)),
@@ -377,13 +377,15 @@
     )(s, qk, qk, v, pre, pre, qgain, kgain, cos, sin, start, live, out, lse, wout, w, *blocks)
 
 
-def ffn_kernel(s_ref, x0, x1, x2, x3, a0, a1, a2, a3, o_in, wg_own, wu_own, p0, p1,
-               gain_ref, n2_ref, hid_ref, fg_ref, fu_ref, res_ref, wout_ref, wg, wu, xs, att, wout, asem, xsem, osem, gsem, usem):
+def ffn_kernel(s_ref, *refs):
+    x_in, a_in, o_in, refs = refs[:4], refs[4:8], refs[8], refs[9:]
+    wg_own, wg_parts, wu_own, wu_parts, refs = refs[0], refs[1:9], refs[9], refs[10:18], refs[18:]
+    gain_ref, n2_ref, hid_ref, fg_ref, fu_ref, res_ref, wout_ref, refs = *refs[:7], refs[7:]
+    wg, wu, xs, att, wout, asem, xsem, osem, gsem, usem = refs
     j = pl.program_id(0)
-    b = x0.shape[0]
-    x_in, a_in = (x0, x1, x2, x3), (a0, a1, a2, a3)
-    gate_w = Weight(s_ref, (wg_own,), (p0, p1), wg, gsem)
-    up_w = Weight(s_ref, (wu_own,), (p0, p1), wu, usem, wg.shape[1])
+    b = xs.shape[1]
+    gate_w = Weight(s_ref, (wg_own,), wg_parts, wg, gsem)
+    up_w = Weight(s_ref, (wu_own,), wu_parts, wu, usem)
 
     def out_copy(i):
         return pltpu.make_async_copy(o_in.at[:, i ^ (2 * s_ref[1])], wout.at[i], osem.at[i])
@@ -407,7 +409,7 @@
         for i in range(4):
             out_copy(i).wait()
 
-    pltpu.make_async_copy(x0, xs.at[j], xsem.at[j]).wait()
+    pltpu.make_async_copy(x_in[0], xs.at[j], xsem.at[j]).wait()
     for i in range(4):
         pltpu.make_async_copy(a_in[i].at[pl.ds(0, b), :], att.at[j, :, pl.ds(i * b, b)], asem.at[j, i]).wait()
     res = xs[j].astype(f32) + jnp.dot(att[j], wout[...].reshape(4 * b, -1), preferred_element_type=f32)
@@ -431,7 +433,7 @@
     fu_ref[...] = silu.astype(bf16)
 
 
-def ffn_call(s, xs, atts, wout, wg, wu, parts, gain):
+def ffn_call(s, xs, atts, wout, wg, g_parts, wu, u_parts, gain):
     b, d = xs[0].shape
     h = wg.shape[1]
     block = lambda wid: pl.BlockSpec((b, wid), lambda j, s: (j, 0))
@@ -440,7 +442,7 @@
         grid_spec=pltpu.PrefetchScalarGridSpec(
             num_scalar_prefetch=1,
             grid=(4,),
-            in_specs=[ANY] * 13 + [fixed(1, d)],
+            in_specs=[ANY] * 27 + [fixed(1, d)],
             out_specs=[block(d), block(h), block(h), block(h), fixed(b, d), fixed(b, d)],
             scratch_shapes=[
                 pltpu.VMEM((d, h), bf16),
@@ -458,19 +460,20 @@
         out_shape=[jax.ShapeDtypeStruct((4 * b, d), bf16)]
         + [jax.ShapeDtypeStruct((4 * b, h), bf16)] * 3
         + [jax.ShapeDtypeStruct((b, d), f32), jax.ShapeDtypeStruct((b, d), bf16)],
-        compiler_params=params(23),
+        compiler_params=params(58),
         cost_estimate=cost(1 << 24),
         name="ffn",
-    )(s, *xs, *atts, wout, wg, wu, *parts, gain)
-
-
-def ffn_back_kernel(s_ref, y0, y1, y2, y3, wd_own, d0, d1, wg_own, wu_own, p0, p1, fg_ref, fu_ref,
-                    gg_ref, gu_ref, lo_ref, hi_ref, wd, wg, wu, dy, ysem, dsem, gsem, usem):
+    )(s, *xs, *atts, wout, wg, *g_parts, wu, *u_parts, gain)
+
+
+def ffn_back_kernel(s_ref, *refs):
+    y_in, wd_own, wd_parts, refs = refs[:4], refs[4], refs[5:13], refs[13:]
+    wg_own, wg_parts, wu_own, wu_parts, refs = refs[0], refs[1:9], refs[9], refs[10:18], refs[18:]
+    fg_ref, fu_ref, gg_ref, gu_ref, lo_ref, hi_ref, wd, wg, wu, dy, ysem, dsem, gsem, usem = refs
     j = pl.program_id(0)
-    y_in = (y0, y1, y2, y3)
-    down_w = Weight(s_ref, (wd_own,), (d0, d1), wd, dsem)
-    gate_w = Weight(s_ref, (wg_own,), (p0, p1), wg, gsem)
-    up_w = Weight(s_ref, (wu_own,), (p0, p1), wu, usem, wg.shape[1])
+    down_w = Weight(s_ref, (wd_own,), wd_parts, wd, dsem)
+    gate_w = Weight(s_ref, (wg_own,), wg_parts, wg, gsem)
+    up_w = Weight(s_ref, (wu_own,), wu_parts, wu, usem)
 
     @pl.when(j == 0)
     def _():
@@ -482,7 +485,7 @@
         up_w.start()
         down_w.wait()
 
-    pltpu.make_async_copy(y0, dy.at[j], ysem.at[j]).wait()
+    pltpu.make_async_copy(y_in[0], dy.at[j], ysem.at[j]).wait()
     gh = contract(dy[j], wd[...], 1, 1)
     gg = (gh * fg_ref[...].astype(f32)).astype(bf16)
     gu = (gh * fu_ref[...].astype(f32)).astype(bf16)
@@ -505,7 +508,7 @@
         hi_ref[...] = grad
 
 
-def ffn_back_call(s, dys, wd, d_parts, wg, wu, parts, fg, fu):
+def ffn_back_call(s, dys, wd, d_parts, wg, g_parts, wu, u_parts, fg, fu):
     b, d = dys[0].shape
     h = wg.shape[1]
     block = lambda wid: pl.BlockSpec((b, wid), lambda j, s: (j, 0))
@@ -514,7 +517,7 @@
         grid_spec=pltpu.PrefetchScalarGridSpec(
             num_scalar_prefetch=1,
             grid=(4,),
-            in_specs=[ANY] * 11 + [block(h), block(h)],
+            in_specs=[ANY] * 31 + [block(h), block(h)],
             out_specs=[
                 block(h),
                 block(h),
@@ -533,15 +536,16 @@
             ],
         ),
         out_shape=[jax.ShapeDtypeStruct((4 * b, h), bf16)] * 2 + [jax.ShapeDtypeStruct((2 * b, d), bf16)] * 2,
-        compiler_params=params(19),
+        compiler_params=params(58),
         cost_estimate=cost(1 << 24),
         name="ffn_back",
-    )(s, *dys, wd, *d_parts, wg, wu, *parts, fg, fu)
-
-
-def ffn_out_kernel(s_ref, wd_own, d0, d1, hid_ref, lo_ref, hi_ref, wd, dsem):
+    )(s, *dys, wd, *d_parts, wg, *g_parts, wu, *u_parts, fg, fu)
+
+
+def ffn_out_kernel(s_ref, wd_own, *refs):
+    wd_parts, (hid_ref, lo_ref, hi_ref, wd, dsem) = refs[:8], refs[8:]
     j = pl.program_id(0)
-    down_w = Weight(s_ref, (wd_own,), (d0, d1), wd, dsem)
+    down_w = Weight(s_ref, (wd_own,), wd_parts, wd, dsem)
 
     @pl.when(j == 0)
     def _():
@@ -567,7 +571,7 @@
         grid_spec=pltpu.PrefetchScalarGridSpec(
             num_scalar_prefetch=1,
             grid=(4,),
-            in_specs=[ANY] * 3 + [pl.BlockSpec((b, h), lambda j, s: (j, 0))],
+            in_specs=[ANY] * 9 + [pl.BlockSpec((b, h), lambda j, s: (j, 0))],
             out_specs=[
                 pl.BlockSpec((b, d), lambda j, s: (jnp.minimum(j, 1), 0)),
                 pl.BlockSpec((b, d), lambda j, s: (jnp.maximum(j - 2, 0), 0)),
@@ -634,13 +638,24 @@
     )(s, left, right)
 
 
-def grad_cols_kernel(s_ref, left_ref, r0, r1, r2, r3, sent_a, keep_a, sent_b, keep_b):
+def grad_cols_kernel(s_ref, left_ref, r0, r1, r2, r3, sent_a, keep_a, sent_b, keep_b, right, sems):
     k = pl.program_id(0)
     b = r0.shape[0]
-    grad = None
-    for i, right in enumerate((r0, r1, r2, r3)):
-        part = contract(left_ref[i * b : (i + 1) * b, :], right[...], 0, 0)
-        grad = part if grad is None else grad + part
+    cols = left_ref.shape[0] // 4
+
+    def copy(k, i):
+        src = (r0, r1, r2, r3)[i].at[:, pl.ds(pl.multiple_of(k * cols, cols), cols)]
+        return pltpu.make_async_copy(src, right.at[k, pl.ds(i * b, b), :], sems.at[k, i])
+
+    @pl.when(k == 0)
+    def _():
+        for block in range(4):
+            for i in range(4):
+                copy(block, i).start()
+
+    for i in range(4):
+        copy(k, i).wait()
+    grad = contract(left_ref[...], right[k], 0, 0)
     grad = grad.astype(bf16)
     rows = grad.shape[0] // 4
     for a in range(4):
@@ -674,11 +689,12 @@
         grid_spec=pltpu.PrefetchScalarGridSpec(
             num_scalar_prefetch=1,
             grid=(4,),
-            in_specs=[fixed(n, rows)] + [pl.BlockSpec((b, cols // 4), lambda k, s: (0, k))] * 4,
+            in_specs=[fixed(n, rows)] + [ANY] * 4,
             out_specs=[first, first, second, second],
+            scratch_shapes=[pltpu.VMEM((4, n, cols // 4), bf16), pltpu.SemaphoreType.DMA((4, 4))],
         ),
         out_shape=[jax.ShapeDtypeStruct((2, rows // 4, cols // 2), bf16)] * 4,
-        compiler_params=params(11),
+        compiler_params=params(14),
         cost_estimate=cost(1 << 24),
         name=name,
     )(s, left, *rights)
@@ -704,6 +720,119 @@
     )(whole)
 
 
+def place_kernel(write, s_ref, *refs):
+    k = pl.program_id(0)
+    for i in range(8):
+
+        @pl.when(k == i)
+        def _():
+            write(refs[i], refs[8:])
+
+
+def write_rows(piece, outs):
+    outs[0][...] = jnp.concatenate([piece[0], piece[1]], 0).astype(f32)
+
+
+def write_attention(piece, outs):
+    query, key, value, out = outs
+    r, s = query.shape[0], out.shape[0]
+    query[...] = piece[0, :r].astype(f32)
+    key[...] = piece[1, :r, :128].astype(f32)
+    value[...] = piece[1, :r, 128:].astype(f32)
+    sides = [piece[half, r + at * s : r + (at + 1) * s] for half in range(2) for at in range(2)]
+    out[...] = jnp.concatenate(sides, 1).astype(f32)
+
+
+def place_call(s, pieces, write, blocks, name):
+    eighth = lambda k, s: (2 * (s[2] ^ (k % 4)) + (s[1] ^ (k // 4)), 0)
+    return pl.pallas_call(
+        functools.partial(place_kernel, write),
+        grid_spec=pltpu.PrefetchScalarGridSpec(
+            num_scalar_prefetch=1,
+            grid=(8,),
+            in_specs=[fixed(*pieces[0].shape)] * 8,
+            out_specs=[pl.BlockSpec(block, eighth) for block in blocks],
+        ),
+        out_shape=[jax.ShapeDtypeStruct((8 * r, cols), f32) for r, cols in blocks],
+        compiler_params=params(12),
+        cost_estimate=cost(1 << 20),
+        name=name,
+    )(s, *pieces)
+
+
+def grad_attention_kernel(s_ref, n1_ref, low_ref, att_ref, b0, b1, b2, b3, sent_a, keep_a, sent_b, keep_b, whole):
+    j = pl.program_id(0)
+    b = b0.shape[0]
+
+    @pl.when(j == 0)
+    def _():
+        total = None
+        for i, block in enumerate((b0, b1, b2, b3)):
+            part = contract(att_ref[i * b : (i + 1) * b, :], block[...], 0, 0)
+            total = part if total is None else total + part
+        whole[...] = total.astype(bf16)
+
+    qkv = contract(n1_ref[...], low_ref[...], 0, 0).astype(bf16)
+    r = qkv.shape[0] // 2
+    s = whole.shape[0] // 8
+    k = qkv.shape[1] // 2
+    out = whole[pl.ds(pl.multiple_of((s_ref[2] ^ j) * 2 * s, 2 * s), 2 * s), :]
+
+    def joined(at):
+        parts = []
+        for core in range(2):
+            some = out[core * s : (core + 1) * s]
+            parts += [
+                qkv[core * r : (core + 1) * r, at * k : (at + 1) * k],
+                some[:, 2 * at * k : (2 * at + 1) * k],
+                some[:, (2 * at + 1) * k : (2 * at + 2) * k],
+            ]
+        return jnp.concatenate(parts, 0)
+
+    @pl.when(j % 2 == 1)
+    def _():
+        sent_a[0] = joined(0)
+
+    @pl.when(j % 2 == 0)
+    def _():
+        keep_a[0] = joined(0)
+
+    @pl.when(j >= 2)
+    def _():
+        sent_b[0] = joined(1)
+
+    @pl.when(j < 2)
+    def _():
+        keep_b[0] = joined(1)
+
+
+def grad_attention_call(s, n1, low, att, blocks):
+    n, d = n1.shape
+    b = n // 4
+    half = (d // 4 + att.shape[1] // 2, 256)
+    maps = [
+        lambda j, s: (j // 2, 0, 0),
+        lambda j, s: (j // 2, 0, 0),
+        lambda j, s: (jnp.maximum(j - 2, 0), 0, 0),
+        lambda j, s: (jnp.minimum(j, 1), 0, 0),
+    ]
+    return pl.pallas_call(
+        grad_attention_kernel,
+        grid_spec=pltpu.PrefetchScalarGridSpec(
+            num_scalar_prefetch=1,
+            grid=(4,),
+            in_specs=[pl.BlockSpec((n, d // 4), lambda j, s: (0, s[2] ^ j)), fixed(n, low.shape[1]), fixed(n, att.shape[1])]
+            + [fixed(b, d)] * 4,
+            out_specs=[pl.BlockSpec((1,) + half, m) for m in maps],
+            scratch_shapes=[pltpu.VMEM((att.shape[1], d), bf16)],
+        ),
+        out_shape=[jax.ShapeDtypeStruct((2,) + half, bf16)] * 4,
+        compiler_params=params(18),
+        cost_estimate=cost(1 << 24),
+        name="grad_attention",
+    )(s, n1, low, att, *blocks)
+
+
 def permute(x, places, move):
     pairs = []
     for d in range(places):
@@ -738,25 +867,21 @@
     return (d, t) if (d & 1) == (t >> 1) else (d ^ 1, t ^ 2)
 
 
-def gather_row(x, n):
-    over = permute(x, n, flip_z)
-    near = permute(x, n, flip_core)
-    far = permute(over, n, flip_core)
-    return [x, over, near, far]
-
-
-def hop(weights, n, c, e):
-    rows = weights[0].shape[0] // 8
-    mine = [lax.dynamic_slice_in_dim(w, (2 * e + c) * rows, rows, 0) for w in weights]
-    return permute(jnp.concatenate(mine, 1) if len(mine) > 1 else mine[0], n, flip_far)
-
-
-def spread(piece, n, *events):
-    got = [permute(piece, n, lambda d, t, j=j: (d ^ (2 * j), t)) for j in (1, 2, 3)]
-    if events:
-        got = after(got, *events)
-    mine = jnp.concatenate([piece] + got)
-    return mine, permute(mine, n, flip_core)
+def step(*values):
+    return lax.optimization_barrier(values)
+
+
+def eighth(w, c, e):
+    rows = w.shape[0] // 8
+    return lax.dynamic_slice_in_dim(w, (2 * e + c) * rows, rows, 0)
+
+
+def around(piece, n):
+    return [permute(piece, n, lambda d, t, j=j: (d ^ (2 * j), t)) for j in (1, 2, 3)]
+
+
+def across(pieces, n):
+    return [permute(piece, n, flip_core) for piece in pieces]
 
 
 def first_sums(pieces, n):
@@ -784,11 +909,14 @@
     return total
 
 
-def owner_cross(total, n, c):
+def cross_sent(total, c):
     half = total.shape[1] // 2
-    first, second = total[:, :half], total[:, half:]
-    got = permute(jnp.where(c == 0, second, first), n, flip_core)
-    return jnp.where(c == 0, first, got), permute(jnp.where(c == 0, got, second), n, flip_far)
+    return jnp.where(c == 0, total[:, half:], total[:, :half])
+
+
+def cross_got(total, got, c):
+    half = total.shape[1] // 2
+    return jnp.where(c == 0, total[:, :half], got), jnp.where(c == 0, got, total[:, half:])
 
 
 def neighbours(n):
@@ -799,37 +927,9 @@
     return lax.all_gather(mine, "dp", axis_index_groups=neighbours(n))
 
 
-def out_slices(w, n, c, e):
-    rows = w.shape[0] // 8
-    mine = lax.dynamic_slice_in_dim(w, (2 * e + c) * rows, rows, 0)
-    two = jnp.stack([mine, permute(mine, n, flip_z)])
-    return jnp.concatenate([two, permute(two, n, flip_far)])
-
-
-def sum_all(vec, n):
-    bit = 1
-    while bit < n:
-        vec = vec + permute(vec, n, lambda d, t, bit=bit: (d ^ bit, t))
-        bit *= 2
-    for bit in (1, 2):
-        vec = vec + permute(vec, n, lambda d, t, bit=bit: (d, t ^ bit))
-    return vec
-
-
-def join_attention(qkv, out):
-    r, k = qkv.shape[1] // 2, qkv.shape[2]
-    s = out.shape[1] // 2
-    parts = []
-    for half in range(2):
-        some = out[:, half * s : (half + 1) * s]
-        parts += [qkv[:, half * r : (half + 1) * r], some[:, :, :k], some[:, :, k:]]
-    return jnp.concatenate(parts, 1)
-
-
-def widen_out(got):
-    s = got.shape[2] // 2
-    sides = [got[:, half, at * s : (at + 1) * s].reshape(8 * s, -1) for half in range(2) for at in range(2)]
-    return jnp.concatenate(sides, 1).astype(f32)
+def vector_moves(n):
+    bits = [1 << k for k in range(20) if 1 << k < n]
+    return [lambda d, t, bit=bit: (d ^ bit, t) for bit in bits] + [flip_z, flip_far]
 
 
 def local(
@@ -862,16 +962,31 @@
     width = block_input.shape[1]
     s = jnp.stack([shard, c, e]).astype(jnp.int32)
 
+    marks = jnp.concatenate([doc_lengths, pad_mask], 1)
+    mine_out = eighth(w_out, c, e)
+    mine_qkv = jnp.concatenate([eighth(w, c, e) for w in (w_query, w_key, w_value)], 1)
+    mine_gate, mine_up, mine_down = (eighth(w, c, e) for w in (w_gate, w_up, w_down))
     x_own = permute(block_input, n, settle)
-    marks = jnp.concatenate([doc_lengths, pad_mask], 1)
+    qkv_hop = permute(mine_qkv, n, flip_far)
+    out_z = permute(mine_out, n, flip_z)
     marks = jnp.where(home, marks, permute(marks, n, flip_core))
     lengths_row, pad_row = marks[0, : doc_lengths.shape[1]], marks[0, doc_lengths.shape[1] :]
-    out_eighth = out_slices(w_out, n, c, e)
-    out_all = lax.all_gather(out_eighth, "dp", axis_index_groups=neighbours(n))
-    qkv_hop = hop((w_query, w_key, w_value), n, c, e)
-    x_blocks = gather_row(x_own, n)
-    qkv_parts = spread(qkv_hop, n, x_blocks[1])
-    gate_up_hop = hop((after(w_gate, x_blocks[2]), w_up), n, c, e)
+    x_over, x_near = permute(x_own, n, flip_z), permute(x_own, n, flip_core)
+    qkv_hop, out_z, mine_gate, mine_up, mine_down, late_dy = after(
+        [qkv_hop, out_z, mine_gate, mine_up, mine_down, cotangent], x_own
+    )
+    two_out = jnp.stack([mine_out, out_z])
+    out_far = permute(two_out, n, flip_far)
+    qkv_around = around(qkv_hop, n)
+    dy_own = permute(late_dy, n, settle)
+    x_over, x_near = step(x_over, x_near)
+    x_far = permute(x_over, n, flip_core)
+    qkv_around, out_far, mine_gate, mine_up = after([qkv_around, out_far, mine_gate, mine_up], x_over)
+    qkv_mine = [qkv_hop] + qkv_around
+    qkv_other = across(qkv_mine, n)
+    out_all = lax.all_gather(jnp.concatenate([two_out, out_far]), "dp", axis_index_groups=neighbours(n))
+    gate_hop, up_hop = permute(mine_gate, n, flip_far), permute(mine_up, n, flip_far)
+    x_blocks = [x_own, x_over, x_near, x_far]
 
     positions = jnp.arange(seq_len, dtype=jnp.int32)
     doc_starts, cos_half, sin_half = doc_tables(lengths_row, positions, HD)
@@ -887,36 +1002,50 @@
     kgain_pair = jnp.concatenate([key_gain] * 2)[None]
 
     rows_one, pre, qk, values, w_qkv = qkv_call(
-        s, x_blocks, (w_query, w_key, w_value), qkv_parts, norm1_gain[None], after(gains, out_eighth), cos, sin
-    )
-    attended, attended_f, lse = attend_call(s, qk, values, start_col, live_row)
-    att_pieces = gather_row(attended, n)
-    gate_up_parts = spread(after(gate_up_hop, attended), n, att_pieces[1])
-    down_hop = hop((after(w_down, attended),), n, c, e)
-    dy_own = permute(after(cotangent, attended), n, settle)
-    down_hop = after(down_hop, att_pieces[3])
-    dy_own = after(dy_own, att_pieces[3])
-    dy_blocks = gather_row(dy_own, n)
-    down_parts = spread(down_hop, n, dy_blocks[1])
+        s, x_blocks, (w_query, w_key, w_value), qkv_mine + qkv_other, norm1_gain[None], gains, cos, sin
+    )
+    gate_hop, dy_own = after([gate_hop, dy_own], qk)
+    gate_around = around(gate_hop, n)
+    dy_over, dy_near = permute(dy_own, n, flip_z), permute(dy_own, n, flip_core)
+    attended, attended_f, lse = attend_call(s, qk, after(values, gate_hop, dy_own), start_col, live_row)
+
+    att_over, att_near = permute(attended, n, flip_z), permute(attended, n, flip_core)
+    up_hop, mine_down = after([up_hop, mine_down], attended)
+    up_around = around(up_hop, n)
+    down_hop = permute(mine_down, n, flip_far)
+    att_over, att_near = step(att_over, att_near)
+    att_far = permute(att_over, n, flip_core)
+    gate_around, dy_over, dy_near = after([gate_around, dy_over, dy_near], att_over)
+    gate_mine = [gate_hop] + gate_around
+    gate_parts = gate_mine + across(gate_mine, n)
+    dy_far = permute(dy_over, n, flip_core)
+    up_around, down_hop = after([up_around, down_hop], att_far)
+    up_mine = [up_hop] + up_around
+    up_parts = up_mine + across(up_mine, n)
+    down_around = around(down_hop, n)
+    dy_blocks = [dy_own, dy_over, dy_near, dy_far]
     rows_two, hidden, by_gate, by_up, residual, w_out_own = ffn_call(
-        s, x_blocks, att_pieces, out_all, w_gate, w_up, gate_up_parts, after(norm2_gain[None], dy_own, down_hop)
+        s, x_blocks, [attended, att_over, att_near, att_far], out_all, w_gate, gate_parts, w_up, up_parts,
+        after(norm2_gain[None], down_hop),
     )
 
     down = grad_cols_call(s, hidden, dy_blocks, "grad_down")
+    down_mine = [down_hop] + after(down_around, hidden)
+    down_parts = down_mine + across(down_mine, n)
+    down_got = first_sums(down, n)
     gate_grad, up_grad, low2, high2 = ffn_back_call(
-        s, dy_blocks, w_down, down_parts, w_gate, w_up, gate_up_parts, after(by_gate, *down), by_up
-    )
-    high_got = permute(high2, n, flip_core)
-    down_got = first_sums(down, n)
+        s, dy_blocks, w_down, down_parts, w_gate, gate_parts, w_up, up_parts, after(by_gate, *down), by_up
+    )
+    (high_got,) = step(permute(high2, n, flip_core))
     low_half = low2 + high_got
     low_over = permute(low_half[b:], n, flip_z)
-    down = first_add(down, after(down_got, low_half))
-    down_got = second_sums(down, n)
-    gate = grad_rows_call(s, rows_two, after(gate_grad, *down), False, "grad_gate")
+    gate = grad_rows_call(s, rows_two, after(gate_grad, low_half), False, "grad_gate")
     gate_got = first_sums(gate, n)
     up = grad_rows_call(s, rows_two, after(up_grad, *gate), False, "grad_up")
     up_got = first_sums(up, n)
-    grad_n2 = (low_half[:b] + after(low_over, *up)).astype(f32)
+    down = first_add(down, after(down_got, *up))
+    down_got = second_sums(down, n)
+    grad_n2 = (low_half[:b] + after(low_over, *down)).astype(f32)
     inv = lax.rsqrt(jnp.mean(residual * residual, axis=-1, keepdims=True) + epsilon)
     scaled = norm2_gain * grad_n2
     grad_residual = (
@@ -926,80 +1055,115 @@
     )
     grad_norm2 = jnp.sum(grad_n2 * residual * inv, axis=0)
     gb_own = grad_residual.astype(bf16)
-    gb_blocks = gather_row(gb_own, n)
-
-    down = second_add(down, after(down_got, gb_own), n)
-    down_kept, down_got = owner_cross(down, n, c)
-    ffn_low, ffn_high = ffn_out_call(s, w_down, down_parts, after(hidden, down))
-    ffn_got = permute(ffn_high, n, flip_core)
+    gb_over, gb_near = permute(gb_own, n, flip_z), permute(gb_own, n, flip_core)
+    ffn_low, ffn_high = ffn_out_call(s, w_down, down_parts, after(hidden, gb_own))
     gate = first_add(gate, after(gate_got, ffn_low))
     gate_got = second_sums(gate, n)
-    up = first_add(up, after(up_got, gb_blocks[1], *gate))
+    ffn_got = permute(ffn_high, n, flip_core)
+    gb_over, gb_near = step(*after([gb_over, gb_near], *gate))
+    ffn_got = after(ffn_got, gb_over)
+    gb_far = permute(gb_over, n, flip_core)
+    up = first_add(up, after(up_got, gb_over))
     up_got = second_sums(up, n)
-    ffn_half = ffn_low + after(ffn_got, *up)
+    down = second_add(down, after(down_got, gb_over, *up), n)
+    gate = second_add(gate, after(gate_got, down), n)
+    ffn_half = ffn_low + ffn_got
+    gb_far, down_got, gate_got = step(
+        gb_far, permute(cross_sent(down, c), n, flip_core), permute(cross_sent(gate, c), n, flip_core)
+    )
+    down_kept, down_sent = cross_got(down, down_got, c)
+    gate_kept, gate_sent = cross_got(gate, gate_got, c)
+    down_got, gate_got = permute(down_sent, n, flip_far), permute(gate_sent, n, flip_far)
     ffn_over = permute(ffn_half[b:], n, flip_z)
-    down_mine = down_kept + after(down_got, gb_blocks[3], ffn_half)
+    gb_blocks = [gb_own, gb_over, gb_near, gb_far]
+
+    low, gain_terms, low1, high1 = attend_back_call(
+        s, qk, after(values, ffn_half, gate_sent, down_sent), pre, qgain_pair, kgain_pair, cos, sin, start_row, live_col,
+        attended_f, lse, w_out_own, w_qkv, gb_blocks,
+    )
+    up = second_add(up, after(up_got, low), n)
+    high_got, up_got = step(permute(high1, n, flip_core), permute(cross_sent(up, c), n, flip_core))
+    low_half = low1 + high_got
+    low_over = permute(low_half[b:], n, flip_z)
+    up_kept, up_sent = cross_got(up, up_got, c)
+    up_got = permute(up_sent, n, flip_far)
+    down_mine = down_kept + after(down_got, low_half)
     down_all = whole_grad(down_mine, n)
-    gate = second_add(gate, after(gate_got, down_mine), n)
-    gate_kept, gate_got = owner_cross(gate, n, c)
-
-    low, gain_terms, low1, high1 = attend_back_call(
-        s, qk, after(values, gate_kept, ffn_half), pre, qgain_pair, kgain_pair, cos, sin, start_row, live_col, attended_f,
-        lse, w_out_own, w_qkv, gb_blocks,
-    )
-    high_got = permute(high1, n, flip_core)
-    gate_mine = gate_kept + after(gate_got, high_got)
-    gate_all = whole_grad(gate_mine, n)
-    low_half = low1 + after(high_got, gate_mine)
-    low_over = permute(low_half[b:], n, flip_z)
-    up = second_add(up, after(up_got, low_half), n)
-    up_kept, up_got = owner_cross(up, n, c)
-    qkv = grad_rows_call(s, rows_one, after(low, up_kept), True, "grad_qkv")
-    out = grad_cols_call(s, after(attended, *qkv), gb_blocks, "grad_out")
-    att = [join_attention(a, o) for a, o in zip(qkv, out)]
+    att = grad_attention_call(s, rows_one, after(low, down_mine, up_sent), attended, gb_blocks)
     att_got = first_sums(att, n)
     block_output = residual + (ffn_half[:b] + after(ffn_over, *att)).astype(f32)
-    settled_output = permute(block_output.astype(bf16), n, settle)
-
-    grad_n1 = (low_half[:b] + after(low_over, block_output)).astype(f32)
+    gate_mine = gate_kept + after(gate_got, *att)
+    low_over = after(low_over, gate_mine, block_output)
+    grad_n1 = (low_half[:b] + low_over).astype(f32)
+    gate_around = around(gate_mine, n)
+    att = first_add(att, after(att_got, low_over))
+    att_got = second_sums(att, n)
     x_f = x_own.astype(f32)
     inv = lax.rsqrt(jnp.mean(x_f * x_f, axis=-1, keepdims=True) + epsilon)
-    scaled = norm1_gain * grad_n1
+    scaled = norm1_gain * after(grad_n1, *att)
     input_grad = (
         grad_residual
         + inv * scaled
         - x_f * (inv * inv * inv) * jnp.mean(scaled * x_f, axis=-1, keepdims=True)
     )
     grad_norm1 = jnp.sum(grad_n1 * x_f * inv, axis=0)
-    settled_grad = permute(input_grad.astype(bf16), n, settle)
-    up_mine = up_kept + after(up_got, input_grad)
-    up_all = whole_grad(up_mine, n)
-    att = first_add(att, after(att_got, up_mine))
-    att_got = second_sums(att, n)
     head_terms = gain_terms[:, :HD] + gain_terms[:, HD:]
-    vec = jnp.concatenate([grad_norm1, grad_norm2, head_terms[0] + head_terms[1], head_terms[2]])
-    vec = sum_all(after(vec, *att)[None], n)[0]
-    att = second_add(att, after(att_got, vec), n)
-    att_kept, att_got = owner_cross(att, n, c)
-    grad_down = widen_call(after(down_all, att_kept), True, "widen_down")
-    grad_gate = widen_call(after(gate_all, grad_down), False, "widen_gate")
-    att_mine = att_kept + after(att_got, grad_down)
-    att_all = whole_grad(att_mine, n)
-    block_output = jnp.where(home, block_output, after(settled_output, grad_gate).astype(f32))
-    input_grad = jnp.where(home, input_grad, after(settled_grad, grad_gate).astype(f32))
-    grad_up = widen_call(after(up_all, grad_gate), False, "widen_up")
-    att_all = after(att_all, grad_up)
-    eighth = wq // 2
-    grad_query = att_all[:, 0, :eighth].astype(f32).reshape(width, wq)
-    grad_kv = att_all[:, 1, :eighth].astype(f32).reshape(width, wq)
-    grad_out = widen_out(att_all[:, :, eighth:])
+    vec = jnp.concatenate([grad_norm1, grad_norm2, head_terms[0] + head_terms[1], head_terms[2]])[None]
+    moves = vector_moves(n)
+    vec_got = permute(vec, n, moves[0])
+    att = second_add(att, after(att_got, input_grad, vec), n)
+    att_got = permute(cross_sent(att, c), n, flip_core)
+    up_mine = up_kept + after(up_got, att)
+    up_around = around(up_mine, n)
+    att_got, vec_got = step(after(att_got, up_mine), vec_got)
+    att_kept, att_sent = cross_got(att, att_got, c)
+    att_got = permute(att_sent, n, flip_far)
+    vec = vec + vec_got
+    vec_got = permute(after(vec, att_sent), n, moves[1])
+    late_output, late_grad, gate_around = after([block_output, input_grad, gate_around], att_sent)
+    settled_output = permute(late_output.astype(bf16), n, settle)
+    settled_grad = permute(late_grad.astype(bf16), n, settle)
+    gate_across = across([gate_mine] + gate_around, n)
+    att_got, vec_got = step(*after([att_got, vec_got], gate_around))
+    att_mine = att_kept + att_got
+    att_around = around(att_mine, n)
+    vec = vec + vec_got
+    vec_got = permute(after(vec, att_mine), n, moves[2])
+    (grad_gate,) = place_call(
+        s, [gate_mine] + gate_around + after(gate_across, att_mine), write_rows, [(width // 8, w_gate.shape[1])], "place_gate"
+    )
+    up_around = after(up_around, grad_gate)
+    up_across = across([up_mine] + up_around, n)
+    att_around, vec_got = after([att_around, vec_got], up_around)
+    att_across = across([att_mine] + att_around, n)
+    vec = vec + vec_got
+    vec_got = permute(vec, n, moves[3])
+    (grad_up,) = place_call(
+        s, [up_mine] + up_around + after(up_across, vec), write_rows, [(width // 8, w_gate.shape[1])], "place_up"
+    )
+    vec = vec + after(vec_got, grad_up)
+    vec_got = permute(vec, n, moves[4])
+    grad_query, grad_key, grad_value, grad_out = place_call(
+        s,
+        [att_mine] + att_around + after(att_across, vec),
+        write_attention,
+        [(width // 8, wq), (width // 8, wk), (width // 8, wk), (w_out.shape[0] // 8, width)],
+        "place_attention",
+    )
+    vec = vec + after(vec_got, grad_query)
+    for move in moves[5:]:
+        vec = vec + permute(vec, n, move)
+    vec = vec[0]
+    grad_down = widen_call(after(down_all, vec), True, "widen_down")
+    block_output = jnp.where(home, block_output, after(settled_output, grad_down).astype(f32))
+    input_grad = jnp.where(home, input_grad, after(settled_grad, grad_down).astype(f32))
     return (
         block_output,
         input_grad,
         vec[:width],
         grad_query,
-        grad_kv[:, :wk],
-        grad_kv[:, wk:],
+        grad_key,
+        grad_value,
         vec[2 * width : 2 * width + HD],
         vec[2 * width + HD :],
         grad_out,

time: 507 us -> 423 us (0.83)
  waiting for transfers between devices: 207 us -> 118 us
  starting transfers between devices: 65 us -> 112 us
  local copies, waits for them, and re-layouts: 74.4 us -> 34.8 us
  Pallas kernels: 94.6 us -> 107 us
  other arithmetic: 41.6 us -> 30.2 us
    ppermute x69 -> x107, waiting for transfers between devices: 207 us -> 117 us  [permute(): return lax.ppermute(x, AX, pairs)]
    ppermute x69 -> x107, starting transfers between devices: 64.8 us -> 112 us  [permute(): return lax.ppermute(x, AX, pairs)]
    unnamed x221 -> x236, local copies, waits for them, and re-layouts: 59.3 us -> 26.1 us
    pallas_call x0 -> x4, Pallas kernels: none -> 16.4 us  [the longest x3 12.6 us: place_call(): pl.pallas_call(functools.partial(place_kernel, write), grid_spec=pltpu.Pr...]
    pallas_call x3 -> x1, Pallas kernels: 10.8 us -> 3.6 us  [widen_call(): pl.pallas_call(functools.partial(widen_kernel, side), grid=(8,), in_specs...]
    pallas_call x2 -> x1, Pallas kernels: 10.6 us -> 6.73 us  [grad_cols_call(): pl.pallas_call(grad_cols_kernel, grid_spec=pltpu.PrefetchScalarGridSpec(n...]
    pallas_call x3 -> x2, Pallas kernels: 12.4 us -> 9.41 us  [grad_rows_call(): pl.pallas_call(functools.partial(grad_rows_kernel, by_cols), grid_spec=pl...]
  transfers between devices with their start and end apart: 74 -> 109, of which waited for: 31 -> 31; matrix products, arithmetic and copies ran while one was open for 12% -> 9% of each run, Pallas kernels for 16% -> 21%
where the time goes in v2:
time: 423 us; the launch traced here: 417 us
  waiting for transfers between devices  118 us (28%)
  starting transfers between devices  112 us (26%)
  Pallas kernels  107 us (25%)
  local copies, waits for them, and re-layouts  34.8 us (8%)
  other arithmetic  30.2 us (7%)
  between operations  15.9 us (4%)
    ppermute x107, waiting for transfers between devices, permute(): return lax.ppermute(x, AX, pairs)  117 us
    ppermute x107, starting transfers between devices, permute(): return lax.ppermute(x, AX, pairs)  112 us
    unnamed x236, local copies, waits for them, and re-layouts  26.1 us
    pallas_call x1, Pallas kernels, attend_back_call(): pl.pallas_call(attend_back_kernel, grid_spec=pltpu.PrefetchScalarGridSpec...  19.3 us
    pallas_call x1, Pallas kernels, ffn_back_call(): pl.pallas_call(ffn_back_kernel, grid_spec=pltpu.PrefetchScalarGridSpec(nu...  17.5 us
    pallas_call x1, Pallas kernels, ffn_call(): pl.pallas_call(ffn_kernel, grid_spec=pltpu.PrefetchScalarGridSpec(num_sca...  16.6 us
    pallas_call x3, Pallas kernels, place_call(): pl.pallas_call(functools.partial(place_kernel, write), grid_spec=pltpu.Pr...  12.6 us
    pallas_call x2, Pallas kernels, grad_rows_call(): pl.pallas_call(functools.partial(grad_rows_kernel, by_cols), grid_spec=pl...  9.41 us
  transfers between devices with their start and end apart: 109, of which 31 were waited for; matrix products, arithmetic and copies ran while one was open for 9% of the time, Pallas kernels for 21%

profile of v2, /device:TPU:0, one launch (start us, length us, event | category | flops | bytes accessed | tf_op | source)
XLA Modules:
  0.0 417.4 jit_solution(16209226031776707367)
XLA Ops:
  7.3 1.8 collective-permute-start
  10.8 4.3 %collective-permute-start.4 = (bf16[128,512]{1,0:T(8,128)(2,1)S(1)}, bf16[128,512]{1,0:T(8,128)(2,1)S(1)}, u32[]{:S(2)}, u32[]{:S(2)}) collective-permute-start(bf16[128,512]{1,0:T(8,128)(2,1)S(1)} %pad_maximum_fusion.7), channel_id=1, source_target_pairs={{0,2},{1,3},{2,0},{3,1},{4,6},{5,7},{6,4},{7,5},{8,10},{9,11},{10,... | collective-permute-start | bytes 393224 | tf_op jit(solution)/shard_map/ppermute | solution.py:843
  15.1 1.6 collective-permute-start.5
  17.2 13.8 %collective-permute-start.2 = (bf16[256,1024]{1,0:T(8,128)(2,1)S(1)}, bf16[256,1024]{1,0:T(8,128)(2,1)S(1)}, u32[]{:S(2)}, u32[]{:S(2)}) collective-permute-start(bf16[256,1024]{1,0:T(8,128)(2,1)S(1)} %collective-permute-done.refs_0_), channel_id=1, source_target_pairs={{0,4},{1,5},{2,6},{3,7},{4,0},{5,1},{6,2},{7,3},{8,12},{9,13},{10,... | collective-permute-start | bytes 1572872 | tf_op jit(solution)/shard_map/ppermute | solution.py:843
  31.0 1.9 constant_dynamic-slice_fusion.1
  32.9 1.7 constant_dynamic-slice_fusion
  34.6 3.6 collective-permute-start.9
  41.7 3.2 collective-permute-done.9
  44.9 2.9 collective-permute-done.7.refs_9_
  50.6 1.7 collective-permute-start.16
  53.8 1.9 fusion.20
  56.2 1.8 collective-permute-start.15
  68.7 7.7 %qkv.1 = (bf16[1024,1024]{1,0:T(8,128)(2,1)S(1)}, f32[1024,384]{1,0:T(8,128)S(1)}, bf16[1024,384]{1,0:T(8,128)(2,1)S(1)}, bf16[1024,128]{1,0:T(8,128)(2,1)S(1)}, bf16[1024,512]{1,0:T(8,128)(2,1)S(1)}) custom-call(s32[3]{0:T(128)S(1)} %pad_add_fusion.1.s_ref, bf16[256,1024]{1,0:T(8,128)(2,1)S(1)} %collective-permute-done.refs_0_, ...), custom_call_target="tpu_custom_call" | custom-call | flops 16777216 | bytes 65536 | tf_op jit(solution)/shard_map/qkv/pallas_call | solution.py:147
  77.7 12.5 %collective-permute-done.15.refs_10_.refs_14_ = bf16[128,1152]{1,0:T(8,128)(2,1)S(1)} collective-permute-done((bf16[128,1152]{1,0:T(8,128)(2,1)}, bf16[128,1152]{1,0:T(8,128)(2,1)S(1)}, u32[]{:S(2)}, u32[]{:S(2)}) %collective-permute-start.15) | collective-permute-done | bytes 294944 | tf_op jit(solution)/shard_map/ppermute | solution.py:843
  90.5 5.4 %attend.1 = (bf16[1024,256]{1,0:T(8,128)(2,1)S(1)}, f32[1024,256]{1,0:T(8,128)S(1)}, f32[2,4,1,512]{3,2,1,0:T(1,128)S(1)}) custom-call(s32[3]{0:T(128)S(1)} %pad_add_fusion.1.s_ref, bf16[1024,384]{1,0:T(8,128)(2,1)S(1)} %get-tuple-element.176.q_ref.k_ref, bf16[1024,384]{1,0:T(8,128)(2,1)S(1)} %get-tuple-element.176.q_ref.k_ref, ...), custom_call_target="tpu_custom_call" | custom-call | flops 16777216 | bytes 65536 | tf_op jit(solution)/shard_map/attend/pallas_call | solution.py:233
  100.5 6.3 %collective-permute-done.30.refs_20_.refs_24_ = bf16[128,1152]{1,0:T(8,128)(2,1)S(1)} collective-permute-done((bf16[128,1152]{1,0:T(8,128)(2,1)S(1)}, bf16[128,1152]{1,0:T(8,128)(2,1)S(1)}, u32[]{:S(2)}, u32[]{:S(2)}) %collective-permute-start.30) | collective-permute-done | bytes 294944 | tf_op jit(solution)/shard_map/ppermute | solution.py:843
  106.8 2.0 collective-permute-start.23
  108.8 1.6 collective-permute-start.21
  112.6 11.9 %collective-permute-done.21.refs_12_.refs_16_ = bf16[128,1152]{1,0:T(8,128)(2,1)S(1)} collective-permute-done((bf16[128,1152]{1,0:T(8,128)(2,1)S(1)}, bf16[128,1152]{1,0:T(8,128)(2,1)S(1)}, u32[]{:S(2)}, u32[]{:S(2)}) %collective-permute-start.21) | collective-permute-done | bytes 294944 | tf_op jit(solution)/shard_map/ppermute | solution.py:843
  124.6 1.8 collective-permute-start.32
  126.3 2.2 collective-permute-start.33
  129.9 4.2 collective-permute-done.32.refs_22_.refs_26_
  134.0 7.2 %collective-permute-done.33.refs_5_.refs_0_ = bf16[144,1024]{1,0:T(8,128)(2,1)} collective-permute-done((bf16[144,1024]{1,0:T(8,128)(2,1)S(1)}, bf16[144,1024]{1,0:T(8,128)(2,1)}, u32[]{:S(2)}, u32[]{:S(2)}) %collective-permute-start.33) | collective-permute-done | bytes 294944 | tf_op jit(solution)/shard_map/ppermute | solution.py:843
  148.1 16.6 %ffn.1 = (bf16[1024,1024]{1,0:T(8,128)(2,1)}, bf16[1024,1152]{1,0:T(8,128)(2,1)}, bf16[1024,1152]{1,0:T(8,128)(2,1)}, bf16[1024,1152]{1,0:T(8,128)(2,1)}, f32[25...) custom-call(s32[3]{0:T(128)} %copy-done.63, bf16[256,1024]{1,0:T(8,128)(2,1)} %copy-done.2, bf16[256,1024]{1,0:T(8,128)(2,1)} %copy-done.30, ...), custom_call_target="tpu_custom_call" | custom-call | flops 16777216 | bytes 65536 | tf_op jit(solution)/shard_map/ffn/pallas_call | solution.py:440
  165.6 1.7 copy-done.5
  167.3 6.7 %grad_down.1 = (bf16[2,288,512]{2,1,0:T(8,128)(2,1)}, bf16[2,288,512]{2,1,0:T(8,128)(2,1)S(1)}, bf16[2,288,512]{2,1,0:T(8,128)(2,1)}, bf16[2,288,512]{2,1,0:T(8,128)(2,1)S(1)}) custom-call(s32[3]{0:T(128)S(1)} %copy-done.64, bf16[1024,1152]{1,0:T(8,128)(2,1)S(1)} %copy-done.5, bf16[256,1024]{1,0:T(8,128)(2,1)S(1)} %collective-permute-done.16.r0.refs_0_, ...), custom_call_target="tpu_custom_call" | custom-call | flops 16777216 | bytes 65536 | tf_op jit(solution)/shard_map/grad_down/pallas_call | solution.py:687
  176.6 17.5 %ffn_back.1 = (bf16[1024,1152]{1,0:T(8,128)(2,1)}, bf16[1024,1152]{1,0:T(8,128)(2,1)}, bf16[512,1024]{1,0:T(8,128)(2,1)}, bf16[512,1024]{1,0:T(8,128)(2,1)}) custom-call(s32[3]{0:T(128)} %copy-done.63, bf16[256,1024]{1,0:T(8,128)(2,1)} %copy-done.8, bf16[256,1024]{1,0:T(8,128)(2,1)} %copy-done.23, bf16[256,1024]{1,0:T(8,128)(2,1)} %copy-done.24, ...), custom_call_target="tpu_custom_call" | custom-call | flops 16777216 | bytes 65536 | tf_op jit(solution)/shard_map/ffn_back/pallas_call | solution.py:515
  197.2 2.1 add.236
  200.0 4.7 %grad_gate.1 = (bf16[2,128,1152]{2,1,0:T(8,128)(2,1)S(1)}, bf16[2,128,1152]{2,1,0:T(8,128)(2,1)S(1)}, bf16[2,128,1152]{2,1,0:T(8,128)(2,1)S(1)}, bf16[2,128,1152]{2,1,0:T(8,128)(2,1)S(1)}) custom-call(s32[3]{0:T(128)S(1)} %copy-done.65, bf16[1024,1024]{1,0:T(8,128)(2,1)S(1)} %copy-done.7, bf16[1024,1152]{1,0:T(8,128)(2,1)S(1)} %copy-done.16), custom_call_target="tpu_custom_call" | custom-call | flops 16777216 | bytes 65536 | tf_op jit(solution)/shard_map/grad_gate/pallas_call | solution.py:626
  205.4 1.5 collective-permute-start.54
  207.0 4.7 %grad_up.1 = (bf16[2,128,1152]{2,1,0:T(8,128)(2,1)S(1)}, bf16[2,128,1152]{2,1,0:T(8,128)(2,1)S(1)}, bf16[2,128,1152]{2,1,0:T(8,128)(2,1)S(1)}, bf16[2,128,1152]{2,1,0:T(8,128)(2,1)S(1)}) custom-call(s32[3]{0:T(128)S(1)} %copy-done.65, bf16[1024,1024]{1,0:T(8,128)(2,1)S(1)} %copy-done.7, bf16[1024,1152]{1,0:T(8,128)(2,1)S(1)} %copy-done.15), custom_call_target="tpu_custom_call" | custom-call | flops 16777216 | bytes 65536 | tf_op jit(solution)/shard_map/grad_up/pallas_call | solution.py:626
  217.6 4.5 %ffn_out.1 = (bf16[512,1024]{1,0:T(8,128)(2,1)S(1)}, bf16[512,1024]{1,0:T(8,128)(2,1)S(1)}) custom-call(s32[3]{0:T(128)S(1)} %copy-done.65, bf16[1152,1024]{1,0:T(8,128)(2,1)S(1)} %copy-done.4, bf16[144,1024]{1,0:T(8,128)(2,1)} %collective-permute-done.33.refs_5_.refs_0_, bf16[144,1024]{1,0:T(8,128)(2,1)} %collective-permute-done.38.refs_6_.refs_1_, ...), custom_call_target="tpu_custom_call" | custom-call | flops 16777216 | bytes 65536 | tf_op jit(solution)/shard_map/ffn_out/pallas_call | solution.py:569
  229.0 4.6 %collective-permute-done.63 = bf16[128,1152]{1,0:T(8,128)(2,1)S(1)} collective-permute-done((bf16[128,1152]{1,0:T(8,128)(2,1)S(1)}, bf16[128,1152]{1,0:T(8,128)(2,1)S(1)}, u32[]{:S(2)}, u32[]{:S(2)}) %collective-permute-start.63) | collective-permute-done | bytes 294944 | tf_op jit(solution)/shard_map/ppermute | solution.py:843
  234.9 9.6 %collective-permute-done.51.b1 = bf16[256,1024]{1,0:T(8,128)(2,1)S(1)} collective-permute-done((bf16[256,1024]{1,0:T(8,128)(2,1)S(1)}, bf16[256,1024]{1,0:T(8,128)(2,1)S(1)}, u32[]{:S(2)}, u32[]{:S(2)}) %collective-permute-start.51) | collective-permute-done | bytes 524320 | tf_op jit(solution)/shard_map/ppermute | solution.py:843
  246.9 3.6 collective-permute-done.58
  252.9 1.7 collective-permute-start.67
  256.0 2.5 collective-permute-start.55
  259.4 2.9 collective-permute-start.71
  262.6 19.3 %attend_back.1 = (bf16[1024,512]{1,0:T(8,128)(2,1)S(1)}, f32[8,128]{1,0:T(8,128)S(1)}, bf16[512,1024]{1,0:T(8,128)(2,1)S(1)}, bf16[512,1024]{1,0:T(8,128)(2,1)S(1)}) custom-call(s32[3]{0:T(128)S(1)} %copy-done.65, bf16[1024,384]{1,0:T(8,128)(2,1)S(1)} %get-tuple-element.176.q_ref.k_ref, bf16[1024,384]{1,0:T(8,128)(2,1)S(1)} %get-tuple-element.176.q_ref.k_ref, ...), custom_call_target="tpu_custom_call" | custom-call | flops 16777216 | bytes 65536 | tf_op jit(solution)/shard_map/attend_back/pallas_call | solution.py:354
  282.9 2.3 collective-permute-done.69
  294.0 3.9 grad_attention.1
  299.9 2.0 collective-permute-start.70
  305.9 7.4 %collective-permute-done.70 = bf16[256,1024]{1,0:T(8,128)(2,1)S(1)} collective-permute-done((bf16[256,1024]{1,0:T(8,128)(2,1)S(1)}, bf16[256,1024]{1,0:T(8,128)(2,1)S(1)}, u32[]{:S(2)}, u32[]{:S(2)}) %collective-permute-start.70) | collective-permute-done | bytes 524320 | tf_op jit(solution)/shard_map/ppermute | solution.py:843
  317.0 1.7 collective-permute-start.77
  319.3 1.9 fusion.9
  321.2 11.1 %collective-permute-done.78 = bf16[384,256]{1,0:T(8,128)(2,1)} collective-permute-done((bf16[384,256]{1,0:T(8,128)(2,1)}, bf16[384,256]{1,0:T(8,128)(2,1)}, u32[]{:S(2)}, u32[]{:S(2)}) %collective-permute-start.78) | collective-permute-done | bytes 196640 | tf_op jit(solution)/shard_map/ppermute | solution.py:843
  338.6 2.4 collective-permute-start.84
  342.5 3.2 collective-permute-done.85
  345.8 4.5 %collective-permute-done.84 = bf16[2,192,256]{2,1,0:T(8,128)(2,1)S(1)} collective-permute-done((bf16[2,192,256]{2,1,0:T(8,128)(2,1)S(1)}, bf16[2,192,256]{2,1,0:T(8,128)(2,1)S(1)}, u32[]{:S(2)}, u32[]{:S(2)}) %collective-permute-start.84) | collective-permute-done | bytes 196640 | tf_op jit(solution)/shard_map/ppermute | solution.py:843
  352.2 1.6 collective-permute-start.86
  355.9 4.3 %place_gate.1 = f32[1024,1152]{1,0:T(8,128)} custom-call(s32[3]{0:T(128)S(1)} %copy-done.65, bf16[2,64,1152]{2,1,0:T(8,128)(2,1)S(1)} %select_add_fusion.1.refs_0_, bf16[2,64,1152]{2,1,0:T(8,128)(2,1)S(1)} %collective-permute-done.74.refs_1_, bf16[2,64,1152]{2,1,0:T(8,128)(2,1)S(1)} %collective-permute-done.75.refs_2_, ...), custom_call_target="tpu_custom_call" | custom-call | flops 1048576 | bytes 65536 | tf_op jit(solution)/shard_map/place_gate/pallas_call | solution.py:748
  361.0 2.3 collective-permute-done.89
  365.1 6.4 %collective-permute-done.88.refs_3_ = bf16[2,192,256]{2,1,0:T(8,128)(2,1)S(1)} collective-permute-done((bf16[2,192,256]{2,1,0:T(8,128)(2,1)S(1)}, bf16[2,192,256]{2,1,0:T(8,128)(2,1)S(1)}, u32[]{:S(2)}, u32[]{:S(2)}) %collective-permute-start.88) | collective-permute-done | bytes 196640 | tf_op jit(solution)/shard_map/ppermute | solution.py:843
  371.5 1.6 collective-permute-start.97
  373.1 2.1 collective-permute-done.97
  377.4 4.3 %place_up.1 = f32[1024,1152]{1,0:T(8,128)} custom-call(s32[3]{0:T(128)S(1)} %copy-done.65, bf16[2,64,1152]{2,1,0:T(8,128)(2,1)S(1)} %select_add_fusion.refs_0_, bf16[2,64,1152]{2,1,0:T(8,128)(2,1)S(1)} %collective-permute-done.90.refs_1_, bf16[2,64,1152]{2,1,0:T(8,128)(2,1)S(1)} %collective-permute-done.91.refs_2_, ...), custom_call_target="tpu_custom_call" | custom-call | flops 1048576 | bytes 65536 | tf_op jit(solution)/shard_map/place_up/pallas_call | solution.py:748
  381.7 3.5 collective-permute-start.102
  386.1 5.4 %collective-permute-start.82 = (bf16[256,1024]{1,0:T(8,128)(2,1)}, bf16[256,1024]{1,0:T(8,128)(2,1)}, u32[]{:S(2)}, u32[]{:S(2)}) collective-permute-start(bf16[256,1024]{1,0:T(8,128)(2,1)} %convert_element_type.44), channel_id=1, source_target_pairs={{0,0},{1,1},{2,4},{3,5},{4,2},{5,3},{6,6},{7,7},{8,8},{9,9},{10,12... | collective-permute-start | bytes 1572872 | tf_op jit(solution)/shard_map/ppermute | solution.py:843
  391.5 4.0 place_attention.1
  395.4 4.1 collective-permute-done.102
  400.8 1.7 copy-done.14
  402.4 3.6 widen_down.1
  406.0 2.1 convert_select_fusion
  408.2 2.1 convert_select_fusion.1
  (498 shorter events, 104.6 us)
Async XLA Ops:
  7.2 140.8 %all-gather.5.cloned.1.call-start = ((), (), s32[]{:S(2)}) async-start(), calls=%async_computation | async-start | bytes 2359296 | tf_op jit(solution)/shard_map/all_gather | solution.py:987
  10.8 23.8 %collective-permute-start.4 = (bf16[128,512]{1,0:T(8,128)(2,1)S(1)}, bf16[128,512]{1,0:T(8,128)(2,1)S(1)}, u32[]{:S(2)}, u32[]{:S(2)}) collective-permute-start(bf16[128,512]{1,0:T(8,128)(2,1)S(1)} %pad_maximum_fusion.7), channel_id=1, source_target_pairs={{0,2},{1,3},{2,0},{3,1},{4,6},{5,7},{6,4},{7,5},{8,10},{9,11},{10,... | collective-permute-start | bytes 393224 | tf_op jit(solution)/shard_map/ppermute | solution.py:843
  15.1 19.5 %collective-permute-start.5 = (bf16[32,1024]{1,0:T(8,128)(2,1)S(1)}, bf16[32,1024]{1,0:T(8,128)(2,1)S(1)}, u32[]{:S(2)}, u32[]{:S(2)}) collective-permute-start(bf16[32,1024]{1,0:T(8,128)(2,1)S(1)} %constant_dynamic-slice_fusion.3), channel_id=1, source_target_pairs={{0,1},{1,0},{2,3},{3,2},{4,5},{5,4},{6,7},{7,6},{8,9},{9,8},{10,11... | collective-permute-start | bytes 196616 | tf_op jit(solution)/shard_map/ppermute | solution.py:843
  16.8 24.4 %collective-permute-start.1 = (bf16[256,1024]{1,0:T(8,128)(2,1)S(1)}, bf16[256,1024]{1,0:T(8,128)(2,1)S(1)}, u32[]{:S(2)}, u32[]{:S(2)}) collective-permute-start(bf16[256,1024]{1,0:T(8,128)(2,1)S(1)} %collective-permute-done.refs_0_), channel_id=1, source_target_pairs={{0,1},{1,0},{2,3},{3,2},{4,5},{5,4},{6,7},{7,6},{8,9},{9,8},{10,11... | collective-permute-start | bytes 1572872 | tf_op jit(solution)/shard_map/ppermute | solution.py:843
  17.2 24.5 %collective-permute-start.2 = (bf16[256,1024]{1,0:T(8,128)(2,1)S(1)}, bf16[256,1024]{1,0:T(8,128)(2,1)S(1)}, u32[]{:S(2)}, u32[]{:S(2)}) collective-permute-start(bf16[256,1024]{1,0:T(8,128)(2,1)S(1)} %collective-permute-done.refs_0_), channel_id=1, source_target_pairs={{0,4},{1,5},{2,6},{3,7},{4,0},{5,1},{6,2},{7,3},{8,12},{9,13},{10,... | collective-permute-start | bytes 1572872 | tf_op jit(solution)/shard_map/ppermute | solution.py:843
  48.6 352.1 %all-gather.7.cloned.1.call-start = ((), (), s32[]{:S(2)}) async-start(), calls=%async_computation.1 | async-start | bytes 2654208 | tf_op jit(solution)/shard_map/all_gather | solution.py:927
  50.6 27.1 %collective-permute-start.16 = (bf16[256,1024]{1,0:T(8,128)(2,1)}, bf16[256,1024]{1,0:T(8,128)(2,1)S(1)}, u32[]{:S(2)}, u32[]{:S(2)}) collective-permute-start(bf16[256,1024]{1,0:T(8,128)(2,1)} %param.29), channel_id=1, source_target_pairs={{0,0},{1,1},{2,4},{3,5},{4,2},{5,3},{6,6},{7,7},{8,8},{9,9},{10,12... | collective-permute-start | bytes 1572872 | tf_op jit(solution)/shard_map/ppermute | solution.py:843
  56.2 34.0 %collective-permute-start.15 = (bf16[128,1152]{1,0:T(8,128)(2,1)}, bf16[128,1152]{1,0:T(8,128)(2,1)S(1)}, u32[]{:S(2)}, u32[]{:S(2)}) collective-permute-start(bf16[128,1152]{1,0:T(8,128)(2,1)} %get-tuple-element.178), channel_id=1, source_target_pairs={{0,2},{1,3},{2,0},{3,1},{4,6},{5,7},{6,4},{7,5},{8,10},{9,11},{10,... | collective-permute-start | bytes 884744 | tf_op jit(solution)/shard_map/ppermute | solution.py:843
  58.1 38.8 %collective-permute-start.29 = (bf16[128,1152]{1,0:T(8,128)(2,1)}, bf16[128,1152]{1,0:T(8,128)(2,1)S(1)}, u32[]{:S(2)}, u32[]{:S(2)}) collective-permute-start(bf16[128,1152]{1,0:T(8,128)(2,1)} %get-tuple-element.190), channel_id=1, source_target_pairs={{0,2},{1,3},{2,0},{3,1},{4,6},{5,7},{6,4},{7,5},{8,10},{9,11},{10,... | collective-permute-start | bytes 884744 | tf_op jit(solution)/shard_map/ppermute | solution.py:843
  96.9 11.9 %collective-permute-start.17 = (bf16[1024,256]{1,0:T(8,128)(2,1)S(1)}, bf16[1024,256]{1,0:T(8,128)(2,1)S(1)}, u32[]{:S(2)}, u32[]{:S(2)}) collective-permute-start(bf16[1024,256]{1,0:T(8,128)(2,1)S(1)} %get-tuple-element.183.refs_4_.att_ref), channel_id=1, source_target_pairs={{0,1},{1,0},{2,3},{3,2},{4,5},{5,4},{6,7},{7,6},{8,9},{9,8},{10,11... | collective-permute-start | bytes 1572872 | tf_op jit(solution)/shard_map/ppermute | solution.py:843
  96.9 13.5 %collective-permute-start.18 = (bf16[1024,256]{1,0:T(8,128)(2,1)S(1)}, bf16[1024,256]{1,0:T(8,128)(2,1)}, u32[]{:S(2)}, u32[]{:S(2)}) collective-permute-start(bf16[1024,256]{1,0:T(8,128)(2,1)S(1)} %get-tuple-element.183.refs_4_.att_ref), channel_id=1, source_target_pairs={{0,4},{1,5},{2,6},{3,7},{4,0},{5,1},{6,2},{7,3},{8,12},{9,13},{10,... | collective-permute-start | bytes 1572872 | tf_op jit(solution)/shard_map/ppermute | solution.py:843
  99.3 13.3 %collective-permute-start.20 = (bf16[128,1152]{1,0:T(8,128)(2,1)S(1)}, bf16[128,1152]{1,0:T(8,128)(2,1)S(1)}, u32[]{:S(2)}, u32[]{:S(2)}) collective-permute-start(bf16[128,1152]{1,0:T(8,128)(2,1)S(1)} %collective-permute-done.15.refs_10_.refs_14_), channel_id=1, source_target_pairs={{0,8},{1,9},{2,10},{3,11},{4,12},{5,13},{6,14},{7,15},{8,0},{9,1},... | collective-permute-start | bytes 884744 | tf_op jit(solution)/shard_map/ppermute | solution.py:843
  106.8 21.7 %collective-permute-start.23 = (bf16[256,1024]{1,0:T(8,128)(2,1)S(1)}, bf16[256,1024]{1,0:T(8,128)(2,1)S(1)}, u32[]{:S(2)}, u32[]{:S(2)}) collective-permute-start(bf16[256,1024]{1,0:T(8,128)(2,1)S(1)} %collective-permute-done.16.r0.refs_0_), channel_id=1, source_target_pairs={{0,1},{1,0},{2,3},{3,2},{4,5},{5,4},{6,7},{7,6},{8,9},{9,8},{10,11... | collective-permute-start | bytes 1572872 | tf_op jit(solution)/shard_map/ppermute | solution.py:843
  108.8 19.7 %collective-permute-start.24 = (bf16[256,1024]{1,0:T(8,128)(2,1)S(1)}, bf16[256,1024]{1,0:T(8,128)(2,1)S(1)}, u32[]{:S(2)}, u32[]{:S(2)}) collective-permute-start(bf16[256,1024]{1,0:T(8,128)(2,1)S(1)} %collective-permute-done.16.r0.refs_0_), channel_id=1, source_target_pairs={{0,4},{1,5},{2,6},{3,7},{4,0},{5,1},{6,2},{7,3},{8,12},{9,13},{10,... | collective-permute-start | bytes 1572872 | tf_op jit(solution)/shard_map/ppermute | solution.py:843
  108.8 15.7 %collective-permute-start.21 = (bf16[128,1152]{1,0:T(8,128)(2,1)S(1)}, bf16[128,1152]{1,0:T(8,128)(2,1)S(1)}, u32[]{:S(2)}, u32[]{:S(2)}) collective-permute-start(bf16[128,1152]{1,0:T(8,128)(2,1)S(1)} %collective-permute-done.15.refs_10_.refs_14_), channel_id=1, source_target_pairs={{0,16},{1,17},{2,18},{3,19},{4,20},{5,21},{6,22},{7,23},{8,24},{9,... | collective-permute-start | bytes 884744 | tf_op jit(solution)/shard_map/ppermute | solution.py:843
  110.4 15.9 %collective-permute-start.22 = (bf16[128,1152]{1,0:T(8,128)(2,1)S(1)}, bf16[128,1152]{1,0:T(8,128)(2,1)S(1)}, u32[]{:S(2)}, u32[]{:S(2)}) collective-permute-start(bf16[128,1152]{1,0:T(8,128)(2,1)S(1)} %collective-permute-done.15.refs_10_.refs_14_), channel_id=1, source_target_pairs={{0,24},{1,25},{2,26},{3,27},{4,28},{5,29},{6,30},{7,31},{8,16},{9,... | collective-permute-start | bytes 884744 | tf_op jit(solution)/shard_map/ppermute | solution.py:843
  112.6 28.6 %collective-permute-start.19 = (bf16[1024,256]{1,0:T(8,128)(2,1)S(1)}, bf16[1024,256]{1,0:T(8,128)(2,1)S(1)}, u32[]{:S(2)}, u32[]{:S(2)}) collective-permute-start(bf16[1024,256]{1,0:T(8,128)(2,1)S(1)} %collective-permute-done.17.refs_5_), channel_id=1, source_target_pairs={{0,4},{1,5},{2,6},{3,7},{4,0},{5,1},{6,2},{7,3},{8,12},{9,13},{10,... | collective-permute-start | bytes 1572872 | tf_op jit(solution)/shard_map/ppermute | solution.py:843
  126.3 14.9 %collective-permute-start.33 = (bf16[144,1024]{1,0:T(8,128)(2,1)S(1)}, bf16[144,1024]{1,0:T(8,128)(2,1)}, u32[]{:S(2)}, u32[]{:S(2)}) collective-permute-start(bf16[144,1024]{1,0:T(8,128)(2,1)S(1)} %copy-done.108), channel_id=1, source_target_pairs={{0,2},{1,3},{2,0},{3,1},{4,6},{5,7},{6,4},{7,5},{8,10},{9,11},{10,... | collective-permute-start | bytes 884744 | tf_op jit(solution)/shard_map/ppermute | solution.py:843
  128.5 13.6 %collective-permute-start.34 = (bf16[128,1152]{1,0:T(8,128)(2,1)S(1)}, bf16[128,1152]{1,0:T(8,128)(2,1)S(1)}, u32[]{:S(2)}, u32[]{:S(2)}) collective-permute-start(bf16[128,1152]{1,0:T(8,128)(2,1)S(1)} %collective-permute-done.29.refs_19_.refs_23_), channel_id=1, source_target_pairs={{0,4},{1,5},{2,6},{3,7},{4,0},{5,1},{6,2},{7,3},{8,12},{9,13},{10,... | collective-permute-start | bytes 884744 | tf_op jit(solution)/shard_map/ppermute | solution.py:843
  129.4 13.2 %collective-permute-start.25 = (bf16[128,1152]{1,0:T(8,128)(2,1)S(1)}, bf16[128,1152]{1,0:T(8,128)(2,1)S(1)}, u32[]{:S(2)}, u32[]{:S(2)}) collective-permute-start(bf16[128,1152]{1,0:T(8,128)(2,1)S(1)} %collective-permute-done.15.refs_10_.refs_14_), channel_id=1, source_target_pairs={{0,4},{1,5},{2,6},{3,7},{4,0},{5,1},{6,2},{7,3},{8,12},{9,13},{10,... | collective-permute-start | bytes 884744 | tf_op jit(solution)/shard_map/ppermute | solution.py:843
  143.1 21.6 %collective-permute-start.38 = (bf16[144,1024]{1,0:T(8,128)(2,1)}, bf16[144,1024]{1,0:T(8,128)(2,1)}, u32[]{:S(2)}, u32[]{:S(2)}) collective-permute-start(bf16[144,1024]{1,0:T(8,128)(2,1)} %collective-permute-done.33.refs_5_.refs_0_), channel_id=1, source_target_pairs={{0,8},{1,9},{2,10},{3,11},{4,12},{5,13},{6,14},{7,15},{8,0},{9,1},... | collective-permute-start | bytes 884744 | tf_op jit(solution)/shard_map/ppermute | solution.py:843
  144.2 20.5 %collective-permute-start.39 = (bf16[144,1024]{1,0:T(8,128)(2,1)}, bf16[144,1024]{1,0:T(8,128)(2,1)}, u32[]{:S(2)}, u32[]{:S(2)}) collective-permute-start(bf16[144,1024]{1,0:T(8,128)(2,1)} %collective-permute-done.33.refs_5_.refs_0_), channel_id=1, source_target_pairs={{0,16},{1,17},{2,18},{3,19},{4,20},{5,21},{6,22},{7,23},{8,24},{9,... | collective-permute-start | bytes 884744 | tf_op jit(solution)/shard_map/ppermute | solution.py:843
  145.5 19.2 %collective-permute-start.40 = (bf16[144,1024]{1,0:T(8,128)(2,1)}, bf16[144,1024]{1,0:T(8,128)(2,1)}, u32[]{:S(2)}, u32[]{:S(2)}) collective-permute-start(bf16[144,1024]{1,0:T(8,128)(2,1)} %collective-permute-done.33.refs_5_.refs_0_), channel_id=1, source_target_pairs={{0,24},{1,25},{2,26},{3,27},{4,28},{5,29},{6,30},{7,31},{8,16},{9,... | collective-permute-start | bytes 884744 | tf_op jit(solution)/shard_map/ppermute | solution.py:843
  146.6 18.9 %collective-permute-start.45 = (bf16[256,1024]{1,0:T(8,128)(2,1)S(1)}, bf16[256,1024]{1,0:T(8,128)(2,1)}, u32[]{:S(2)}, u32[]{:S(2)}) collective-permute-start(bf16[256,1024]{1,0:T(8,128)(2,1)S(1)} %collective-permute-done.23.r1.refs_1_), channel_id=1, source_target_pairs={{0,4},{1,5},{2,6},{3,7},{4,0},{5,1},{6,2},{7,3},{8,12},{9,13},{10,... | collective-permute-start | bytes 1572872 | tf_op jit(solution)/shard_map/ppermute | solution.py:843
  148.1 27.6 %collective-permute-start.41 = (bf16[144,1024]{1,0:T(8,128)(2,1)}, bf16[144,1024]{1,0:T(8,128)(2,1)}, u32[]{:S(2)}, u32[]{:S(2)}) collective-permute-start(bf16[144,1024]{1,0:T(8,128)(2,1)} %collective-permute-done.33.refs_5_.refs_0_), channel_id=1, source_target_pairs={{0,4},{1,5},{2,6},{3,7},{4,0},{5,1},{6,2},{7,3},{8,12},{9,13},{10,... | collective-permute-start | bytes 884744 | tf_op jit(solution)/shard_map/ppermute | solution.py:843
  194.6 17.1 %collective-permute-start.48 = (bf16[2,288,512]{2,1,0:T(8,128)(2,1)}, bf16[2,288,512]{2,1,0:T(8,128)(2,1)}, u32[]{:S(2)}, u32[]{:S(2)}) collective-permute-start(bf16[2,288,512]{2,1,0:T(8,128)(2,1)} %get-tuple-element.207), channel_id=1, source_target_pairs={{0,8},{1,9},{2,10},{3,11},{4,12},{5,13},{6,14},{7,15},{8,0},{9,1},... | collective-permute-start | bytes 1769480 | tf_op jit(solution)/shard_map/ppermute | solution.py:843
  195.6 16.5 %collective-permute-start.49 = (bf16[2,288,512]{2,1,0:T(8,128)(2,1)}, bf16[2,288,512]{2,1,0:T(8,128)(2,1)}, u32[]{:S(2)}, u32[]{:S(2)}) collective-permute-start(bf16[2,288,512]{2,1,0:T(8,128)(2,1)} %get-tuple-element.209), channel_id=1, source_target_pairs={{0,16},{1,17},{2,18},{3,19},{4,20},{5,21},{6,22},{7,23},{8,24},{9,... | collective-permute-start | bytes 1769480 | tf_op jit(solution)/shard_map/ppermute | solution.py:843
  199.4 15.2 %collective-permute-start.47 = (bf16[256,1024]{1,0:T(8,128)(2,1)S(1)}, bf16[256,1024]{1,0:T(8,128)(2,1)S(1)}, u32[]{:S(2)}, u32[]{:S(2)}) collective-permute-start(bf16[256,1024]{1,0:T(8,128)(2,1)S(1)} %slice.255), channel_id=1, source_target_pairs={{0,1},{1,0},{2,3},{3,2},{4,5},{5,4},{6,7},{7,6},{8,9},{9,8},{10,11... | collective-permute-start | bytes 1572872 | tf_op jit(solution)/shard_map/ppermute | solution.py:843
  204.7 18.0 %collective-permute-start.53 = (bf16[2,128,1152]{2,1,0:T(8,128)(2,1)S(1)}, bf16[2,128,1152]{2,1,0:T(8,128)(2,1)S(1)}, u32[]{:S(2)}, u32[]{:S(2)}) collective-permute-start(bf16[2,128,1152]{2,1,0:T(8,128)(2,1)S(1)} %get-tuple-element.219), channel_id=1, source_target_pairs={{0,8},{1,9},{2,10},{3,11},{4,12},{5,13},{6,14},{7,15},{8,0},{9,1},... | collective-permute-start | bytes 1769480 | tf_op jit(solution)/shard_map/ppermute | solution.py:843
  205.4 18.1 %collective-permute-start.54 = (bf16[2,128,1152]{2,1,0:T(8,128)(2,1)S(1)}, bf16[2,128,1152]{2,1,0:T(8,128)(2,1)S(1)}, u32[]{:S(2)}, u32[]{:S(2)}) collective-permute-start(bf16[2,128,1152]{2,1,0:T(8,128)(2,1)S(1)} %get-tuple-element.221), channel_id=1, source_target_pairs={{0,16},{1,17},{2,18},{3,19},{4,20},{5,21},{6,22},{7,23},{8,24},{9,... | collective-permute-start | bytes 1769480 | tf_op jit(solution)/shard_map/ppermute | solution.py:843
  225.8 20.4 %collective-permute-start.59 = (bf16[2,128,1152]{2,1,0:T(8,128)(2,1)S(1)}, bf16[2,128,1152]{2,1,0:T(8,128)(2,1)S(1)}, u32[]{:S(2)}, u32[]{:S(2)}) collective-permute-start(bf16[2,128,1152]{2,1,0:T(8,128)(2,1)S(1)} %get-tuple-element.224), channel_id=1, source_target_pairs={{0,8},{1,9},{2,10},{3,11},{4,12},{5,13},{6,14},{7,15},{8,0},{9,1},... | collective-permute-start | bytes 1769480 | tf_op jit(solution)/shard_map/ppermute | solution.py:843
  227.4 18.9 %collective-permute-start.60 = (bf16[2,128,1152]{2,1,0:T(8,128)(2,1)S(1)}, bf16[2,128,1152]{2,1,0:T(8,128)(2,1)S(1)}, u32[]{:S(2)}, u32[]{:S(2)}) collective-permute-start(bf16[2,128,1152]{2,1,0:T(8,128)(2,1)S(1)} %get-tuple-element.226), channel_id=1, source_target_pairs={{0,16},{1,17},{2,18},{3,19},{4,20},{5,21},{6,22},{7,23},{8,24},{9,... | collective-permute-start | bytes 1769480 | tf_op jit(solution)/shard_map/ppermute | solution.py:843
  228.0 22.5 %collective-permute-start.58 = (bf16[288,512]{1,0:T(8,128)(2,1)S(1)}, bf16[288,512]{1,0:T(8,128)(2,1)S(1)}, u32[]{:S(2)}, u32[]{:S(2)}) collective-permute-start(bf16[288,512]{1,0:T(8,128)(2,1)S(1)} %get-tuple-element.336), channel_id=1, source_target_pairs={{0,8},{1,9},{2,10},{3,11},{4,12},{5,13},{6,14},{7,15},{8,0},{9,1},... | collective-permute-start | bytes 884744 | tf_op jit(solution)/shard_map/ppermute | solution.py:843
  233.6 11.0 %collective-permute-start.51 = (bf16[256,1024]{1,0:T(8,128)(2,1)S(1)}, bf16[256,1024]{1,0:T(8,128)(2,1)S(1)}, u32[]{:S(2)}, u32[]{:S(2)}) collective-permute-start(bf16[256,1024]{1,0:T(8,128)(2,1)S(1)} %get-tuple-element.329.b0), channel_id=1, source_target_pairs={{0,1},{1,0},{2,3},{3,2},{4,5},{5,4},{6,7},{7,6},{8,9},{9,8},{10,11... | collective-permute-start | bytes 1572872 | tf_op jit(solution)/shard_map/ppermute | solution.py:843
  246.2 12.2 %collective-permute-start.56 = (bf16[256,1024]{1,0:T(8,128)(2,1)S(1)}, bf16[256,1024]{1,0:T(8,128)(2,1)S(1)}, u32[]{:S(2)}, u32[]{:S(2)}) collective-permute-start(bf16[256,1024]{1,0:T(8,128)(2,1)S(1)} %collective-permute-done.51.b1), channel_id=1, source_target_pairs={{0,4},{1,5},{2,6},{3,7},{4,0},{5,1},{6,2},{7,3},{8,12},{9,13},{10,... | collective-permute-start | bytes 1572872 | tf_op jit(solution)/shard_map/ppermute | solution.py:843
  251.8 30.2 %collective-permute-start.68 = (bf16[128,1152]{1,0:T(8,128)(2,1)S(1)}, bf16[128,1152]{1,0:T(8,128)(2,1)S(1)}, u32[]{:S(2)}, u32[]{:S(2)}) collective-permute-start(bf16[128,1152]{1,0:T(8,128)(2,1)S(1)} %get-tuple-element.332), channel_id=1, source_target_pairs={{0,8},{1,9},{2,10},{3,11},{4,12},{5,13},{6,14},{7,15},{8,0},{9,1},... | collective-permute-start | bytes 884744 | tf_op jit(solution)/shard_map/ppermute | solution.py:843
  252.9 29.0 %collective-permute-start.67 = (bf16[128,1152]{1,0:T(8,128)(2,1)S(1)}, bf16[128,1152]{1,0:T(8,128)(2,1)S(1)}, u32[]{:S(2)}, u32[]{:S(2)}) collective-permute-start(bf16[128,1152]{1,0:T(8,128)(2,1)S(1)} %get-tuple-element.334), channel_id=1, source_target_pairs={{0,16},{1,17},{2,18},{3,19},{4,20},{5,21},{6,22},{7,23},{8,24},{9,... | collective-permute-start | bytes 884744 | tf_op jit(solution)/shard_map/ppermute | solution.py:843
  256.0 47.0 %collective-permute-start.55 = (bf16[256,1024]{1,0:T(8,128)(2,1)}, bf16[256,1024]{1,0:T(8,128)(2,1)}, u32[]{:S(2)}, u32[]{:S(2)}) collective-permute-start(bf16[256,1024]{1,0:T(8,128)(2,1)} %slice.257), channel_id=1, source_target_pairs={{0,1},{1,0},{2,3},{3,2},{4,5},{5,4},{6,7},{7,6},{8,9},{9,8},{10,11... | collective-permute-start | bytes 1572872 | tf_op jit(solution)/shard_map/ppermute | solution.py:843
  258.5 29.1 %collective-permute-start.65 = (bf16[2,144,512]{2,1,0:T(8,128)(2,1)S(1)}, bf16[2,144,512]{2,1,0:T(8,128)(2,1)S(1)}, u32[]{:S(2)}, u32[]{:S(2)}) collective-permute-start(bf16[2,144,512]{2,1,0:T(8,128)(2,1)S(1)} %broadcast_select_fusion), channel_id=1, source_target_pairs={{0,2},{1,3},{2,0},{3,1},{4,6},{5,7},{6,4},{7,5},{8,10},{9,11},{10,... | collective-permute-start | bytes 884744 | tf_op jit(solution)/shard_map/ppermute | solution.py:843
  259.4 40.5 %collective-permute-start.71 = (bf16[2,64,1152]{2,1,0:T(8,128)(2,1)}, bf16[2,64,1152]{2,1,0:T(8,128)(2,1)}, u32[]{:S(2)}, u32[]{:S(2)}) collective-permute-start(bf16[2,64,1152]{2,1,0:T(8,128)(2,1)} %broadcast_select_fusion.4), channel_id=1, source_target_pairs={{0,2},{1,3},{2,0},{3,1},{4,6},{5,7},{6,4},{7,5},{8,10},{9,11},{10,... | collective-permute-start | bytes 884744 | tf_op jit(solution)/shard_map/ppermute | solution.py:843
  286.0 19.1 %collective-permute-start.80 = (bf16[2,64,1152]{2,1,0:T(8,128)(2,1)}, bf16[2,64,1152]{2,1,0:T(8,128)(2,1)}, u32[]{:S(2)}, u32[]{:S(2)}) collective-permute-start(bf16[2,64,1152]{2,1,0:T(8,128)(2,1)} %broadcast_select_fusion.2), channel_id=1, source_target_pairs={{0,2},{1,3},{2,0},{3,1},{4,6},{5,7},{6,4},{7,5},{8,10},{9,11},{10,... | collective-permute-start | bytes 884744 | tf_op jit(solution)/shard_map/ppermute | solution.py:843
  297.8 17.0 %collective-permute-start.72 = (bf16[2,384,256]{2,1,0:T(8,128)(2,1)S(1)}, bf16[2,384,256]{2,1,0:T(8,128)(2,1)S(1)}, u32[]{:S(2)}, u32[]{:S(2)}) collective-permute-start(bf16[2,384,256]{2,1,0:T(8,128)(2,1)S(1)} %get-tuple-element.266), channel_id=1, source_target_pairs={{0,8},{1,9},{2,10},{3,11},{4,12},{5,13},{6,14},{7,15},{8,0},{9,1},... | collective-permute-start | bytes 1179656 | tf_op jit(solution)/shard_map/ppermute | solution.py:843
  298.5 16.4 %collective-permute-start.73 = (bf16[2,384,256]{2,1,0:T(8,128)(2,1)S(1)}, bf16[2,384,256]{2,1,0:T(8,128)(2,1)S(1)}, u32[]{:S(2)}, u32[]{:S(2)}) collective-permute-start(bf16[2,384,256]{2,1,0:T(8,128)(2,1)S(1)} %get-tuple-element.268), channel_id=1, source_target_pairs={{0,16},{1,17},{2,18},{3,19},{4,20},{5,21},{6,22},{7,23},{8,24},{9,... | collective-permute-start | bytes 1179656 | tf_op jit(solution)/shard_map/ppermute | solution.py:843
  299.9 13.4 %collective-permute-start.70 = (bf16[256,1024]{1,0:T(8,128)(2,1)S(1)}, bf16[256,1024]{1,0:T(8,128)(2,1)S(1)}, u32[]{:S(2)}, u32[]{:S(2)}) collective-permute-start(bf16[256,1024]{1,0:T(8,128)(2,1)S(1)} %copy-done.105), channel_id=1, source_target_pairs={{0,1},{1,0},{2,3},{3,2},{4,5},{5,4},{6,7},{7,6},{8,9},{9,8},{10,11... | collective-permute-start | bytes 1572872 | tf_op jit(solution)/shard_map/ppermute | solution.py:843
  304.3 33.7 %collective-permute-start.74 = (bf16[2,64,1152]{2,1,0:T(8,128)(2,1)S(1)}, bf16[2,64,1152]{2,1,0:T(8,128)(2,1)S(1)}, u32[]{:S(2)}, u32[]{:S(2)}) collective-permute-start(bf16[2,64,1152]{2,1,0:T(8,128)(2,1)S(1)} %select_add_fusion.1.refs_0_), channel_id=1, source_target_pairs={{0,8},{1,9},{2,10},{3,11},{4,12},{5,13},{6,14},{7,15},{8,0},{9,1},... | collective-permute-start | bytes 884744 | tf_op jit(solution)/shard_map/ppermute | solution.py:843
  305.1 33.5 %collective-permute-start.75 = (bf16[2,64,1152]{2,1,0:T(8,128)(2,1)S(1)}, bf16[2,64,1152]{2,1,0:T(8,128)(2,1)S(1)}, u32[]{:S(2)}, u32[]{:S(2)}) collective-permute-start(bf16[2,64,1152]{2,1,0:T(8,128)(2,1)S(1)} %select_add_fusion.1.refs_0_), channel_id=1, source_target_pairs={{0,16},{1,17},{2,18},{3,19},{4,20},{5,21},{6,22},{7,23},{8,24},{9,... | collective-permute-start | bytes 884744 | tf_op jit(solution)/shard_map/ppermute | solution.py:843
  313.3 27.7 %collective-permute-start.76 = (bf16[2,64,1152]{2,1,0:T(8,128)(2,1)S(1)}, bf16[2,64,1152]{2,1,0:T(8,128)(2,1)S(1)}, u32[]{:S(2)}, u32[]{:S(2)}) collective-permute-start(bf16[2,64,1152]{2,1,0:T(8,128)(2,1)S(1)} %select_add_fusion.1.refs_0_), channel_id=1, source_target_pairs={{0,24},{1,25},{2,26},{3,27},{4,28},{5,29},{6,30},{7,31},{8,16},{9,... | collective-permute-start | bytes 884744 | tf_op jit(solution)/shard_map/ppermute | solution.py:843
  316.6 15.7 %collective-permute-start.78 = (bf16[384,256]{1,0:T(8,128)(2,1)}, bf16[384,256]{1,0:T(8,128)(2,1)}, u32[]{:S(2)}, u32[]{:S(2)}) collective-permute-start(bf16[384,256]{1,0:T(8,128)(2,1)} %get-tuple-element.340), channel_id=1, source_target_pairs={{0,8},{1,9},{2,10},{3,11},{4,12},{5,13},{6,14},{7,15},{8,0},{9,1},... | collective-permute-start | bytes 589832 | tf_op jit(solution)/shard_map/ppermute | solution.py:843
  317.0 15.5 %collective-permute-start.77 = (bf16[384,256]{1,0:T(8,128)(2,1)}, bf16[384,256]{1,0:T(8,128)(2,1)}, u32[]{:S(2)}, u32[]{:S(2)}) collective-permute-start(bf16[384,256]{1,0:T(8,128)(2,1)} %get-tuple-element.342), channel_id=1, source_target_pairs={{0,16},{1,17},{2,18},{3,19},{4,20},{5,21},{6,22},{7,23},{8,24},{9,... | collective-permute-start | bytes 589832 | tf_op jit(solution)/shard_map/ppermute | solution.py:843
  336.1 15.5 %collective-permute-start.93 = (bf16[2,64,1152]{2,1,0:T(8,128)(2,1)S(1)}, bf16[2,64,1152]{2,1,0:T(8,128)(2,1)S(1)}, u32[]{:S(2)}, u32[]{:S(2)}) collective-permute-start(bf16[2,64,1152]{2,1,0:T(8,128)(2,1)S(1)} %select_add_fusion.1.refs_0_), channel_id=1, source_target_pairs={{0,4},{1,5},{2,6},{3,7},{4,0},{5,1},{6,2},{7,3},{8,12},{9,13},{10,... | collective-permute-start | bytes 884744 | tf_op jit(solution)/shard_map/ppermute | solution.py:843
  336.5 15.2 %collective-permute-start.90 = (bf16[2,64,1152]{2,1,0:T(8,128)(2,1)S(1)}, bf16[2,64,1152]{2,1,0:T(8,128)(2,1)S(1)}, u32[]{:S(2)}, u32[]{:S(2)}) collective-permute-start(bf16[2,64,1152]{2,1,0:T(8,128)(2,1)S(1)} %select_add_fusion.refs_0_), channel_id=1, source_target_pairs={{0,8},{1,9},{2,10},{3,11},{4,12},{5,13},{6,14},{7,15},{8,0},{9,1},... | collective-permute-start | bytes 884744 | tf_op jit(solution)/shard_map/ppermute | solution.py:843
  338.0 14.3 %collective-permute-start.91 = (bf16[2,64,1152]{2,1,0:T(8,128)(2,1)S(1)}, bf16[2,64,1152]{2,1,0:T(8,128)(2,1)S(1)}, u32[]{:S(2)}, u32[]{:S(2)}) collective-permute-start(bf16[2,64,1152]{2,1,0:T(8,128)(2,1)S(1)} %select_add_fusion.refs_0_), channel_id=1, source_target_pairs={{0,16},{1,17},{2,18},{3,19},{4,20},{5,21},{6,22},{7,23},{8,24},{9,... | collective-permute-start | bytes 884744 | tf_op jit(solution)/shard_map/ppermute | solution.py:843
  338.6 11.6 %collective-permute-start.84 = (bf16[2,192,256]{2,1,0:T(8,128)(2,1)S(1)}, bf16[2,192,256]{2,1,0:T(8,128)(2,1)S(1)}, u32[]{:S(2)}, u32[]{:S(2)}) collective-permute-start(bf16[2,192,256]{2,1,0:T(8,128)(2,1)S(1)} %broadcast_select_fusion.6), channel_id=1, source_target_pairs={{0,2},{1,3},{2,0},{3,1},{4,6},{5,7},{6,4},{7,5},{8,10},{9,11},{10,... | collective-permute-start | bytes 589832 | tf_op jit(solution)/shard_map/ppermute | solution.py:843
  352.2 11.3 %collective-permute-start.86 = (bf16[2,192,256]{2,1,0:T(8,128)(2,1)S(1)}, bf16[2,192,256]{2,1,0:T(8,128)(2,1)S(1)}, u32[]{:S(2)}, u32[]{:S(2)}) collective-permute-start(bf16[2,192,256]{2,1,0:T(8,128)(2,1)S(1)} %select_add_fusion.3.refs_0_), channel_id=1, source_target_pairs={{0,8},{1,9},{2,10},{3,11},{4,12},{5,13},{6,14},{7,15},{8,0},{9,1},... | collective-permute-start | bytes 589832 | tf_op jit(solution)/shard_map/ppermute | solution.py:843
  353.8 11.0 %collective-permute-start.87 = (bf16[2,192,256]{2,1,0:T(8,128)(2,1)S(1)}, bf16[2,192,256]{2,1,0:T(8,128)(2,1)S(1)}, u32[]{:S(2)}, u32[]{:S(2)}) collective-permute-start(bf16[2,192,256]{2,1,0:T(8,128)(2,1)S(1)} %select_add_fusion.3.refs_0_), channel_id=1, source_target_pairs={{0,16},{1,17},{2,18},{3,19},{4,20},{5,21},{6,22},{7,23},{8,24},{9,... | collective-permute-start | bytes 589832 | tf_op jit(solution)/shard_map/ppermute | solution.py:843
  355.9 17.2 %collective-permute-start.98 = (bf16[2,64,1152]{2,1,0:T(8,128)(2,1)S(1)}, bf16[2,64,1152]{2,1,0:T(8,128)(2,1)S(1)}, u32[]{:S(2)}, u32[]{:S(2)}) collective-permute-start(bf16[2,64,1152]{2,1,0:T(8,128)(2,1)S(1)} %select_add_fusion.refs_0_), channel_id=1, source_target_pairs={{0,4},{1,5},{2,6},{3,7},{4,0},{5,1},{6,2},{7,3},{8,12},{9,13},{10,... | collective-permute-start | bytes 884744 | tf_op jit(solution)/shard_map/ppermute | solution.py:843
  361.0 14.2 %collective-permute-start.100 = (bf16[2,64,1152]{2,1,0:T(8,128)(2,1)S(1)}, bf16[2,64,1152]{2,1,0:T(8,128)(2,1)S(1)}, u32[]{:S(2)}, u32[]{:S(2)}) collective-permute-start(bf16[2,64,1152]{2,1,0:T(8,128)(2,1)S(1)} %collective-permute-done.91.refs_2_), channel_id=1, source_target_pairs={{0,4},{1,5},{2,6},{3,7},{4,0},{5,1},{6,2},{7,3},{8,12},{9,13},{10,... | collective-permute-start | bytes 884744 | tf_op jit(solution)/shard_map/ppermute | solution.py:843
  363.3 12.5 %collective-permute-start.101 = (bf16[2,64,1152]{2,1,0:T(8,128)(2,1)S(1)}, bf16[2,64,1152]{2,1,0:T(8,128)(2,1)S(1)}, u32[]{:S(2)}, u32[]{:S(2)}) collective-permute-start(bf16[2,64,1152]{2,1,0:T(8,128)(2,1)S(1)} %collective-permute-done.92.refs_3_), channel_id=1, source_target_pairs={{0,4},{1,5},{2,6},{3,7},{4,0},{5,1},{6,2},{7,3},{8,12},{9,13},{10,... | collective-permute-start | bytes 884744 | tf_op jit(solution)/shard_map/ppermute | solution.py:843
  364.8 11.1 %collective-permute-start.99 = (bf16[2,64,1152]{2,1,0:T(8,128)(2,1)S(1)}, bf16[2,64,1152]{2,1,0:T(8,128)(2,1)S(1)}, u32[]{:S(2)}, u32[]{:S(2)}) collective-permute-start(bf16[2,64,1152]{2,1,0:T(8,128)(2,1)S(1)} %collective-permute-done.90.refs_1_), channel_id=1, source_target_pairs={{0,4},{1,5},{2,6},{3,7},{4,0},{5,1},{6,2},{7,3},{8,12},{9,13},{10,... | collective-permute-start | bytes 884744 | tf_op jit(solution)/shard_map/ppermute | solution.py:843
  375.2 16.2 %collective-permute-start.105 = (bf16[2,192,256]{2,1,0:T(8,128)(2,1)S(1)}, bf16[2,192,256]{2,1,0:T(8,128)(2,1)S(1)}, u32[]{:S(2)}, u32[]{:S(2)}) collective-permute-start(bf16[2,192,256]{2,1,0:T(8,128)(2,1)S(1)} %collective-permute-done.87.refs_2_), channel_id=1, source_target_pairs={{0,4},{1,5},{2,6},{3,7},{4,0},{5,1},{6,2},{7,3},{8,12},{9,13},{10,... | collective-permute-start | bytes 589832 | tf_op jit(solution)/shard_map/ppermute | solution.py:843
  375.8 15.7 %collective-permute-start.106 = (bf16[2,192,256]{2,1,0:T(8,128)(2,1)S(1)}, bf16[2,192,256]{2,1,0:T(8,128)(2,1)S(1)}, u32[]{:S(2)}, u32[]{:S(2)}) collective-permute-start(bf16[2,192,256]{2,1,0:T(8,128)(2,1)S(1)} %collective-permute-done.88.refs_3_), channel_id=1, source_target_pairs={{0,4},{1,5},{2,6},{3,7},{4,0},{5,1},{6,2},{7,3},{8,12},{9,13},{10,... | collective-permute-start | bytes 589832 | tf_op jit(solution)/shard_map/ppermute | solution.py:843
  375.9 30.1 %collective-permute-start.83 = (bf16[256,1024]{1,0:T(8,128)(2,1)S(1)}, bf16[256,1024]{1,0:T(8,128)(2,1)}, u32[]{:S(2)}, u32[]{:S(2)}) collective-permute-start(bf16[256,1024]{1,0:T(8,128)(2,1)S(1)} %convert_element_type.46), channel_id=1, source_target_pairs={{0,0},{1,1},{2,4},{3,5},{4,2},{5,3},{6,6},{7,7},{8,8},{9,9},{10,12... | collective-permute-start | bytes 1572872 | tf_op jit(solution)/shard_map/ppermute | solution.py:843
  381.7 17.9 %collective-permute-start.102 = (f32[1,2176]{1,0:T(1,128)S(1)}, f32[1,2176]{1,0:T(1,128)S(1)}, u32[]{:S(2)}, u32[]{:S(2)}) collective-permute-start(f32[1,2176]{1,0:T(1,128)S(1)} %add.296), channel_id=1, source_target_pairs={{0,2},{1,3},{2,0},{3,1},{4,6},{5,7},{6,4},{7,5},{8,10},{9,11},{10,... | collective-permute-start | bytes 26120 | tf_op jit(solution)/shard_map/ppermute | solution.py:843
  386.1 22.1 %collective-permute-start.82 = (bf16[256,1024]{1,0:T(8,128)(2,1)}, bf16[256,1024]{1,0:T(8,128)(2,1)}, u32[]{:S(2)}, u32[]{:S(2)}) collective-permute-start(bf16[256,1024]{1,0:T(8,128)(2,1)} %convert_element_type.44), channel_id=1, source_target_pairs={{0,0},{1,1},{2,4},{3,5},{4,2},{5,3},{6,6},{7,7},{8,8},{9,9},{10,12... | collective-permute-start | bytes 1572872 | tf_op jit(solution)/shard_map/ppermute | solution.py:843
  (163 other events, 1945.0 us)
Sparse Core Ops, SparseCore 0:
  48.8 28.1 all-gather.4
  288.6 42.6 all-gather.6
